TPU v7x, 128 devices: a whole 4x4x4 slice. The times are simulated.
128 devices in a mesh: dom: 8 (over x, core), band: 16 (over z, y).
Axes of the slice: x: 4, y: 4, z: 4, core: 2. Of those that a mesh axis runs over, the one named last changes fastest.
Arguments:
- wavefunctions: bfloat16 [128, 64, 128, 128], P('band', 'dom'), may hold values from -6 to 6
- potential: float32 [64, 128, 128], P('dom'), may hold values from -3 to 1
- projectors: bfloat16 [288, 8, 1024], P('dom'), may hold values from -0.1875 to 0.1875
- margin_atoms: int32 [288], P('dom'), may hold values from 0 to 95, as said below
- tile_rows: int32 [288], P('dom'), may hold values from 0 to 1016
- coupling: float32 [8, 8], replicated, may hold values from -4 to 4
- band_weights: float32 [128], P('band'), may hold values from 0.005 to 0.03
Outputs:
- applied: bfloat16 [128, 64, 128, 128], P('band', 'dom')
- forces: float32 [3, 96], P(None, 'dom')
Inputs may be any that keep to these rules, and one draw needn't show every extreme that they name: `margin_atoms`: the list of domain d holds each atom a with a // 12 equal to d - 1, d or d + 1 (cyclically over the domains) exactly once, in an order drawn from the seed; so every atom is listed in three domains.
All inputs are finite; a program needn't handle non-finite values.
Results may differ from a plain program's by a relative error of at most 0.0095.
Values may be sent and summed in bfloat16 or wider, within the bound.
No kernel may reach another device: no remote copies, remote signals or barrier semaphores. Data moves between devices by JAX's collectives and lax.ppermute only.
A program may use at most 64 MiB of HBM per device.

v0:
```python
import jax
import jax.numpy as jnp
from jax import lax
from jax.sharding import PartitionSpec as P

ATOM_DEV = 12


second_coef = (-1.0 / 12.0, 4.0 / 3.0, -2.5, 4.0 / 3.0, -1.0 / 12.0)
first_coef = (1.0 / 12.0, -2.0 / 3.0, 0.0, 2.0 / 3.0, -1.0 / 12.0)


def padded_2(shard, sides, width):
    for axis, dim in sides:
        count, length = (lax.axis_size(axis), shard.shape[dim])
        up = [(i, (i + 1) % count) for i in range(count)]
        down = [(j, i) for i, j in up]
        last = lax.slice_in_dim(shard, length - width, length, axis=dim)
        leading = lax.slice_in_dim(shard, 0, width, axis=dim)
        before = lax.ppermute(last, axis, up)
        after = lax.ppermute(leading, axis, down)
        shard = jnp.concatenate([before, shard, after], axis=dim)
    return shard


def along_first(padded, plane_count, stencil):
    summed = jnp.zeros(
        (padded.shape[0], plane_count, padded.shape[2], padded.shape[3]), jnp.float32
    )
    for offset in range(-2, 3):
        if stencil[offset + 2] != 0.0:
            summed = summed + stencil[offset + 2] * padded[
                :, 2 + offset : 2 + offset + plane_count
            ].astype(jnp.float32)
    return summed


def along_second(center):
    width_y = center.shape[2]
    extended = jnp.concatenate([center[:, :, width_y - 2 :], center, center[:, :, :2]], 2)
    second_sum = jnp.zeros_like(center)
    first_sum = jnp.zeros_like(center)
    for offset in range(-2, 3):
        shifted = extended[:, :, 2 + offset : 2 + offset + width_y]
        second_sum = second_sum + second_coef[offset + 2] * shifted
        if first_coef[offset + 2] != 0.0:
            first_sum = first_sum + first_coef[offset + 2] * shifted
    return (second_sum, first_sum)


def third_table(width_z):
    source = jnp.arange(width_z, dtype=jnp.int32)[:, None]
    target = jnp.arange(width_z, dtype=jnp.int32)[None, :]
    distance = (source - target + width_z) % width_z
    second_tab = jnp.zeros((width_z, width_z), jnp.float32)
    first_tab = jnp.zeros((width_z, width_z), jnp.float32)
    for offset in range(-2, 3):
        hit = (distance == (offset + width_z) % width_z).astype(jnp.float32)
        second_tab = second_tab + second_coef[offset + 2] * hit
        first_tab = first_tab + first_coef[offset + 2] * hit
    return jnp.concatenate([second_tab, first_tab], 1)


def per_device(
    wavefunctions, potential, projectors, margin_atoms, tile_rows, coupling, band_weights
):
    band_count, plane_count, width_y, width_z = wavefunctions.shape
    entry_count = tile_rows.shape[0]
    proj_count = projectors.shape[1]
    tile_len = projectors.shape[2]
    tile_depth = tile_len // width_z
    row_count = plane_count * width_y
    padded = padded_2(wavefunctions, (("dom", 1),), 2)
    center = wavefunctions.astype(jnp.float32)
    third_both = jnp.dot(
        center.reshape(-1, width_z), third_table(width_z), precision=lax.Precision.HIGHEST
    )
    third_second = third_both[:, :width_z].reshape(center.shape)
    third_first = third_both[:, width_z:].reshape(center.shape)
    second_y, first_y = along_second(center)
    laplace_term = along_first(padded, plane_count, second_coef) + second_y + third_second
    local_part = -0.5 * laplace_term + potential[None] * center
    gather_rows = (tile_rows[:, None] + jnp.arange(tile_depth, dtype=jnp.int32)[None, :]).reshape(
        -1
    )
    field_list = [
        wavefunctions,
        along_first(padded, plane_count, first_coef).astype(jnp.bfloat16),
        first_y.astype(jnp.bfloat16),
        third_first.astype(jnp.bfloat16),
    ]
    measured_list = []
    for field in field_list:
        field_tiles = field.reshape(band_count, row_count, width_z)[:, gather_rows].reshape(
            band_count, entry_count, tile_len
        )
        measured_list.append(
            jnp.einsum("bet,eit->ebi", field_tiles, projectors, preferred_element_type=jnp.float32)
        )
    measured = jnp.stack(measured_list, 1).reshape(entry_count, 4 * band_count * proj_count)
    symmetric = 0.5 * (coupling + coupling.T)
    domain_count = lax.axis_size("dom")
    own_index = lax.axis_index("dom")
    owner = margin_atoms // ATOM_DEV
    relative = (owner - own_index + 1 + domain_count) % domain_count
    slots = relative * ATOM_DEV + margin_atoms % ATOM_DEV
    indicator = (slots[None, :] == jnp.arange(3 * ATOM_DEV, dtype=jnp.int32)[:, None]).astype(
        jnp.float32
    )
    sorted_rows = jnp.dot(indicator, measured, precision=lax.Precision.HIGHEST)
    extended = padded_2(sorted_rows.astype(jnp.bfloat16), (("dom", 0),), ATOM_DEV).astype(
        sorted_rows.dtype
    )
    owned_flat = (
        extended[:ATOM_DEV]
        + extended[2 * ATOM_DEV : 3 * ATOM_DEV]
        + extended[4 * ATOM_DEV : 5 * ATOM_DEV]
    )
    owned = owned_flat.reshape(ATOM_DEV, 4, band_count, proj_count)
    scaled_own = jnp.einsum("abj,ij->abi", owned[:, 0], symmetric, precision=lax.Precision.HIGHEST)
    scaled_flat = scaled_own.astype(jnp.bfloat16).reshape(ATOM_DEV, band_count * proj_count)
    near_scaled = padded_2(scaled_flat, (("dom", 0),), ATOM_DEV)
    entry_coef = near_scaled[slots].reshape(entry_count, band_count, proj_count)
    partial_value = -2.0 * jnp.einsum(
        "abi,akbi,b->ka", scaled_own, owned[:, 1:4], band_weights, precision=lax.Precision.HIGHEST
    )
    forces = lax.psum(partial_value, "band")
    tile_terms = jnp.einsum(
        "ebi,eit->bet", entry_coef, projectors, preferred_element_type=jnp.float32
    ).reshape(band_count, entry_count * tile_depth, width_z)
    nonlocal_part = (
        jnp.zeros((band_count, row_count, width_z), jnp.float32).at[:, gather_rows].add(tile_terms)
    )
    applied = (
        local_part + nonlocal_part.reshape(band_count, plane_count, width_y, width_z)
    ).astype(jnp.bfloat16)
    return (applied, forces)


def solution(mesh):
    placed = (
        P("band", "dom", None, None),
        P("dom", None, None),
        P("dom", None, None),
        P("dom"),
        P("dom"),
        P(),
        P("band"),
    )
    return jax.shard_map(
        per_device,
        mesh=mesh,
        in_specs=placed,
        out_specs=(P("band", "dom", None, None), P(None, "dom")),
        check_vma=False,
    )
```

profile of v0, /device:TPU:0, one launch (start us, length us, event | category | flops | bytes accessed | tf_op | source)
XLA Modules:
  0.0 179.1 jit_solution(9210305164281522998)
XLA Ops:
  0.7 2.5 %fusion.38 = (bf16[8,2,128,128]{3,2,1,0:T(8,128)(2,1)}, bf16[8,2,128,128]{3,2,1,0:T(8,128)(2,1)}) fusion(bf16[8,8,128,128]{3,2,1,0:T(8,128)(2,1)} %param.7), kind=kLoop, calls=%fused_computation.96 | loop fusion | bytes 2097152 | tf_op jit(solution)/shard_map/slice | solution.py:18
  3.1 3.0 %collective-permute-start.1 = (bf16[8,2,128,128]{3,2,1,0:T(8,128)(2,1)}, bf16[8,2,128,128]{3,2,1,0:T(8,128)(2,1)}, u32[]{:S(2)}, u32[]{:S(2)}) collective-permute-start(bf16[8,2,128,128]{3,2,1,0:T(8,128)(2,1)} %get-tuple-element.8), channel_id=1, source_target_pairs={{16,0},{32,16},{48,32},{64,48},{80,64},{96,80},{112,96},{0,112},{1... | collective-permute-start | bytes 1572872 | tf_op jit(solution)/shard_map/ppermute | solution.py:21
  6.2 4.3 %copy.39 = bf16[8,8,128,128]{3,0,2,1:T(8,128)(2,1)} copy(bf16[8,8,128,128]{3,2,1,0:T(8,128)(2,1)} %param.7) | data formatting | bytes 4194304 | tf_op args[0]
  10.7 3.5 %convolution_bitcast_fusion = f32[8192,256]{0,1:T(8,128)S(1)} fusion(bf16[8192,128]{1,0:T(8,128)(2,1)S(1)} %bitcast.75, f32[128,128]{1,0:T(8,128)S(1)} %get-tuple-element.13, f32[128,128]{1,0:T(8,128)S(1)} %get-tuple-element.14), kind=kOutput, calls=%fused_computation.6 | convolution fusion | flops 3221258240 | bytes 10616832 | tf_op jit(solution)/shard_map/dot_general | solution.py:75
  14.4 3.3 %copy.73 = bf16[16,8,8,1024]{3,2,1,0:T(8,128)(2,1)} copy(bf16[16,8,8,1024]{3,1,2,0:T(8,128)(2,1)S(1)} %bitcast.79) | data formatting | bytes 4194304
  17.7 0.3 copy-done.4
  18.0 4.5 %copy.48 = bf16[8,1024,128]{2,0,1:T(8,128)(2,1)} copy(bf16[8,1024,128]{1,0,2:T(8,128)(2,1)} %bitcast.78) | data formatting | bytes 4194304 | tf_op jit(solution)/shard_map/convert_element_type | solution.py:90
  22.5 2.5 %gather_fusion.3 = bf16[288,8,128]{2,1,0:T(8,128)(2,1)S(1)} fusion(bf16[8,1024,128]{2,0,1:T(8,128)(2,1)} %copy.48, s32[1024]{0:T(1024)S(1)} %pad_clamp_fusion.1), kind=kCustom, calls=%fused_computation.3 | custom fusion | bytes 1180800 | tf_op jit(solution)/shard_map/gather | solution.py:94
  25.0 3.3 %gather_fusion = bf16[288,8,128]{2,1,0:T(8,128)(2,1)} fusion(bf16[8,1024,128]{2,0,1:T(8,128)(2,1)} %bitcast.81, s32[1024]{0:T(1024)S(1)} %pad_clamp_fusion.1), kind=kCustom, calls=%fused_computation | custom fusion | bytes 1180800 | tf_op jit(solution)/shard_map/gather | solution.py:94
  28.3 0.4 convolution_bitcast_fusion.1
  28.7 1.5 convolution_bitcast_fusion.4
  30.2 0.8 copy.54
  31.0 0.7 copy.51
  31.8 1.1 constant_dynamic-update-slice_fusion.1
  32.9 3.8 %constant_dynamic-update-slice_fusion = (bf16[8,10,128,128]{3,2,1,0:T(8,128)(2,1)S(1)}, bf16[8,10,128,128]{3,2,1,0:T(8,128)(2,1)S(1)}, f32[8,8,128,128]{3,2,1,0:T(8,128)S(1)}) fusion(bf16[8,10,128,128]{3,2,1,0:T(8,128)(2,1)S(1)} %constant_dynamic-update-slice_fusion.1, bf16[8,8,128,128]{3,2,1,0:T(8,128)(2,1)} %param.7), kind=kLoop, calls=%fused_computation.73 | loop fusion | flops 1048575 | bytes 10485760 | tf_op jit(solution)/shard_map/concatenate | solution.py:22
  36.7 1.5 constant_dynamic-update-slice_fusion.2
  38.2 5.3 %fusion.15 = (bf16[8,8,128,128]{3,2,1,0:T(8,128)(2,1)}, bf16[8,8,128,128]{3,2,1,0:T(8,128)(2,1)S(1)}) fusion(bf16[8,10,128,128]{3,2,1,0:T(8,128)(2,1)S(1)} %constant_dynamic-update-slice_fusion.2, bf16[8,10,128,128]{3,2,1,0:T(8,128)(2,1)S(1)} %get-tuple-element.4, f32[8,8,2,128]{3,2,1,0:T(2,128)S(1)} %get-tuple-element.9, ...), kind=kLoop, calls=%fused_computation.32 | loop fusion | flops 25165824 | bytes 16908288 | tf_op jit(solution)/shard_map/convert_element_type | solution.py:88
  43.5 2.8 %copy.45 = bf16[8,8,128,128]{3,0,2,1:T(8,128)(2,1)} copy(bf16[8,8,128,128]{3,2,1,0:T(8,128)(2,1)S(1)} %get-tuple-element.16) | data formatting | bytes 4194304 | tf_op jit(solution)/shard_map/convert_element_type | solution.py:89
  46.3 3.3 %gather_fusion.2 = bf16[288,8,128]{2,1,0:T(8,128)(2,1)} fusion(bf16[8,1024,128]{2,0,1:T(8,128)(2,1)} %bitcast.83, s32[1024]{0:T(1024)S(1)} %pad_clamp_fusion.1), kind=kCustom, calls=%fused_computation.2 | custom fusion | bytes 1180800 | tf_op jit(solution)/shard_map/gather | solution.py:94
  49.5 1.5 convolution_bitcast_fusion.2
  51.0 0.8 copy.53
  51.8 4.3 %copy.42 = bf16[8,8,128,128]{3,0,2,1:T(8,128)(2,1)} copy(bf16[8,8,128,128]{3,2,1,0:T(8,128)(2,1)} %get-tuple-element.15) | data formatting | bytes 4194304 | tf_op jit(solution)/shard_map/convert_element_type | solution.py:88
  56.1 3.3 %gather_fusion.1 = bf16[288,8,128]{2,1,0:T(8,128)(2,1)} fusion(bf16[8,1024,128]{2,0,1:T(8,128)(2,1)} %bitcast.82, s32[1024]{0:T(1024)S(1)} %pad_clamp_fusion.1), kind=kCustom, calls=%fused_computation.1 | custom fusion | bytes 1180800 | tf_op jit(solution)/shard_map/gather | solution.py:94
  59.3 1.5 convolution_bitcast_fusion.3
  60.8 0.8 copy.52
  61.6 0.8 pad_maximum_fusion.2
  62.6 0.5 collective-permute-start.2
  63.1 0.6 pad_clamp_fusion
  63.7 4.5 %slice.117 = f32[8192,128]{0,1:T(8,128)} slice(f32[8192,256]{0,1:T(8,128)} %copy-done.4), slice={[0:8192], [0:128]} | slice | bytes 8388608 | tf_op jit(solution)/shard_map/slice | solution.py:78
  68.3 5.6 %copy.71 = f32[8192,128]{1,0:T(8,128)} copy(f32[8192,128]{0,1:T(8,128)} %slice.117) | data formatting | bytes 8388608 | tf_op jit(solution)/shard_map/reshape | solution.py:78
  73.9 0.7 copy.56
  74.7 0.6 slice.121
  75.3 1.5 copy.72
  76.8 0.9 fusion.23
  77.8 0.6 copy-done.5
  78.4 0.7 copy.57
  79.0 2.5 %collective-permute-start.5 = (bf16[12,64]{1,0:T(8,128)(2,1)}, bf16[12,64]{1,0:T(8,128)(2,1)S(1)}, u32[]{:S(2)}, u32[]{:S(2)}) collective-permute-start(bf16[12,64]{1,0:T(8,128)(2,1)} %copy.57), channel_id=1, source_target_pairs={{16,0},{32,16},{48,32},{64,48},{80,64},{96,80},{112,96},{0,112},{1... | collective-permute-start | bytes 4616 | tf_op jit(solution)/shard_map/ppermute | solution.py:21
  81.5 0.7 slice.122
  82.2 0.9 copy.64
  83.1 1.7 fusion.17
  84.8 0.7 multiply_reduce_fusion
  85.6 42.6 %psum.7 = f32[3,12]{1,0:T(4,128)} all-reduce(f32[3,12]{1,0:T(4,128)S(1)} %bitcast.92), channel_id=1, replica_groups=mesh['dom'=8,'band'=16] {'band'}, use_global_device_ids=true, to_apply=%region_1.2 | all-reduce | flops 36 | bytes 288 | tf_op jit(solution)/shard_map/psum | solution.py:127
  128.2 0.7 pad_maximum_fusion.3
  128.9 0.7 gather_fusion.4
  129.8 1.3 fusion.41
  131.2 2.2 %broadcast_in_dim.4 = f32[8,1024,128]{2,0,1:T(8,128)} broadcast(f32[]{:T(128)} %constant.88.clone.1), dimensions={} | broadcast | bytes 4194308 | tf_op jit(solution)/shard_map/broadcast_in_dim | solution.py:132
  133.4 31.4 %scatter_fusion = f32[8,1024,128]{2,0,1:T(8,128)} fusion(f32[8,1024,128]{2,0,1:T(8,128)} %broadcast_in_dim.4, s32[288]{0:T(512)S(1)} %copy-done.8, f32[288,8,128]{2,1,0:T(8,128)} %bitcast.80), kind=kCustom, calls=%fused_computation.5 | custom fusion | flops 294912 | bytes 3540096 | tf_op jit(solution)/shard_map/scatter-add | solution.py:132
  164.8 14.3 %fusion.11 = bf16[8,8,128,128]{3,2,1,0:T(8,128)(2,1)} fusion(f32[8,8,128,128]{3,2,1,0:T(8,128)} %bitcast.77, f32[8,8,128,128]{3,0,2,1:T(8,128)} %bitcast.76, f32[8,8,128,128]{3,2,1,0:T(8,128)} %copy-done.1, f32[8,8,2,128]{3,2,1,0:T(2,128)S(1)} %get-tuple-element.10, f32[8,8,2,128]{3,2,1,0:T(2,128)S(1)} %get-tuple-element.9, f32[8,128,128]{2,1,0:T(8,128)} %param.8, ...), kind=kLoop, calls=%fused_computation.28 | loop fusion | flops 33554432 | bytes 23724032 | tf_op jit(solution)/shard_map/convert_element_type | solution.py:136
  (48 shorter events, 1.4 us)
Async XLA Ops:
  0.6 27.6 %copy-start = (bf16[36,8,1024]{2,1,0:T(8,128)(2,1)S(1)}, bf16[36,8,1024]{2,1,0:T(8,128)(2,1)}, u32[]{:S(2)}) copy-start(bf16[36,8,1024]{2,1,0:T(8,128)(2,1)} %param.9) | copy-start | bytes 1769476
  0.6 10.0 %copy-start.3 = (bf16[8,8,128,128]{3,2,1,0:T(8,128)(2,1)S(1)}, bf16[8,8,128,128]{3,2,1,0:T(8,128)(2,1)}, u32[]{:S(2)}) copy-start(bf16[8,8,128,128]{3,2,1,0:T(8,128)(2,1)} %param.7) | copy-start | bytes 6291460
  0.7 9.8 %copy-start.11 = (s32[36]{0:T(128)S(1)}, s32[36]{0:T(128)}, u32[]{:S(2)}) copy-start(s32[36]{0:T(128)} %param.11) | copy-start | bytes 436
  3.1 28.7 %collective-permute-start = (bf16[8,2,128,128]{3,2,1,0:T(8,128)(2,1)}, bf16[8,2,128,128]{3,2,1,0:T(8,128)(2,1)}, u32[]{:S(2)}, u32[]{:S(2)}) collective-permute-start(bf16[8,2,128,128]{3,2,1,0:T(8,128)(2,1)} %get-tuple-element.7), channel_id=1, source_target_pairs={{0,16},{16,32},{32,48},{48,64},{64,80},{80,96},{96,112},{112,0},{1... | collective-permute-start | bytes 1572872 | tf_op jit(solution)/shard_map/ppermute | solution.py:20
  3.1 33.6 %collective-permute-start.1 = (bf16[8,2,128,128]{3,2,1,0:T(8,128)(2,1)}, bf16[8,2,128,128]{3,2,1,0:T(8,128)(2,1)}, u32[]{:S(2)}, u32[]{:S(2)}) collective-permute-start(bf16[8,2,128,128]{3,2,1,0:T(8,128)(2,1)} %get-tuple-element.8), channel_id=1, source_target_pairs={{16,0},{32,16},{48,32},{64,48},{80,64},{96,80},{112,96},{0,112},{1... | collective-permute-start | bytes 1572872 | tf_op jit(solution)/shard_map/ppermute | solution.py:21
  10.7 11.9 %copy-start.7 = (s32[288]{0:T(512)}, s32[288]{0:T(512)S(1)}, u32[]{:S(2)}) copy-start(s32[288]{0:T(512)S(1)} %fusion.31) | copy-start | bytes 3460
  14.2 3.9 %copy-start.4 = (f32[8192,256]{0,1:T(8,128)}, f32[8192,256]{0,1:T(8,128)S(1)}, u32[]{:S(2)}) copy-start(f32[8192,256]{0,1:T(8,128)S(1)} %convolution_bitcast_fusion) | copy-start | bytes 25165828
  18.0 13.7 %copy-start.10 = (s32[36]{0:T(128)S(1)}, s32[36]{0:T(128)}, u32[]{:S(2)}) copy-start(s32[36]{0:T(128)} %param.10) | copy-start | bytes 436
  36.7 6.8 %copy-start.1 = (f32[8,8,128,128]{3,2,1,0:T(8,128)}, f32[8,8,128,128]{3,2,1,0:T(8,128)S(1)}, u32[]{:S(2)}) copy-start(f32[8,8,128,128]{3,2,1,0:T(8,128)S(1)} %get-tuple-element.6) | copy-start | bytes 12582916
  36.7 6.8 %copy-start.2 = (bf16[8,10,128,128]{3,2,1,0:T(8,128)(2,1)}, bf16[8,10,128,128]{3,2,1,0:T(8,128)(2,1)S(1)}, u32[]{:S(2)}) copy-start(bf16[8,10,128,128]{3,2,1,0:T(8,128)(2,1)S(1)} %get-tuple-element.4) | copy-start | bytes 7864324
  49.5 12.1 %copy-start.6 = (f32[36,1,8,8]{0,3,2,1:T(8,128)S(1)}, f32[36,1,8,8]{0,3,2,1:T(8,128)}, u32[]{:S(2)}) copy-start(f32[36,1,8,8]{0,3,2,1:T(8,128)} %copy.54) | copy-start | bytes 27652
  62.6 11.9 %collective-permute-start.3 = (bf16[12,256]{1,0:T(8,128)(2,1)S(1)}, bf16[12,256]{1,0:T(8,128)(2,1)S(1)}, u32[]{:S(2)}, u32[]{:S(2)}) collective-permute-start(bf16[12,256]{1,0:T(8,128)(2,1)S(1)} %get-tuple-element.12), channel_id=1, source_target_pairs={{16,0},{32,16},{48,32},{64,48},{80,64},{96,80},{112,96},{0,112},{1... | collective-permute-start | bytes 18440 | tf_op jit(solution)/shard_map/ppermute | solution.py:21
  62.6 11.9 %collective-permute-start.2 = (bf16[12,256]{1,0:T(8,128)(2,1)S(1)}, bf16[12,256]{1,0:T(8,128)(2,1)S(1)}, u32[]{:S(2)}, u32[]{:S(2)}) collective-permute-start(bf16[12,256]{1,0:T(8,128)(2,1)S(1)} %get-tuple-element.11), channel_id=1, source_target_pairs={{0,16},{16,32},{32,48},{48,64},{64,80},{80,96},{96,112},{112,0},{1... | collective-permute-start | bytes 18440 | tf_op jit(solution)/shard_map/ppermute | solution.py:20
  68.3 5.6 %copy-start.9 = (f32[8,8]{1,0:T(8,128)S(1)}, f32[8,8]{1,0:T(8,128)}, u32[]{:S(2)}) copy-start(f32[8,8]{1,0:T(8,128)} %param.12) | copy-start | bytes 772
  77.7 0.6 copy-start.5
  79.0 54.4 %copy-start.8 = (s32[288]{0:T(512)S(1)}, s32[288]{0:T(512)}, u32[]{:S(2)}) copy-start(s32[288]{0:T(512)} %copy-done.7) | copy-start | bytes 3460
  79.0 49.1 %collective-permute-start.5 = (bf16[12,64]{1,0:T(8,128)(2,1)}, bf16[12,64]{1,0:T(8,128)(2,1)S(1)}, u32[]{:S(2)}, u32[]{:S(2)}) collective-permute-start(bf16[12,64]{1,0:T(8,128)(2,1)} %copy.57), channel_id=1, source_target_pairs={{16,0},{32,16},{48,32},{64,48},{80,64},{96,80},{112,96},{0,112},{1... | collective-permute-start | bytes 4616 | tf_op jit(solution)/shard_map/ppermute | solution.py:21
  81.5 46.7 %collective-permute-start.4 = (bf16[12,64]{1,0:T(8,128)(2,1)}, bf16[12,64]{1,0:T(8,128)(2,1)S(1)}, u32[]{:S(2)}, u32[]{:S(2)}) collective-permute-start(bf16[12,64]{1,0:T(8,128)(2,1)} %copy.57), channel_id=1, source_target_pairs={{0,16},{16,32},{32,48},{48,64},{64,80},{80,96},{96,112},{112,0},{1... | collective-permute-start | bytes 4616 | tf_op jit(solution)/shard_map/ppermute | solution.py:20
where the time goes:
time: 181 us; the launch traced here: 179 us
  local copies, waits for them, and re-layouts  59.4 us (33%)
  other arithmetic  57.8 us (32%)
  blocking collectives  42.6 us (24%)
  matrix products  12.6 us (7%)
  starting transfers between devices  5.94 us (3%)
    psum x1, blocking collectives, per_device(): forces = lax.psum(partial_value, 'band')  42.6 us
    scatter-add x1, other arithmetic, per_device(): jnp.zeros((band_count, row_count, width_z), jnp.float32).at[:, gather_rows]  31.4 us
    convert_element_type x1, other arithmetic, per_device(): applied = (local_part + nonlocal_part.reshape(band_count, plane_count, wi...  14.3 us
    gather x4, local copies, waits for them, and re-layouts, per_device(): field.reshape(band_count, row_count, width_z)[:, gather_rows]  12.3 us
    unnamed x30, local copies, waits for them, and re-layouts  11.9 us
    reshape x1, local copies, waits for them, and re-layouts, per_device(): third_second = third_both[:, :width_z].reshape(center.shape)  5.59 us
    ppermute x3, starting transfers between devices, padded_2(): after = lax.ppermute(leading, axis, down)  5.44 us
    convert_element_type x1, other arithmetic, per_device(): along_first(padded, plane_count, first_coef).astype(jnp.bfloat16)  5.29 us
  transfers between devices with their start and end apart: 6, of which 0 were waited for; matrix products, arithmetic and copies ran while one was open for 25% of the time, Pallas kernels for 0%

commit v1 on v0

v1 whole, which is shorter than its diff:
```python
import functools

import jax
import jax.numpy as jnp
from jax import lax
from jax.experimental import pallas as pl
from jax.experimental.pallas import tpu as pltpu
from jax.sharding import PartitionSpec as P

ATOM_DEV = 12
GROUPS = 3
LANES = 128
PAD = 2

f32 = jnp.float32
bf16 = jnp.bfloat16


def ring(x, axis, step):
    count = lax.axis_size(axis)
    return lax.ppermute(x, axis, [(i, (i + step) % count) for i in range(count)])


def to_rows(src, b, plane, y0, dst, base):
    part = src[b, plane, pl.ds(y0, 16), :].astype(f32)
    dst[pl.ds(base + b, 16, stride=8), :] = part


def tile_base(first_row, k, width_y):
    row = first_row + k
    plane = lax.shift_right_logical(row, 7)
    return (row + plane * (2 * PAD) + PAD + PAD * (width_y + 2 * PAD)) * 8


def at_row(ref, base):
    return ref[pl.ds(pl.multiple_of(base, 8), 8), :]


def diagonal_blocks(product, field):
    lane = lax.broadcasted_iota(jnp.int32, (8, LANES), 1)
    total = jnp.zeros((8, LANES), f32)
    for s in range(ATOM_DEV):
        start = (field * ATOM_DEV + s) * 8
        total = total + jnp.where(
            lax.shift_right_logical(lane, 3) == s, product[start : start + 8, :], 0.0
        )
    return total


def measure(rows_ref, group, table, width_y, fields):
    stacked = []
    for field in fields:
        for s in range(ATOM_DEV):
            first = rows_ref[group * ATOM_DEV + s]
            stacked.append(
                jnp.concatenate(
                    [field(tile_base(first, k, width_y)) for k in range(8)], axis=1
                )
            )
    values = jnp.concatenate(stacked, axis=0).astype(bf16)
    product = lax.dot_general(
        values, table, (((1,), (1,)), ((), ())), preferred_element_type=f32
    )
    return [diagonal_blocks(product, q) for q in range(len(fields))]


def relayout_kernel(
    rows_ref, entry_ref, wave_ref, proj_ref, grid_ref, table_ref, margin_ref, proj_scr, *, width_y
):
    stride = width_y + 2 * PAD
    planes = wave_ref.shape[1]
    chunks = width_y // 16

    def convert(step, carry):
        plane = step // chunks
        y0 = pl.multiple_of((step % chunks) * 16, 16)
        base = ((plane + PAD) * stride + PAD + y0) * 8
        for b in range(8):
            to_rows(wave_ref, b, plane, y0, grid_ref, base)
        return carry

    lax.fori_loop(0, planes * chunks, convert, 0)

    def wrap(plane, carry):
        base = pl.multiple_of((plane + PAD) * stride * 8, 8)
        grid_ref[pl.ds(base, 8 * PAD), :] = grid_ref[pl.ds(base + width_y * 8, 8 * PAD), :]
        grid_ref[pl.ds(base + (width_y + PAD) * 8, 8 * PAD), :] = grid_ref[
            pl.ds(base + PAD * 8, 8 * PAD), :
        ]
        return carry

    lax.fori_loop(0, planes, wrap, 0)

    def clear(step, carry):
        for plane in (0, 1, planes + PAD, planes + PAD + 1):
            base = pl.multiple_of((plane * stride + PAD + step * 8) * 8, 8)
            grid_ref[pl.ds(base, 64), :] = jnp.zeros((64, LANES), f32)
        return carry

    lax.fori_loop(0, width_y // 8, clear, 0)

    def one_group(group, carry):
        proj_scr[ATOM_DEV * 8 :, :] = jnp.zeros((LANES - ATOM_DEV * 8, proj_scr.shape[1]), f32)
        for s in range(ATOM_DEV):
            entry = entry_ref[group * ATOM_DEV + s]
            proj_scr[s * 8 : s * 8 + 8, :] = proj_ref[entry].astype(f32)
        table = proj_scr[...].astype(bf16)
        table_ref[group] = table
        (margin_ref[group],) = measure(
            rows_ref, group, table, width_y, [lambda base: at_row(grid_ref, base)]
        )
        return carry

    lax.fori_loop(0, GROUPS, one_group, 0)


def third_shift(center, offset):
    return pltpu.roll(center, (-offset) % center.shape[-1], 1)


def local_kernel(rows_ref, grid_ref, pot_ref, table_ref, local_ref, margin_ref, *, width_y):
    stride = width_y + 2 * PAD
    planes = pot_ref.shape[0]
    chunk = 8

    def one_chunk(step, carry):
        plane = step // (width_y // chunk)
        y0 = pl.multiple_of((step % (width_y // chunk)) * chunk, chunk)
        base = ((plane + PAD) * stride + PAD + y0) * 8
        column = [at_row(grid_ref, base + (k - 2) * 8) for k in range(chunk + 4)]
        out_base = pl.multiple_of((plane * width_y + y0) * 8, 8)
        hop = stride * 8
        for k in range(chunk):
            here = base + k * 8
            center = column[k + 2]
            near = column[k + 1] + column[k + 3]
            far = column[k] + column[k + 4]
            near = near + at_row(grid_ref, here - hop)
            near = near + at_row(grid_ref, here + hop)
            far = far + at_row(grid_ref, here - 2 * hop)
            far = far + at_row(grid_ref, here + 2 * hop)
            near = near + (third_shift(center, -1) + third_shift(center, 1))
            far = far + (third_shift(center, -2) + third_shift(center, 2))
            weight = pot_ref[plane, pl.ds(y0 + k, 1), :] + 3.75
            local_ref[pl.ds(out_base + k * 8, 8), :] = (
                weight * center - (2.0 / 3.0) * near + (1.0 / 24.0) * far
            )
        return carry

    lax.fori_loop(0, planes * (width_y // chunk), one_chunk, 0)

    def along_y(base):
        near = at_row(grid_ref, base + 8) - at_row(grid_ref, base - 8)
        far = at_row(grid_ref, base + 16) - at_row(grid_ref, base - 16)
        return (2.0 / 3.0) * near - (1.0 / 12.0) * far

    def along_z(base):
        center = at_row(grid_ref, base)
        near = third_shift(center, 1) - third_shift(center, -1)
        far = third_shift(center, 2) - third_shift(center, -2)
        return (2.0 / 3.0) * near - (1.0 / 12.0) * far

    def one_group(group, carry):
        second, third = measure(rows_ref, group, table_ref[group], width_y, [along_y, along_z])
        margin_ref[0, group] = second
        margin_ref[1, group] = third
        return carry

    lax.fori_loop(0, GROUPS, one_group, 0)


def first_kernel(
    rows_ref, grid_in, low_ref, high_ref, table_ref, yz_ref, grid_ref, margin_ref, *, width_y
):
    del grid_in
    stride = width_y + 2 * PAD
    planes = grid_ref.shape[0] // (8 * stride) - 2 * PAD
    chunks = width_y // 16
    hop = stride * 8

    def convert(step, carry):
        y0 = pl.multiple_of(step * 16, 16)
        for plane in range(PAD):
            low = (plane * stride + PAD + y0) * 8
            high = ((plane + planes + PAD) * stride + PAD + y0) * 8
            for b in range(8):
                to_rows(low_ref, b, plane, y0, grid_ref, low)
                to_rows(high_ref, b, plane, y0, grid_ref, high)
        return carry

    lax.fori_loop(0, chunks, convert, 0)

    def along_x(base):
        near = at_row(grid_ref, base + hop) - at_row(grid_ref, base - hop)
        far = at_row(grid_ref, base + 2 * hop) - at_row(grid_ref, base - 2 * hop)
        return (2.0 / 3.0) * near - (1.0 / 12.0) * far

    def one_group(group, carry):
        (first,) = measure(rows_ref, group, table_ref[group], width_y, [along_x])
        margin_ref[group, 0] = first
        margin_ref[group, 1] = yz_ref[0, group]
        margin_ref[group, 2] = yz_ref[1, group]
        return carry

    lax.fori_loop(0, GROUPS, one_group, 0)


def apply_kernel(
    rows_ref, local_in, low_ref, high_ref, table_ref, scaled_ref, local_ref, out_ref, *, width_y
):
    del local_in
    planes = out_ref.shape[1]
    chunks = width_y // 16
    lane = lax.broadcasted_iota(jnp.int32, (8, LANES), 1)

    def one_group(group, carry):
        scaled = scaled_ref[group]
        blocks = [
            jnp.where(lax.shift_right_logical(lane, 3) == s, scaled, 0.0)
            for s in range(ATOM_DEV)
        ]
        coef = jnp.concatenate(blocks, axis=0).astype(bf16)
        terms = jnp.dot(coef, table_ref[group], preferred_element_type=f32)
        for s in range(ATOM_DEV):
            base = pl.multiple_of(rows_ref[group * ATOM_DEV + s] * 8, 8)
            for k in range(8):
                where = pl.ds(base + k * 8, 8)
                local_ref[where, :] = (
                    local_ref[where, :] + terms[s * 8 : s * 8 + 8, k * LANES : (k + 1) * LANES]
                )
        return carry

    lax.fori_loop(0, GROUPS, one_group, 0)

    def read(plane, y0, b):
        base = (plane * width_y + y0) * 8
        return local_ref[pl.ds(base + b, 16, stride=8), :]

    def edges(step, carry):
        y0 = pl.multiple_of(step * 16, 16)
        at_y = pl.ds(y0, 16)
        for b in range(8):
            low2 = low_ref[b, 0, at_y, :].astype(f32)
            low1 = low_ref[b, 1, at_y, :].astype(f32)
            high1 = high_ref[b, 0, at_y, :].astype(f32)
            high2 = high_ref[b, 1, at_y, :].astype(f32)
            out_ref[b, 0, at_y, :] = (
                read(0, y0, b) - (2.0 / 3.0) * low1 + (1.0 / 24.0) * low2
            ).astype(bf16)
            out_ref[b, 1, at_y, :] = (read(1, y0, b) + (1.0 / 24.0) * low1).astype(bf16)
            out_ref[b, planes - 2, at_y, :] = (
                read(planes - 2, y0, b) + (1.0 / 24.0) * high1
            ).astype(bf16)
            out_ref[b, planes - 1, at_y, :] = (
                read(planes - 1, y0, b) - (2.0 / 3.0) * high1 + (1.0 / 24.0) * high2
            ).astype(bf16)
        return carry

    lax.fori_loop(0, chunks, edges, 0)

    def inner(step, carry):
        plane = 2 + step // chunks
        y0 = pl.multiple_of((step % chunks) * 16, 16)
        for b in range(8):
            out_ref[b, plane, pl.ds(y0, 16), :] = read(plane, y0, b).astype(bf16)
        return carry

    lax.fori_loop(0, (planes - 4) * chunks, inner, 0)


def scale_kernel(own_ref, above_ref, below_ref, mixing_ref, scaled_ref):
    total = own_ref[...] + above_ref[...] + below_ref[...]
    scaled_ref[...] = jnp.dot(
        total, mixing_ref[...], precision=lax.Precision.HIGHEST, preferred_element_type=f32
    )


VMEM = pl.BlockSpec(memory_space=pltpu.VMEM)
SMEM = pl.BlockSpec(memory_space=pltpu.SMEM)
PARAMS = pltpu.CompilerParams(vmem_limit_bytes=24 * 1024 * 1024)


def cost(flops, moved):
    return pl.CostEstimate(flops=flops, bytes_accessed=moved, transcendentals=0)


def per_device(
    wavefunctions, potential, projectors, margin_atoms, tile_rows, coupling, band_weights
):
    band_count, plane_count, width_y, width_z = wavefunctions.shape
    proj_count, tile_len = projectors.shape[1:]
    assert (band_count, proj_count, width_y, width_z) == (8, 8, 128, LANES)
    grid_rows = (plane_count + 2 * PAD) * (width_y + 2 * PAD) * 8
    local_rows = plane_count * width_y * 8

    above = wavefunctions[:, plane_count - PAD :]
    below = wavefunctions[:, :PAD]
    low_halo = ring(above, "dom", 1)
    high_halo = ring(below, "dom", -1)

    domain_count = lax.axis_size("dom")
    own_index = lax.axis_index("dom")
    relative = (margin_atoms // ATOM_DEV - own_index + 1 + domain_count) % domain_count
    slots = relative * ATOM_DEV + margin_atoms % ATOM_DEV
    entry_count = slots.shape[0]
    assert entry_count == GROUPS * ATOM_DEV
    hit = slots[None, :] == jnp.arange(entry_count, dtype=jnp.int32)[:, None]
    entry_of = jnp.where(hit, jnp.arange(entry_count, dtype=jnp.int32)[None, :], 0).sum(1)
    row_of = jnp.where(hit, tile_rows[None, :], 0).sum(1)

    grid, table, margins = pl.pallas_call(
        functools.partial(relayout_kernel, width_y=width_y),
        out_shape=(
            jax.ShapeDtypeStruct((grid_rows, LANES), f32),
            jax.ShapeDtypeStruct((GROUPS, LANES, tile_len), bf16),
            jax.ShapeDtypeStruct((GROUPS, 8, LANES), f32),
        ),
        in_specs=[SMEM, SMEM, VMEM, VMEM],
        out_specs=(VMEM, VMEM, VMEM),
        scratch_shapes=[pltpu.VMEM((LANES, tile_len), f32)],
        compiler_params=PARAMS,
        cost_estimate=cost(10**7, 10 * 2**20),
        name="relayout",
    )(row_of, entry_of, wavefunctions, projectors)

    from_above = ring(margins[0], "dom", -1)
    from_below = ring(margins[2], "dom", 1)

    local, yz_margins = pl.pallas_call(
        functools.partial(local_kernel, width_y=width_y),
        out_shape=(
            jax.ShapeDtypeStruct((local_rows, LANES), f32),
            jax.ShapeDtypeStruct((2, GROUPS, 8, LANES), f32),
        ),
        in_specs=[SMEM, VMEM, VMEM, VMEM],
        out_specs=(VMEM, VMEM),
        compiler_params=PARAMS,
        cost_estimate=cost(10**7, 16 * 2**20),
        name="local",
    )(row_of, grid, potential, table)

    symmetric = 0.5 * (coupling + coupling.T)
    lane_atom = jnp.arange(LANES, dtype=jnp.int32) // proj_count
    same = (lane_atom[:, None] == lane_atom[None, :]) & (lane_atom[:, None] < ATOM_DEV)
    mixing = jnp.where(same, jnp.tile(symmetric, (LANES // proj_count,) * 2), 0.0)
    scaled = pl.pallas_call(
        scale_kernel,
        out_shape=jax.ShapeDtypeStruct((8, LANES), f32),
        in_specs=[VMEM] * 4,
        out_specs=VMEM,
        name="scale",
    )(margins[1], from_above, from_below, mixing)
    scaled_low = ring(scaled, "dom", 1)
    scaled_high = ring(scaled, "dom", -1)

    _, force_margins = pl.pallas_call(
        functools.partial(first_kernel, width_y=width_y),
        out_shape=(
            jax.ShapeDtypeStruct((grid_rows, LANES), f32),
            jax.ShapeDtypeStruct((GROUPS, 3, 8, LANES), f32),
        ),
        in_specs=[SMEM, VMEM, VMEM, VMEM, VMEM, VMEM],
        out_specs=(VMEM, VMEM),
        input_output_aliases={1: 0},
        compiler_params=PARAMS,
        cost_estimate=cost(10**7, 4 * 2**20),
        name="first",
    )(row_of, grid, low_halo, high_halo, table, yz_margins)
    force_above = ring(force_margins[0], "dom", -1)
    force_below = ring(force_margins[2], "dom", 1)

    _, applied = pl.pallas_call(
        functools.partial(apply_kernel, width_y=width_y),
        out_shape=(
            jax.ShapeDtypeStruct((local_rows, LANES), f32),
            jax.ShapeDtypeStruct(wavefunctions.shape, bf16),
        ),
        in_specs=[SMEM, VMEM, VMEM, VMEM, VMEM, VMEM],
        out_specs=(VMEM, VMEM),
        input_output_aliases={1: 0},
        compiler_params=PARAMS,
        cost_estimate=cost(10**7, 8 * 2**20),
        name="apply",
    )(row_of, local, low_halo, high_halo, table, jnp.stack([scaled_low, scaled, scaled_high]))

    owned = force_margins[1] + force_above + force_below
    weighted = -2.0 * band_weights[:, None] * scaled
    contribution = (owned * weighted[None]).sum(1)
    block_count = lax.axis_size("band")
    copies = jnp.broadcast_to(contribution[None], (block_count,) + contribution.shape)
    gathered = lax.all_to_all(copies, "band", 0, 0)
    summed = gathered.sum(0)[:, : ATOM_DEV * proj_count]
    forces = summed.reshape(3, ATOM_DEV, proj_count).sum(2)
    return (applied, forces)


def solution(mesh):
    placed = (
        P("band", "dom", None, None),
        P("dom", None, None),
        P("dom", None, None),
        P("dom"),
        P("dom"),
        P(),
        P("band"),
    )
    return jax.shard_map(
        per_device,
        mesh=mesh,
        in_specs=placed,
        out_specs=(P("band", "dom", None, None), P(None, "dom")),
        check_vma=False,
    )
```

time: 181 us -> 71.6 us (0.40)
  other arithmetic: 57.8 us -> 2.99 us
  blocking collectives: 42.6 us -> 0 us
  local copies, waits for them, and re-layouts: 59.4 us -> 20.2 us
  Pallas kernels: 0 us -> 27.2 us
  matrix products: 12.6 us -> 0 us
  starting transfers between devices: 5.94 us -> 17 us
  waiting for transfers between devices: 0.02 us -> 2.92 us
    psum x1 -> x0, blocking collectives: 42.6 us -> none  [per_device(): forces = lax.psum(partial_value, 'band')]
    scatter-add x1 -> x0, other arithmetic: 31.4 us -> none  [per_device(): jnp.zeros((band_count, row_count, width_z), jnp.float32).at[:, gather_rows]]
    pallas_call x0 -> x5, Pallas kernels: none -> 27.2 us  [the longest x1 16.4 us: per_device(): pl.pallas_call(functools.partial(local_kernel, width_y=width_y), out_shap...]
    convert_element_type x2 -> x0, other arithmetic: 19.5 us -> none  [the longest x1 14.3 us: per_device(): applied = (local_part + nonlocal_part.reshape(band_count, plane_count, wi...]
    gather x6 -> x0, local copies, waits for them, and re-layouts: 13.1 us -> none  [the longest x4 12.3 us: per_device(): field.reshape(band_count, row_count, width_z)[:, gather_rows]]
    dot_general x9 -> x0, matrix products: 12.6 us -> none  [the longest x4 4.95 us: per_device(): jnp.einsum('bet,eit->ebi', field_tiles, projectors, preferred_element_typ...]
    convert_element_type x3 -> x0, local copies, waits for them, and re-layouts: 11.5 us -> none  [the longest x1 4.5 us: per_device(): third_first.astype(jnp.bfloat16)]
    all_to_all x0 -> x1, starting transfers between devices: none -> 8.13 us  [per_device(): gathered = lax.all_to_all(copies, 'band', 0, 0)]
  transfers between devices with their start and end apart: 6 -> 9, of which waited for: 0 -> 2; matrix products, arithmetic and copies ran while one was open for 25% -> 6% of each run, Pallas kernels for 0% -> 38%
where the time goes in v1:
time: 71.6 us; the launch traced here: 71.1 us
  Pallas kernels  27.2 us (38%)
  local copies, waits for them, and re-layouts  20.2 us (28%)
  starting transfers between devices  17 us (24%)
  other arithmetic  2.99 us (4%)
  waiting for transfers between devices  2.92 us (4%)
  between operations  0.8 us (1%)
    pallas_call x1, Pallas kernels, per_device(): pl.pallas_call(functools.partial(local_kernel, width_y=width_y), out_shap...  16.4 us
    unnamed x27, local copies, waits for them, and re-layouts  16 us
    ppermute x8, starting transfers between devices, ring(): lax.ppermute(x, axis, [(i, (i + step) % count) for i in range(count)])  8.89 us
    all_to_all x1, starting transfers between devices, per_device(): gathered = lax.all_to_all(copies, 'band', 0, 0)  8.13 us
    pallas_call x1, Pallas kernels, per_device(): pl.pallas_call(functools.partial(apply_kernel, width_y=width_y), out_shap...  3.81 us
    pallas_call x1, Pallas kernels, per_device(): pl.pallas_call(functools.partial(relayout_kernel, width_y=width_y), out_s...  3.06 us
    slice x1, local copies, waits for them, and re-layouts, per_device(): below = wavefunctions[:, :PAD]  2.35 us
    pallas_call x1, Pallas kernels, per_device(): pl.pallas_call(functools.partial(first_kernel, width_y=width_y), out_shap...  2.35 us
  transfers between devices with their start and end apart: 9, of which 2 were waited for; matrix products, arithmetic and copies ran while one was open for 6% of the time, Pallas kernels for 38%

profile of v1, /device:TPU:0, one launch (start us, length us, event | category | flops | bytes accessed | tf_op | source)
XLA Modules:
  0.0 71.1 jit_solution(13634495353427210678)
XLA Ops:
  0.6 0.0 copy-start.9
  0.6 0.0 copy-start.12
  0.7 0.0 copy-start.7
  0.7 2.4 %fusion.7 = (bf16[8,2,128,128]{3,2,1,0:T(8,128)(2,1)}, bf16[8,2,128,128]{3,2,1,0:T(8,128)(2,1)}) fusion(bf16[8,8,128,128]{3,2,1,0:T(8,128)(2,1)} %wave_ref.1), kind=kLoop, calls=%fused_computation.31 | loop fusion | bytes 2097152 | tf_op jit(solution)/shard_map/slice | solution.py:297
  3.0 0.0 collective-permute-start
  3.0 3.0 %collective-permute-start.1 = (bf16[8,2,128,128]{3,2,1,0:T(8,128)(2,1)}, bf16[8,2,128,128]{3,2,1,0:T(8,128)(2,1)S(1)}, u32[]{:S(2)}, u32[]{:S(2)}) collective-permute-start(bf16[8,2,128,128]{3,2,1,0:T(8,128)(2,1)} %get-tuple-element.18), channel_id=1, source_target_pairs={{0,112},{16,0},{32,16},{48,32},{64,48},{80,64},{96,80},{112,96},{1... | collective-permute-start | bytes 1572872 | tf_op jit(solution)/shard_map/ppermute | solution.py:21
  6.0 0.7 fusion.4
  6.7 0.8 %select_reduce_fusion = (s32[36]{0:T(128)S(1)}, s32[36]{0:T(128)S(1)}) fusion(s32[36]{0:T(128)S(1)} %fusion.4, s32[36]{0:T(128)} %param.11), kind=kLoop, calls=%fused_computation.1 | loop fusion | flops 6408 | bytes 576 | tf_op jit(solution)/shard_map/reduce_sum | solution.py:308
  7.4 0.0 copy-start.3
  7.4 1.6 %copy-done.3 = bf16[8,8,128,128]{3,2,1,0:T(8,128)(2,1)S(1)} copy-done((bf16[8,8,128,128]{3,2,1,0:T(8,128)(2,1)S(1)}, bf16[8,8,128,128]{3,2,1,0:T(8,128)(2,1)}, u32[]{:S(2)}) %copy-start.3) | copy-done | bytes 2097176
  9.0 1.1 %copy-done.6 = bf16[36,8,1024]{2,1,0:T(8,128)(2,1)S(1)} copy-done((bf16[36,8,1024]{2,1,0:T(8,128)(2,1)S(1)}, bf16[36,8,1024]{2,1,0:T(8,128)(2,1)}, u32[]{:S(2)}) %copy-start.6) | copy-done | bytes 589848
  10.1 3.1 %relayout.1 = (f32[12672,128]{1,0:T(8,128)S(1)}, bf16[3,128,1024]{2,1,0:T(8,128)(2,1)S(1)}, f32[3,8,128]{2,1,0:T(8,128)S(1)}) custom-call(s32[36]{0:T(128)S(1)} %get-tuple-element.17.rows_ref, s32[36]{0:T(128)S(1)} %get-tuple-element.16.entry_ref, bf16[8,8,128,128]{3,2,1,0:T(8,128)(2,1)S(1)} %copy-done.3, bf16[36,8,1024]{2,1,0:T(8,128)(2,1)S(1)} %copy-done.6), custom_call_target="tpu_custom_call" | custom-call | flops 10000000 | bytes 10485760 | tf_op jit(solution)/shard_map/relayout/pallas_call | solution.py:311
  13.2 2.7 %copy-done = f32[12672,128]{1,0:T(8,128)} copy-done((f32[12672,128]{1,0:T(8,128)}, f32[12672,128]{1,0:T(8,128)S(1)}, u32[]{:S(2)}) %copy-start) | copy-done | bytes 6488088
  15.9 0.6 slice_bitcast_fusion.2
  16.4 0.0 collective-permute-start.2
  16.4 0.5 collective-permute-start.3
  17.0 0.1 copy.14
  17.0 0.1 tile.4
  17.1 0.5 tile.10
  17.7 0.7 %and_select_fusion.mixing_ref = f32[128,128]{1,0:T(8,128)} fusion(f32[128,128]{1,0:T(8,128)S(1)} %tile.10, s32[128]{0:T(128)S(1)} %and_select_fusion.1, pred[128]{0:T(512)(128)(4,1)S(1)} %broadcast_compare_fusion), kind=kLoop, calls=%fused_computation | loop fusion | flops 49152 | bytes 131712 | tf_op jit(solution)/shard_map/jit(_where)/select_n | solution.py:345
  18.4 2.8 %copy-done.1 = f32[12672,128]{1,0:T(8,128)S(1)} copy-done((f32[12672,128]{1,0:T(8,128)S(1)}, f32[12672,128]{1,0:T(8,128)}, u32[]{:S(2)}) %copy-start.1) | copy-done | bytes 6488088
  21.2 16.4 %local.1 = (f32[8192,128]{1,0:T(8,128)S(1)}, f32[2,3,8,128]{3,2,1,0:T(8,128)S(1)}) custom-call(s32[36]{0:T(128)S(1)} %get-tuple-element.17.rows_ref, f32[12672,128]{1,0:T(8,128)S(1)} %copy-done.1, f32[8,128,128]{2,1,0:T(8,128)S(1)} %copy-done.7, bf16[3,128,1024]{2,1,0:T(8,128)(2,1)S(1)} %get-tuple-element.10.table_ref), custom_call_target="tpu_custom_call" | custom-call | flops 10000000 | bytes 16777216 | tf_op jit(solution)/shard_map/local/pallas_call | solution.py:329
  37.6 2.1 %copy-done.4 = f32[8192,128]{1,0:T(8,128)} copy-done((f32[8192,128]{1,0:T(8,128)}, f32[8192,128]{1,0:T(8,128)S(1)}, u32[]{:S(2)}) %copy-start.4) | copy-done | bytes 4194328
  39.7 0.0 collective-permute-done.2.above_ref
  39.7 0.0 collective-permute-done.3.below_ref
  39.7 0.6 copy-done.10
  40.3 0.0 copy-done.11
  40.3 1.6 %scale.1 = f32[8,128]{1,0:T(8,128)} custom-call(f32[8,128]{1,0:T(8,128)} %get-tuple-element.24.own_ref, f32[8,128]{1,0:T(8,128)} %copy-done.10, f32[8,128]{1,0:T(8,128)} %copy-done.11, f32[128,128]{1,0:T(8,128)} %and_select_fusion.mixing_ref), custom_call_target="tpu_custom_call" | custom-call | tf_op jit(solution)/shard_map/scale/pallas_call | solution.py:346
  41.9 2.4 %collective-permute-start.5 = (f32[8,128]{1,0:T(8,128)}, f32[8,128]{1,0:T(8,128)S(1)}, u32[]{:S(2)}, u32[]{:S(2)}) collective-permute-start(f32[8,128]{1,0:T(8,128)} %scale.1), channel_id=1, source_target_pairs={{0,112},{16,0},{32,16},{48,32},{64,48},{80,64},{96,80},{112,96},{1... | collective-permute-start | bytes 12296 | tf_op jit(solution)/shard_map/ppermute | solution.py:21
  44.4 0.0 collective-permute-start.4
  44.4 0.0 collective-permute-done.low_ref
  44.4 0.0 collective-permute-done.1.high_ref
  44.4 2.8 %copy-done.2 = f32[12672,128]{1,0:T(8,128)S(1)} copy-done((f32[12672,128]{1,0:T(8,128)S(1)}, f32[12672,128]{1,0:T(8,128)}, u32[]{:S(2)}) %copy-start.2) | copy-done | bytes 6488088
  47.2 2.3 %first.1 = (f32[12672,128]{1,0:T(8,128)S(1)}, f32[3,3,8,128]{3,2,1,0:T(8,128)S(1)}) custom-call(s32[36]{0:T(128)S(1)} %get-tuple-element.17.rows_ref, f32[12672,128]{1,0:T(8,128)S(1)} %copy-done.2, bf16[8,2,128,128]{3,2,1,0:T(8,128)(2,1)S(1)} %collective-permute-done.low_ref, ...), custom_call_target="tpu_custom_call", output_to_operand_aliasing={{0}: (1, {})} | custom-call | flops 10000000 | bytes 4194304 | tf_op jit(solution)/shard_map/first/pallas_call | solution.py:356
  49.6 0.0 collective-permute-start.7
  49.6 3.0 %collective-permute-start.6 = (f32[3,8,128]{2,1,0:T(8,128)S(1)}, f32[3,8,128]{2,1,0:T(8,128)S(1)}, u32[]{:S(2)}, u32[]{:S(2)}) collective-permute-start(f32[3,8,128]{2,1,0:T(8,128)S(1)} %get-tuple-element.20), channel_id=1, source_target_pairs={{0,112},{16,0},{32,16},{48,32},{64,48},{80,64},{96,80},{112,96},{1... | collective-permute-start | bytes 36872 | tf_op jit(solution)/shard_map/ppermute | solution.py:21
  52.6 0.1 broadcast_multiply_fusion
  52.6 1.3 %collective-permute-done.7 = f32[3,8,128]{2,1,0:T(8,128)S(1)} collective-permute-done((f32[3,8,128]{2,1,0:T(8,128)S(1)}, f32[3,8,128]{2,1,0:T(8,128)S(1)}, u32[]{:S(2)}, u32[]{:S(2)}) %collective-permute-start.7) | collective-permute-done | bytes 12320 | tf_op jit(solution)/shard_map/ppermute | solution.py:21
  53.9 0.0 collective-permute-done.6
  54.0 0.6 broadcast_in_dim.41
  54.6 8.1 %all-to-all-start = ((f32[16,3,128]{2,1,0:T(4,128)}), f32[16,3,128]{2,1,0:T(4,128)S(1)}, u32[]{:S(2)}, u32[]{:S(2)}) async-start(f32[16,3,128]{2,1,0:T(4,128)} %broadcast_in_dim.41), calls=%async_computation | async-start | bytes 65536 | tf_op jit(solution)/shard_map/all_to_all | solution.py:391
  62.8 0.0 collective-permute-done.5
  62.8 0.0 collective-permute-done.4
  62.8 2.2 %copy-done.5 = f32[8192,128]{1,0:T(8,128)S(1)} copy-done((f32[8192,128]{1,0:T(8,128)S(1)}, f32[8192,128]{1,0:T(8,128)}, u32[]{:S(2)}) %copy-start.5) | copy-done | bytes 4194328
  65.0 3.8 %apply.1 = (f32[8192,128]{1,0:T(8,128)S(1)}, bf16[8,8,128,128]{3,2,1,0:T(8,128)(2,1)}) custom-call(s32[36]{0:T(128)S(1)} %get-tuple-element.17.rows_ref, f32[8192,128]{1,0:T(8,128)S(1)} %copy-done.5, bf16[8,2,128,128]{3,2,1,0:T(8,128)(2,1)S(1)} %collective-permute-done.low_ref, ...), custom_call_target="tpu_custom_call", output_to_operand_aliasing={{0}: (1, {})} | custom-call | flops 10000000 | bytes 8388608 | tf_op jit(solution)/shard_map/apply/pallas_call | solution.py:372
  68.8 1.6 %all-to-all-done = f32[16,3,128]{2,1,0:T(4,128)S(1)} async-done(((f32[16,3,128]{2,1,0:T(4,128)}), f32[16,3,128]{2,1,0:T(4,128)S(1)}, u32[]{:S(2)}, u32[]{:S(2)}) %all-to-all-start) | async-done | bytes 24608 | tf_op jit(solution)/shard_map/all_to_all | solution.py:391
  70.4 0.1 reshape.44
  70.5 0.7 reduce_sum.49
  (21 shorter events, 0.1 us)
Async XLA Ops:
  0.6 16.3 %copy-start.9 = (f32[8,8]{1,0:T(8,128)S(1)}, f32[8,8]{1,0:T(8,128)}, u32[]{:S(2)}) copy-start(f32[8,8]{1,0:T(8,128)} %param.12) | copy-start | bytes 772
  0.6 17.7 %copy-start.12 = (f32[8]{0:T(128)S(1)}, f32[8]{0:T(128)}, u32[]{:S(2)}) copy-start(f32[8]{0:T(128)} %param.13) | copy-start | bytes 100
  0.7 17.7 %copy-start.7 = (f32[8,128,128]{2,1,0:T(8,128)S(1)}, f32[8,128,128]{2,1,0:T(8,128)}, u32[]{:S(2)}) copy-start(f32[8,128,128]{2,1,0:T(8,128)} %pot_ref.1) | copy-start | bytes 1572868
  3.0 41.3 %collective-permute-start = (bf16[8,2,128,128]{3,2,1,0:T(8,128)(2,1)}, bf16[8,2,128,128]{3,2,1,0:T(8,128)(2,1)S(1)}, u32[]{:S(2)}, u32[]{:S(2)}) collective-permute-start(bf16[8,2,128,128]{3,2,1,0:T(8,128)(2,1)} %get-tuple-element.19), channel_id=1, source_target_pairs={{0,16},{16,32},{32,48},{48,64},{64,80},{80,96},{96,112},{112,0},{1... | collective-permute-start | bytes 1572872 | tf_op jit(solution)/shard_map/ppermute | solution.py:21
  3.0 41.3 %collective-permute-start.1 = (bf16[8,2,128,128]{3,2,1,0:T(8,128)(2,1)}, bf16[8,2,128,128]{3,2,1,0:T(8,128)(2,1)S(1)}, u32[]{:S(2)}, u32[]{:S(2)}) collective-permute-start(bf16[8,2,128,128]{3,2,1,0:T(8,128)(2,1)} %get-tuple-element.18), channel_id=1, source_target_pairs={{0,112},{16,0},{32,16},{48,32},{64,48},{80,64},{96,80},{112,96},{1... | collective-permute-start | bytes 1572872 | tf_op jit(solution)/shard_map/ppermute | solution.py:21
  7.4 1.6 %copy-start.3 = (bf16[8,8,128,128]{3,2,1,0:T(8,128)(2,1)S(1)}, bf16[8,8,128,128]{3,2,1,0:T(8,128)(2,1)}, u32[]{:S(2)}) copy-start(bf16[8,8,128,128]{3,2,1,0:T(8,128)(2,1)} %wave_ref.1) | copy-start | bytes 6291460
  9.0 1.1 %copy-start.6 = (bf16[36,8,1024]{2,1,0:T(8,128)(2,1)S(1)}, bf16[36,8,1024]{2,1,0:T(8,128)(2,1)}, u32[]{:S(2)}) copy-start(bf16[36,8,1024]{2,1,0:T(8,128)(2,1)} %proj_ref.1) | copy-start | bytes 1769476
  13.1 2.7 %copy-start = (f32[12672,128]{1,0:T(8,128)}, f32[12672,128]{1,0:T(8,128)S(1)}, u32[]{:S(2)}) copy-start(f32[12672,128]{1,0:T(8,128)S(1)} %get-tuple-element.9.grid_ref.grid_in) | copy-start | bytes 19464196
  16.4 23.2 %collective-permute-start.2 = (f32[8,128]{1,0:T(8,128)S(1)}, f32[8,128]{1,0:T(8,128)S(1)}, u32[]{:S(2)}, u32[]{:S(2)}) collective-permute-start(f32[8,128]{1,0:T(8,128)S(1)} %get-tuple-element.23), channel_id=1, source_target_pairs={{0,112},{16,0},{32,16},{48,32},{64,48},{80,64},{96,80},{112,96},{1... | collective-permute-start | bytes 12296 | tf_op jit(solution)/shard_map/ppermute | solution.py:21
  16.4 23.2 %collective-permute-start.3 = (f32[8,128]{1,0:T(8,128)S(1)}, f32[8,128]{1,0:T(8,128)S(1)}, u32[]{:S(2)}, u32[]{:S(2)}) collective-permute-start(f32[8,128]{1,0:T(8,128)S(1)} %get-tuple-element.22), channel_id=1, source_target_pairs={{0,16},{16,32},{32,48},{48,64},{64,80},{80,96},{96,112},{112,0},{1... | collective-permute-start | bytes 12296 | tf_op jit(solution)/shard_map/ppermute | solution.py:21
  18.4 2.8 %copy-start.1 = (f32[12672,128]{1,0:T(8,128)S(1)}, f32[12672,128]{1,0:T(8,128)}, u32[]{:S(2)}) copy-start(f32[12672,128]{1,0:T(8,128)} %copy-done) | copy-start | bytes 19464196
  37.6 2.1 %copy-start.4 = (f32[8192,128]{1,0:T(8,128)}, f32[8192,128]{1,0:T(8,128)S(1)}, u32[]{:S(2)}) copy-start(f32[8192,128]{1,0:T(8,128)S(1)} %get-tuple-element.11.local_in) | copy-start | bytes 12582916
  39.7 0.6 copy-start.10
  39.7 0.6 copy-start.11
  41.9 20.8 %collective-permute-start.5 = (f32[8,128]{1,0:T(8,128)}, f32[8,128]{1,0:T(8,128)S(1)}, u32[]{:S(2)}, u32[]{:S(2)}) collective-permute-start(f32[8,128]{1,0:T(8,128)} %scale.1), channel_id=1, source_target_pairs={{0,112},{16,0},{32,16},{48,32},{64,48},{80,64},{96,80},{112,96},{1... | collective-permute-start | bytes 12296 | tf_op jit(solution)/shard_map/ppermute | solution.py:21
  44.4 18.4 %collective-permute-start.4 = (f32[8,128]{1,0:T(8,128)}, f32[8,128]{1,0:T(8,128)S(1)}, u32[]{:S(2)}, u32[]{:S(2)}) collective-permute-start(f32[8,128]{1,0:T(8,128)} %scale.1), channel_id=1, source_target_pairs={{0,16},{16,32},{32,48},{48,64},{64,80},{80,96},{96,112},{112,0},{1... | collective-permute-start | bytes 12296 | tf_op jit(solution)/shard_map/ppermute | solution.py:21
  44.4 2.8 %copy-start.2 = (f32[12672,128]{1,0:T(8,128)S(1)}, f32[12672,128]{1,0:T(8,128)}, u32[]{:S(2)}) copy-start(f32[12672,128]{1,0:T(8,128)} %copy-done) | copy-start | bytes 19464196
  47.2 5.4 %copy-start.8 = (f32[8,128]{1,0:T(8,128)S(1)}, f32[8,128]{1,0:T(8,128)}, u32[]{:S(2)}) copy-start(f32[8,128]{1,0:T(8,128)} %scale.1) | copy-start | bytes 12292
  49.6 4.3 %collective-permute-start.7 = (f32[3,8,128]{2,1,0:T(8,128)S(1)}, f32[3,8,128]{2,1,0:T(8,128)S(1)}, u32[]{:S(2)}, u32[]{:S(2)}) collective-permute-start(f32[3,8,128]{2,1,0:T(8,128)S(1)} %get-tuple-element.21), channel_id=1, source_target_pairs={{0,16},{16,32},{32,48},{48,64},{64,80},{80,96},{96,112},{112,0},{1... | collective-permute-start | bytes 36872 | tf_op jit(solution)/shard_map/ppermute | solution.py:21
  49.6 4.4 %collective-permute-start.6 = (f32[3,8,128]{2,1,0:T(8,128)S(1)}, f32[3,8,128]{2,1,0:T(8,128)S(1)}, u32[]{:S(2)}, u32[]{:S(2)}) collective-permute-start(f32[3,8,128]{2,1,0:T(8,128)S(1)} %get-tuple-element.20), channel_id=1, source_target_pairs={{0,112},{16,0},{32,16},{48,32},{64,48},{80,64},{96,80},{112,96},{1... | collective-permute-start | bytes 36872 | tf_op jit(solution)/shard_map/ppermute | solution.py:21
  54.6 15.7 %all-to-all-start = ((f32[16,3,128]{2,1,0:T(4,128)}), f32[16,3,128]{2,1,0:T(4,128)S(1)}, u32[]{:S(2)}, u32[]{:S(2)}) async-start(f32[16,3,128]{2,1,0:T(4,128)} %broadcast_in_dim.41), calls=%async_computation | async-start | bytes 65536 | tf_op jit(solution)/shard_map/all_to_all | solution.py:391
  62.8 2.2 %copy-start.5 = (f32[8192,128]{1,0:T(8,128)S(1)}, f32[8192,128]{1,0:T(8,128)}, u32[]{:S(2)}) copy-start(f32[8192,128]{1,0:T(8,128)} %copy-done.4) | copy-start | bytes 12582916

commit v2 on v1

v2 whole, which is shorter than its diff:
```python
import functools

import jax
import jax.numpy as jnp
from jax import lax
from jax.experimental import pallas as pl
from jax.experimental.pallas import tpu as pltpu
from jax.sharding import PartitionSpec as P

ATOM_DEV = 12
GROUPS = 3
LANES = 128
PAD = 2

f32 = jnp.float32
bf16 = jnp.bfloat16


def ring(x, axis, step):
    count = lax.axis_size(axis)
    return lax.ppermute(x, axis, [(i, (i + step) % count) for i in range(count)])


def to_rows(src, b, plane, y0, dst, base):
    part = src[b, plane, pl.ds(y0, 16), :].astype(f32)
    dst[pl.ds(base + b, 16, stride=8), :] = part


def tile_base(first_row, k, width_y):
    row = first_row + k
    plane = lax.shift_right_logical(row, 7)
    return (row + plane * (2 * PAD) + PAD + PAD * (width_y + 2 * PAD)) * 8


def at_row(ref, base):
    return ref[pl.ds(pl.multiple_of(base, 8), 8), :]


def diagonal_blocks(product, field):
    lane = lax.broadcasted_iota(jnp.int32, (8, LANES), 1)
    total = jnp.zeros((8, LANES), f32)
    for s in range(ATOM_DEV):
        start = (field * ATOM_DEV + s) * 8
        total = total + jnp.where(
            lax.shift_right_logical(lane, 3) == s, product[start : start + 8, :], 0.0
        )
    return total


def measure(rows_ref, group, table, width_y, fields):
    stacked = []
    for field in fields:
        for s in range(ATOM_DEV):
            first = rows_ref[group * ATOM_DEV + s]
            stacked.append(
                jnp.concatenate(
                    [field(tile_base(first, k, width_y)) for k in range(8)], axis=1
                )
            )
    values = jnp.concatenate(stacked, axis=0).astype(bf16)
    product = lax.dot_general(
        values, table, (((1,), (1,)), ((), ())), preferred_element_type=f32
    )
    return [diagonal_blocks(product, q) for q in range(len(fields))]


def edge_kernel(wave_ref, below_ref, above_ref, sems):
    planes = wave_ref.shape[1]
    copies = [
        pltpu.make_async_copy(wave_ref.at[:, pl.ds(0, PAD)], below_ref, sems.at[0]),
        pltpu.make_async_copy(wave_ref.at[:, pl.ds(planes - PAD, PAD)], above_ref, sems.at[1]),
    ]
    for copy in copies:
        copy.start()
    for copy in copies:
        copy.wait()


def relayout_kernel(
    own_ref,
    atoms_hbm,
    first_rows_hbm,
    wave_hbm,
    proj_hbm,
    rows_ref,
    wave_ref,
    grid_ref,
    table_ref,
    low_ref,
    mid_ref,
    high_ref,
    entry_ref,
    atoms_ref,
    first_rows_ref,
    proj_ref,
    proj_scr,
    wave_sems,
    other_sems,
    *,
    width_y,
    domain_count,
):
    stride = width_y + 2 * PAD
    planes = wave_ref.shape[1]
    chunks = width_y // 16

    def plane_copy(plane):
        at_plane = (slice(None), pl.ds(plane, 1))
        return pltpu.make_async_copy(
            wave_hbm.at[at_plane], wave_ref.at[at_plane], wave_sems.at[plane]
        )

    proj_copy = pltpu.make_async_copy(proj_hbm, proj_ref, other_sems.at[0])
    atoms_copy = pltpu.make_async_copy(atoms_hbm, atoms_ref, other_sems.at[1])
    rows_copy = pltpu.make_async_copy(first_rows_hbm, first_rows_ref, other_sems.at[2])
    atoms_copy.start()
    rows_copy.start()
    for plane in range(planes):
        plane_copy(plane).start()
    proj_copy.start()

    def clear(step, carry):
        for plane in (0, 1, planes + PAD, planes + PAD + 1):
            base = pl.multiple_of((plane * stride + PAD + step * 8) * 8, 8)
            grid_ref[pl.ds(base, 64), :] = jnp.zeros((64, LANES), f32)
        return carry

    lax.fori_loop(0, width_y // 8, clear, 0)

    atoms_copy.wait()
    rows_copy.wait()

    def place(entry, carry):
        atom = atoms_ref[entry]
        owner = lax.shift_right_logical(atom * 171, 11)
        relative = lax.rem(owner - own_ref[0] + 1 + domain_count, domain_count)
        slot = relative * ATOM_DEV + atom - owner * ATOM_DEV
        entry_ref[slot] = entry
        rows_ref[slot] = first_rows_ref[entry]
        return carry

    lax.fori_loop(0, GROUPS * ATOM_DEV, place, 0)

    def one_plane(plane, carry):
        plane_copy(plane).wait()

        def convert(step, inner):
            y0 = pl.multiple_of(step * 16, 16)
            base = ((plane + PAD) * stride + PAD + y0) * 8
            for b in range(8):
                to_rows(wave_ref, b, plane, y0, grid_ref, base)
            return inner

        lax.fori_loop(0, chunks, convert, 0)
        base = pl.multiple_of((plane + PAD) * stride * 8, 8)
        grid_ref[pl.ds(base, 8 * PAD), :] = grid_ref[pl.ds(base + width_y * 8, 8 * PAD), :]
        grid_ref[pl.ds(base + (width_y + PAD) * 8, 8 * PAD), :] = grid_ref[
            pl.ds(base + PAD * 8, 8 * PAD), :
        ]
        return carry

    lax.fori_loop(0, planes, one_plane, 0)
    proj_copy.wait()
    proj_scr[ATOM_DEV * 8 :, :] = jnp.zeros((LANES - ATOM_DEV * 8, proj_scr.shape[1]), f32)
    for group, margin_ref in enumerate((low_ref, mid_ref, high_ref)):
        for s in range(ATOM_DEV):
            entry = entry_ref[group * ATOM_DEV + s]
            proj_scr[s * 8 : s * 8 + 8, :] = proj_ref[entry].astype(f32)
        table = proj_scr[...].astype(bf16)
        table_ref[group] = table
        (margin_ref[...],) = measure(
            rows_ref, group, table, width_y, [lambda base: at_row(grid_ref, base)]
        )


def third_shift(center, offset):
    return pltpu.roll(center, (-offset) % center.shape[-1], 1)


def circulant(near, far, center, length):
    row = lax.broadcasted_iota(jnp.int32, (length, length), 0)
    column = lax.broadcasted_iota(jnp.int32, (length, length), 1)
    distance = lax.bitwise_and(row - column, length - 1)
    table = jnp.where((distance == 1) | (distance == length - 1), near, 0.0)
    table = jnp.where((distance == 2) | (distance == length - 2), far, table)
    return jnp.where(distance == 0, center, table).astype(bf16)


def local_kernel(wave_ref, pot_ref, local_ref, token_ref):
    token_ref[...] = jnp.zeros(token_ref.shape, f32)
    bands, planes, width_y, width_z = wave_ref.shape
    along_y = circulant(-16.0, 1.0, 0.0, width_y)
    along_z = circulant(-16.0, 1.0, 90.0, width_z)

    def one_band(b, carry):
        for plane in range(planes):
            wave = wave_ref[b, plane]
            summed = jnp.dot(
                jnp.concatenate([wave, along_y], axis=1),
                jnp.concatenate([along_z, wave], axis=0),
                preferred_element_type=f32,
            )
            for offset, factor in ((1, -16.0), (2, 1.0)):
                sides = [q for q in (plane - offset, plane + offset) if 0 <= q < planes]
                side = wave_ref[b, sides[0]].astype(f32)
                for q in sides[1:]:
                    side = side + wave_ref[b, q].astype(f32)
                summed = summed + (side if factor == 1.0 else factor * side)
            local_ref[pl.ds(plane * width_y * bands + b, width_y, stride=bands), :] = (
                summed * (1.0 / 24.0) + pot_ref[plane] * wave.astype(f32)
            )
        return carry

    lax.fori_loop(0, bands, one_band, 0)


def gradient_kernel(rows_ref, grid_ref, table_ref, coupling_ref, margin_ref, mixing_ref, *, width_y):
    def along_y(base):
        near = at_row(grid_ref, base + 8) - at_row(grid_ref, base - 8)
        far = at_row(grid_ref, base + 16) - at_row(grid_ref, base - 16)
        return (2.0 / 3.0) * near - (1.0 / 12.0) * far

    def along_z(base):
        center = at_row(grid_ref, base)
        near = third_shift(center, 1) - third_shift(center, -1)
        far = third_shift(center, 2) - third_shift(center, -2)
        return (2.0 / 3.0) * near - (1.0 / 12.0) * far

    for group in range(GROUPS):
        second, third = measure(rows_ref, group, table_ref[group], width_y, [along_y, along_z])
        margin_ref[0, group] = second
        margin_ref[1, group] = third

    proj_count = coupling_ref.shape[0]
    symmetric = 0.5 * (coupling_ref[...] + coupling_ref[...].T)
    index = lax.broadcasted_iota(jnp.int32, (proj_count, LANES), 0)
    lane = lax.broadcasted_iota(jnp.int32, (proj_count, LANES), 1)
    spread = (lax.bitwise_and(lane, proj_count - 1) == index).astype(f32)
    tiled = jnp.dot(
        symmetric, spread, precision=lax.Precision.HIGHEST, preferred_element_type=f32
    )
    for a in range(LANES // proj_count):
        keep = (lax.shift_right_logical(lane, 3) == a) & (lane < ATOM_DEV * proj_count)
        mixing_ref[a * proj_count : (a + 1) * proj_count, :] = jnp.where(keep, tiled, 0.0)


def first_kernel(
    rows_ref,
    grid_in,
    low_ref,
    high_ref,
    table_ref,
    yz_ref,
    scaled_ref,
    grid_ref,
    low_out,
    mid_out,
    high_out,
    *,
    width_y,
):
    del grid_in
    stride = width_y + 2 * PAD
    planes = grid_ref.shape[0] // (8 * stride) - 2 * PAD
    chunks = width_y // 16
    hop = stride * 8

    def convert(step, carry):
        y0 = pl.multiple_of(step * 16, 16)
        for plane in range(PAD):
            low = (plane * stride + PAD + y0) * 8
            high = ((plane + planes + PAD) * stride + PAD + y0) * 8
            for b in range(8):
                to_rows(low_ref, b, plane, y0, grid_ref, low)
                to_rows(high_ref, b, plane, y0, grid_ref, high)
        return carry

    lax.fori_loop(0, chunks, convert, 0)

    def along_x(base):
        near = at_row(grid_ref, base + hop) - at_row(grid_ref, base - hop)
        far = at_row(grid_ref, base + 2 * hop) - at_row(grid_ref, base - 2 * hop)
        return (2.0 / 3.0) * near - (1.0 / 12.0) * far

    for group, margin_ref in enumerate((low_out, mid_out, high_out)):
        (first,) = measure(rows_ref, group, table_ref[group], width_y, [along_x])
        margin_ref[0] = first
        margin_ref[1] = yz_ref[0, group]
        margin_ref[2] = yz_ref[1, group]
        margin_ref[3] = scaled_ref[...]


def apply_kernel(
    rows_ref,
    local_in,
    low_ref,
    high_ref,
    table_ref,
    scaled_low_ref,
    scaled_ref,
    scaled_high_ref,
    local_ref,
    out_hbm,
    out_ref,
    sems,
):
    del local_in
    bands, planes, width_y, _ = out_ref.shape
    chunks = width_y // 16
    lane = lax.broadcasted_iota(jnp.int32, (8, LANES), 1)

    for group, source in enumerate((scaled_low_ref, scaled_ref, scaled_high_ref)):
        scaled = source[3]
        blocks = [
            jnp.where(lax.shift_right_logical(lane, 3) == s, scaled, 0.0)
            for s in range(ATOM_DEV)
        ]
        coef = jnp.concatenate(blocks, axis=0).astype(bf16)
        terms = jnp.dot(coef, table_ref[group], preferred_element_type=f32)
        for s in range(ATOM_DEV):
            base = pl.multiple_of(rows_ref[group * ATOM_DEV + s] * 8, 8)
            for k in range(8):
                where = pl.ds(base + k * 8, 8)
                local_ref[where, :] = (
                    local_ref[where, :] + terms[s * 8 : s * 8 + 8, k * LANES : (k + 1) * LANES]
                )

    def plane_copy(plane):
        at_plane = (slice(None), pl.ds(plane, 1))
        return pltpu.make_async_copy(out_ref.at[at_plane], out_hbm.at[at_plane], sems.at[plane])

    near, far = -2.0 / 3.0, 1.0 / 24.0
    halo_terms = {
        0: ((low_ref, 1, near), (low_ref, 0, far)),
        1: ((low_ref, 1, far),),
        planes - 2: ((high_ref, 0, far),),
        planes - 1: ((high_ref, 0, near), (high_ref, 1, far)),
    }
    for plane in range(planes):

        def finish(step, carry, plane=plane):
            y0 = pl.multiple_of(step * 16, 16)
            at_y = pl.ds(y0, 16)
            for b in range(bands):
                base = (plane * width_y + y0) * 8 + b
                value = local_ref[pl.ds(base, 16, stride=8), :]
                for ref, index, factor in halo_terms.get(plane, ()):
                    value = value + factor * ref[b, index, at_y, :].astype(f32)
                out_ref[b, plane, at_y, :] = value.astype(bf16)
            return carry

        lax.fori_loop(0, chunks, finish, 0)
        plane_copy(plane).start()
    for plane in range(planes):
        plane_copy(plane).wait()


def weigh_kernel(own_ref, above_ref, below_ref, weight_ref, _, copies_ref):
    weighted = -2.0 * weight_ref[...] * own_ref[3]
    parts = []
    for k in range(3):
        total = own_ref[k] + above_ref[k] + below_ref[k]
        parts.append(jnp.sum(total * weighted, axis=0, keepdims=True))
    parts = jnp.concatenate(parts, axis=0)
    for copy in range(copies_ref.shape[0]):
        copies_ref[copy] = parts


def scale_kernel(own_ref, above_ref, below_ref, mixing_ref, scaled_ref):
    total = own_ref[...] + above_ref[...] + below_ref[...]
    scaled_ref[...] = jnp.dot(
        total, mixing_ref[...], precision=lax.Precision.HIGHEST, preferred_element_type=f32
    )


VMEM = pl.BlockSpec(memory_space=pltpu.VMEM)
SMEM = pl.BlockSpec(memory_space=pltpu.SMEM)
HBM = pl.BlockSpec(memory_space=pltpu.HBM)
MIB = 2**20


def in_hbm(x):
    return pltpu.with_memory_space_constraint(x, pltpu.HBM)


def call(kernel, name, outs, ins, out_specs, scratch=(), limit=8, **kwargs):
    return pl.pallas_call(
        kernel,
        out_shape=tuple(
            pltpu.HBM(shape, dtype) if spec is HBM else jax.ShapeDtypeStruct(shape, dtype)
            for (shape, dtype), spec in zip(outs, out_specs)
        ),
        in_specs=ins,
        out_specs=tuple(out_specs),
        scratch_shapes=list(scratch),
        compiler_params=pltpu.CompilerParams(vmem_limit_bytes=limit * MIB),
        cost_estimate=pl.CostEstimate(flops=1000, bytes_accessed=1000, transcendentals=0),
        name=name,
        **kwargs,
    )


def per_device(
    wavefunctions, potential, projectors, margin_atoms, tile_rows, coupling, band_weights
):
    band_count, plane_count, width_y, width_z = wavefunctions.shape
    entry_count, proj_count, tile_len = projectors.shape
    assert (band_count, proj_count, width_y, width_z) == (8, 8, 128, LANES)
    assert entry_count == GROUPS * ATOM_DEV
    grid_rows = (plane_count + 2 * PAD) * (width_y + 2 * PAD) * 8
    block = ((8, LANES), f32)
    blocks = ((4, 8, LANES), f32)
    edge = ((band_count, PAD, width_y, width_z), bf16)

    below, above = call(
        edge_kernel,
        "edges",
        [edge, edge],
        [HBM],
        [VMEM, VMEM],
        [pltpu.SemaphoreType.DMA((2,))],
    )(in_hbm(wavefunctions))
    high_halo = ring(below, "dom", -1)
    low_halo = ring(above, "dom", 1)

    own_index = lax.axis_index("dom").astype(jnp.int32).reshape(1)
    rows, wave, grid, table, low, mid, high = call(
        functools.partial(
            relayout_kernel, width_y=width_y, domain_count=lax.axis_size("dom")
        ),
        "relayout",
        [
            ((entry_count,), jnp.int32),
            (wavefunctions.shape, bf16),
            ((grid_rows, LANES), f32),
            ((GROUPS, LANES, tile_len), bf16),
            block,
            block,
            block,
        ],
        [SMEM, HBM, HBM, HBM, HBM],
        [SMEM] + [VMEM] * 6,
        [
            pltpu.SMEM((entry_count,), jnp.int32),
            pltpu.SMEM((entry_count,), jnp.int32),
            pltpu.SMEM((entry_count,), jnp.int32),
            pltpu.VMEM(projectors.shape, bf16),
            pltpu.VMEM((LANES, tile_len), f32),
            pltpu.SemaphoreType.DMA((plane_count,)),
            pltpu.SemaphoreType.DMA((3,)),
        ],
    )(own_index, *map(in_hbm, (margin_atoms, tile_rows, wavefunctions, projectors)))

    from_above = ring(low, "dom", -1)
    from_below = ring(high, "dom", 1)

    yz_margins, mixing = call(
        functools.partial(gradient_kernel, width_y=width_y),
        "gradient",
        [((2, GROUPS, 8, LANES), f32), ((LANES, LANES), f32)],
        [SMEM] + [VMEM] * 3,
        [VMEM, VMEM],
    )(rows, grid, table, coupling)

    local, token = call(
        local_kernel,
        "local",
        [((plane_count * width_y * 8, LANES), f32), block],
        [VMEM, VMEM],
        [VMEM, VMEM],
    )(wave, potential)

    (scaled,) = call(scale_kernel, "scale", [block], [VMEM] * 4, [VMEM], limit=2)(
        mid, from_above, from_below, mixing
    )
    _, low_sums, mid_sums, high_sums = call(
        functools.partial(first_kernel, width_y=width_y),
        "first",
        [((grid_rows, LANES), f32), blocks, blocks, blocks],
        [SMEM] + [VMEM] * 6,
        [VMEM] * 4,
        input_output_aliases={1: 0},
    )(rows, grid, low_halo, high_halo, table, yz_margins, scaled)
    sums_above = ring(low_sums, "dom", -1)
    sums_below = ring(high_sums, "dom", 1)

    (copies,) = call(
        weigh_kernel,
        "weigh",
        [((lax.axis_size("band"), 3, LANES), f32)],
        [VMEM] * 5,
        [VMEM],
        limit=2,
    )(mid_sums, sums_above, sums_below, band_weights[:, None], token)

    _, applied = call(
        apply_kernel,
        "apply",
        [((plane_count * width_y * 8, LANES), f32), (wavefunctions.shape, bf16)],
        [SMEM] + [VMEM] * 7,
        [VMEM, HBM],
        [
            pltpu.VMEM(wavefunctions.shape, bf16),
            pltpu.SemaphoreType.DMA((plane_count,)),
        ],
        input_output_aliases={1: 0},
    )(rows, local, low_halo, high_halo, table, sums_below, mid_sums, sums_above)

    gathered = lax.all_to_all(copies, "band", 0, 0)
    summed = gathered.sum(0)[:, : ATOM_DEV * proj_count]
    forces = summed.reshape(3, ATOM_DEV, proj_count).sum(2)
    return (applied, forces)


def solution(mesh):
    placed = (
        P("band", "dom", None, None),
        P("dom", None, None),
        P("dom", None, None),
        P("dom"),
        P("dom"),
        P(),
        P("band"),
    )
    return jax.shard_map(
        per_device,
        mesh=mesh,
        in_specs=placed,
        out_specs=(P("band", "dom", None, None), P(None, "dom")),
        check_vma=False,
    )
```

time: 71.6 us -> 40.7 us (0.57)
  local copies, waits for them, and re-layouts: 20.2 us -> 4.3 us
  Pallas kernels: 27.2 us -> 16.3 us
  starting transfers between devices: 17 us -> 14.6 us
  other arithmetic: 2.99 us -> 0.7 us
  waiting for transfers between devices: 2.92 us -> 3.86 us
    unnamed x27 -> x10, local copies, waits for them, and re-layouts: 16 us -> 4.13 us
    pallas_call x5 -> x8, Pallas kernels: 27.2 us -> 16.3 us  [the longest x1 3.83 us: per_device(): call(functools.partial(relayout_kernel, width_y=width_y, domain_count=lax...]
    ppermute x8 -> x6, starting transfers between devices: 8.89 us -> 6.44 us  [ring(): lax.ppermute(x, axis, [(i, (i + step) % count) for i in range(count)])]
    slice x1 -> x0, local copies, waits for them, and re-layouts: 2.35 us -> none  [per_device(): below = wavefunctions[:, :PAD]]
    all_to_all x1, waiting for transfers between devices: 1.57 us -> 2.5 us  [per_device(): gathered = lax.all_to_all(copies, 'band', 0, 0)]
    reduce_sum x2 -> x0, other arithmetic: 0.79 us -> none  [the longest x1 0.77 us: per_device(): jnp.where(hit, jnp.arange(entry_count, dtype=jnp.int32)[None, :], 0).sum(1)]
    select_n x2 -> x0, other arithmetic: 0.73 us -> none  [the longest x1 0.73 us: per_device(): jnp.where(same, jnp.tile(symmetric, (LANES // proj_count,) * 2), 0.0)]
  transfers between devices with their start and end apart: 9 -> 7, of which waited for: 2 -> 2; matrix products, arithmetic and copies ran while one was open for 6% -> 0% of each run, Pallas kernels for 38% -> 30%
where the time goes in v2:
time: 40.7 us; the launch traced here: 40.5 us
  Pallas kernels  16.3 us (40%)
  starting transfers between devices  14.6 us (36%)
  local copies, waits for them, and re-layouts  4.3 us (11%)
  waiting for transfers between devices  3.86 us (9%)
  between operations  0.74 us (2%)
  other arithmetic  0.7 us (2%)
    all_to_all x1, starting transfers between devices, per_device(): gathered = lax.all_to_all(copies, 'band', 0, 0)  8.13 us
    ppermute x6, starting transfers between devices, ring(): lax.ppermute(x, axis, [(i, (i + step) % count) for i in range(count)])  6.44 us
    unnamed x10, local copies, waits for them, and re-layouts  4.13 us
    pallas_call x1, Pallas kernels, per_device(): call(functools.partial(relayout_kernel, width_y=width_y, domain_count=lax...  3.83 us
    pallas_call x1, Pallas kernels, per_device(): call(local_kernel, 'local', [((plane_count * width_y * 8, LANES), f32), b...  2.96 us
    pallas_call x1, Pallas kernels, per_device(): call(apply_kernel, 'apply', [((plane_count * width_y * 8, LANES), f32), (...  2.9 us
    all_to_all x1, waiting for transfers between devices, per_device(): gathered = lax.all_to_all(copies, 'band', 0, 0)  2.5 us
    pallas_call x1, Pallas kernels, per_device(): call(functools.partial(gradient_kernel, width_y=width_y), 'gradient', [((...  2.41 us
  transfers between devices with their start and end apart: 7, of which 2 were waited for; matrix products, arithmetic and copies ran while one was open for 0% of the time, Pallas kernels for 30%

profile of v2, /device:TPU:0, one launch (start us, length us, event | category | flops | bytes accessed | tf_op | source)
XLA Modules:
  0.0 40.5 jit_solution(11816560502974839762)
XLA Ops:
  0.6 0.0 copy-start.3
  0.6 1.2 %edges.1 = (bf16[8,2,128,128]{3,2,1,0:T(8,128)(2,1)S(1)}, bf16[8,2,128,128]{3,2,1,0:T(8,128)(2,1)S(1)}) custom-call(bf16[8,8,128,128]{3,2,1,0:T(8,128)(2,1)} %wave_ref.1), custom_call_target="tpu_custom_call" | custom-call | flops 1000 | bytes 1000 | tf_op jit(solution)/shard_map/edges/pallas_call | solution.py:415
  1.9 0.0 collective-permute-start
  1.9 2.9 %collective-permute-start.1 = (bf16[8,2,128,128]{3,2,1,0:T(8,128)(2,1)S(1)}, bf16[8,2,128,128]{3,2,1,0:T(8,128)(2,1)S(1)}, u32[]{:S(2)}, u32[]{:S(2)}) collective-permute-start(bf16[8,2,128,128]{3,2,1,0:T(8,128)(2,1)S(1)} %get-tuple-element.23), channel_id=1, source_target_pairs={{0,112},{16,0},{32,16},{48,32},{64,48},{80,64},{96,80},{112,96},{1... | collective-permute-start | bytes 1572872 | tf_op jit(solution)/shard_map/ppermute | solution.py:21
  4.8 3.8 %relayout.1 = (s32[36]{0:T(128)S(1)}, bf16[8,8,128,128]{3,2,1,0:T(8,128)(2,1)S(1)}, f32[12672,128]{1,0:T(8,128)S(1)}, bf16[3,128,1024]{2,1,0:T(8,128)(2,1)S(1)},...) custom-call(s32[1]{0:T(128)} %bitcast.own_ref, s32[36]{0:T(128)} %atoms_hbm.1, ...), custom_call_target="tpu_custom_call" | custom-call | flops 1000 | bytes 1000 | tf_op jit(solution)/shard_map/relayout/pallas_call | solution.py:427
  8.7 0.0 collective-permute-start.2
  8.7 0.5 %collective-permute-start.3 = (f32[8,128]{1,0:T(8,128)S(1)}, f32[8,128]{1,0:T(8,128)S(1)}, u32[]{:S(2)}, u32[]{:S(2)}) collective-permute-start(f32[8,128]{1,0:T(8,128)S(1)} %get-tuple-element.29), channel_id=1, source_target_pairs={{0,16},{16,32},{32,48},{48,64},{64,80},{80,96},{96,112},{112,0},{1... | collective-permute-start | bytes 12296 | tf_op jit(solution)/shard_map/ppermute | solution.py:21
  9.2 0.0 copy-done.3
  9.2 2.4 %gradient.1 = (f32[2,3,8,128]{3,2,1,0:T(8,128)S(1)}, f32[128,128]{1,0:T(8,128)S(1)}) custom-call(s32[36]{0:T(128)S(1)} %get-tuple-element.19.rows_ref, f32[12672,128]{1,0:T(8,128)S(1)} %get-tuple-element.25.grid_ref.grid_in, bf16[3,128,1024]{2,1,0:T(8,128)(2,1)S(1)} %get-tuple-element.24.table_ref, f32[8,8]{1,0:T(8,128)S(1)} %copy-done.3), custom_call_target="tpu_custom_call" | custom-call | flops 1000 | bytes 1000 | tf_op jit(solution)/shard_map/gradient/pallas_call | solution.py:457
  11.6 0.0 collective-permute-done.2.above_ref
  11.6 1.3 %collective-permute-done.3.below_ref = f32[8,128]{1,0:T(8,128)S(1)} collective-permute-done((f32[8,128]{1,0:T(8,128)S(1)}, f32[8,128]{1,0:T(8,128)S(1)}, u32[]{:S(2)}, u32[]{:S(2)}) %collective-permute-start.3) | collective-permute-done | bytes 4128 | tf_op jit(solution)/shard_map/ppermute | solution.py:21
  13.0 0.2 scale.1.scaled_ref
  13.1 0.0 copy-start.2
  13.1 0.0 collective-permute-done.low_ref
  13.1 0.0 collective-permute-done.1.high_ref
  13.1 0.0 copy-start.4
  13.1 2.1 %first.1 = (f32[12672,128]{1,0:T(8,128)S(1)}, f32[4,8,128]{2,1,0:T(8,128)S(1)}, f32[4,8,128]{2,1,0:T(8,128)S(1)}, f32[4,8,128]{2,1,0:T(8,128)S(1)}) custom-call(s32[36]{0:T(128)S(1)} %get-tuple-element.19.rows_ref, f32[12672,128]{1,0:T(8,128)S(1)} %get-tuple-element.25.grid_ref.grid_in, ...), custom_call_target="tpu_custom_call", output_to_operand_aliasing={{0}: (1, {})} | custom-call | flops 1000 | bytes 1000 | tf_op jit(solution)/shard_map/first/pallas_call | solution.py:476
  15.3 0.0 collective-permute-start.4
  15.3 3.0 %collective-permute-start.5 = (f32[4,8,128]{2,1,0:T(8,128)S(1)}, f32[4,8,128]{2,1,0:T(8,128)S(1)}, u32[]{:S(2)}, u32[]{:S(2)}) collective-permute-start(f32[4,8,128]{2,1,0:T(8,128)S(1)} %get-tuple-element.33), channel_id=1, source_target_pairs={{0,112},{16,0},{32,16},{48,32},{64,48},{80,64},{96,80},{112,96},{1... | collective-permute-start | bytes 49160 | tf_op jit(solution)/shard_map/ppermute | solution.py:21
  18.2 0.0 copy-done.2
  18.2 3.0 %local.1 = (f32[8192,128]{1,0:T(8,128)S(1)}, f32[8,128]{1,0:T(8,128)S(1)}) custom-call(bf16[8,8,128,128]{3,2,1,0:T(8,128)(2,1)S(1)} %get-tuple-element.20.wave_ref, f32[8,128,128]{2,1,0:T(8,128)S(1)} %copy-done.2), custom_call_target="tpu_custom_call" | custom-call | flops 1000 | bytes 1000 | tf_op jit(solution)/shard_map/local/pallas_call | solution.py:465
  21.2 0.0 copy-start
  21.2 1.9 %copy-done = f32[8192,128]{1,0:T(8,128)} copy-done((f32[8192,128]{1,0:T(8,128)}, f32[8192,128]{1,0:T(8,128)S(1)}, u32[]{:S(2)}) %copy-start) | copy-done | bytes 4194328
  23.2 0.0 copy-done.4
  23.2 0.1 copy.12.weight_ref
  23.2 0.0 collective-permute-done.4.scaled_low_ref.below_ref
  23.2 0.0 collective-permute-done.5.scaled_high_ref.above_ref
  23.2 0.7 %weigh.1 = f32[16,3,128]{2,1,0:T(4,128)} custom-call(f32[4,8,128]{2,1,0:T(8,128)S(1)} %get-tuple-element.32.scaled_ref.own_ref, f32[4,8,128]{2,1,0:T(8,128)S(1)} %collective-permute-done.5.scaled_high_ref.above_ref, f32[4,8,128]{2,1,0:T(8,128)S(1)} %collective-permute-done.4.scaled_low_ref.below_ref, f32[8,1]{1,0:T(8,128)S(1)} %copy.12.weight_ref, ...), custom_call_target="tpu_custom_call" | custom-call | flops 1000 | bytes 1000 | tf_op jit(solution)/shard_map/weigh/pallas_call | solution.py:487
  23.9 8.1 %all-to-all-start = ((f32[16,3,128]{2,1,0:T(4,128)}), f32[16,3,128]{2,1,0:T(4,128)S(1)}, u32[]{:S(2)}, u32[]{:S(2)}) async-start(f32[16,3,128]{2,1,0:T(4,128)} %weigh.1), calls=%async_computation | async-start | bytes 65536 | tf_op jit(solution)/shard_map/all_to_all | solution.py:509
  32.1 0.0 copy-start.1
  32.1 2.2 %copy-done.1 = f32[8192,128]{1,0:T(8,128)S(1)} copy-done((f32[8192,128]{1,0:T(8,128)S(1)}, f32[8192,128]{1,0:T(8,128)}, u32[]{:S(2)}) %copy-start.1) | copy-done | bytes 4194328
  34.3 2.9 %apply.1 = (f32[8192,128]{1,0:T(8,128)S(1)}, bf16[8,8,128,128]{3,2,1,0:T(8,128)(2,1)}) custom-call(s32[36]{0:T(128)S(1)} %get-tuple-element.19.rows_ref, f32[8192,128]{1,0:T(8,128)S(1)} %copy-done.1, bf16[8,2,128,128]{3,2,1,0:T(8,128)(2,1)S(1)} %collective-permute-done.low_ref, ...), custom_call_target="tpu_custom_call", output_to_operand_aliasing={{0}: (1, {})} | custom-call | flops 1000 | bytes 1000 | tf_op jit(solution)/shard_map/apply/pallas_call | solution.py:496
  37.2 2.5 %all-to-all-done = f32[16,3,128]{2,1,0:T(4,128)S(1)} async-done(((f32[16,3,128]{2,1,0:T(4,128)}), f32[16,3,128]{2,1,0:T(4,128)S(1)}, u32[]{:S(2)}, u32[]{:S(2)}) %all-to-all-start) | async-done | bytes 24608 | tf_op jit(solution)/shard_map/all_to_all | solution.py:509
  39.7 0.1 reshape.11
  39.8 0.7 %reduce_sum.19 = f32[3,12]{1,0:T(4,128)} reduce(f32[3,12,8]{2,1,0:T(8,128)S(1)} %reshape.11, f32[]{:T(128)} %constant.7.clone.1), dimensions={2}, to_apply=%region_1.0 | reduce | flops 252 | bytes 1300 | tf_op jit(solution)/shard_map/reduce_sum | solution.py:511
  (1 shorter events, 0.0 us)
Async XLA Ops:
  0.6 8.6 %copy-start.3 = (f32[8,8]{1,0:T(8,128)S(1)}, f32[8,8]{1,0:T(8,128)}, u32[]{:S(2)}) copy-start(f32[8,8]{1,0:T(8,128)} %coupling_ref.1) | copy-start | bytes 772
  1.9 11.2 %collective-permute-start = (bf16[8,2,128,128]{3,2,1,0:T(8,128)(2,1)S(1)}, bf16[8,2,128,128]{3,2,1,0:T(8,128)(2,1)S(1)}, u32[]{:S(2)}, u32[]{:S(2)}) collective-permute-start(bf16[8,2,128,128]{3,2,1,0:T(8,128)(2,1)S(1)} %get-tuple-element.22), channel_id=1, source_target_pairs={{0,16},{16,32},{32,48},{48,64},{64,80},{80,96},{96,112},{112,0},{1... | collective-permute-start | bytes 1572872 | tf_op jit(solution)/shard_map/ppermute | solution.py:21
  1.9 11.2 %collective-permute-start.1 = (bf16[8,2,128,128]{3,2,1,0:T(8,128)(2,1)S(1)}, bf16[8,2,128,128]{3,2,1,0:T(8,128)(2,1)S(1)}, u32[]{:S(2)}, u32[]{:S(2)}) collective-permute-start(bf16[8,2,128,128]{3,2,1,0:T(8,128)(2,1)S(1)} %get-tuple-element.23), channel_id=1, source_target_pairs={{0,112},{16,0},{32,16},{48,32},{64,48},{80,64},{96,80},{112,96},{1... | collective-permute-start | bytes 1572872 | tf_op jit(solution)/shard_map/ppermute | solution.py:21
  8.7 2.9 %collective-permute-start.2 = (f32[8,128]{1,0:T(8,128)S(1)}, f32[8,128]{1,0:T(8,128)S(1)}, u32[]{:S(2)}, u32[]{:S(2)}) collective-permute-start(f32[8,128]{1,0:T(8,128)S(1)} %get-tuple-element.28), channel_id=1, source_target_pairs={{0,112},{16,0},{32,16},{48,32},{64,48},{80,64},{96,80},{112,96},{1... | collective-permute-start | bytes 12296 | tf_op jit(solution)/shard_map/ppermute | solution.py:21
  8.7 4.2 %collective-permute-start.3 = (f32[8,128]{1,0:T(8,128)S(1)}, f32[8,128]{1,0:T(8,128)S(1)}, u32[]{:S(2)}, u32[]{:S(2)}) collective-permute-start(f32[8,128]{1,0:T(8,128)S(1)} %get-tuple-element.29), channel_id=1, source_target_pairs={{0,16},{16,32},{32,48},{48,64},{64,80},{80,96},{96,112},{112,0},{1... | collective-permute-start | bytes 12296 | tf_op jit(solution)/shard_map/ppermute | solution.py:21
  13.1 5.1 %copy-start.2 = (f32[8,128,128]{2,1,0:T(8,128)S(1)}, f32[8,128,128]{2,1,0:T(8,128)}, u32[]{:S(2)}) copy-start(f32[8,128,128]{2,1,0:T(8,128)} %pot_ref.1) | copy-start | bytes 1572868
  13.1 10.0 %copy-start.4 = (f32[8]{0:T(128)S(1)}, f32[8]{0:T(128)}, u32[]{:S(2)}) copy-start(f32[8]{0:T(128)} %param.13) | copy-start | bytes 100
  15.3 8.0 %collective-permute-start.4 = (f32[4,8,128]{2,1,0:T(8,128)S(1)}, f32[4,8,128]{2,1,0:T(8,128)S(1)}, u32[]{:S(2)}, u32[]{:S(2)}) collective-permute-start(f32[4,8,128]{2,1,0:T(8,128)S(1)} %get-tuple-element.31), channel_id=1, source_target_pairs={{0,16},{16,32},{32,48},{48,64},{64,80},{80,96},{96,112},{112,0},{1... | collective-permute-start | bytes 49160 | tf_op jit(solution)/shard_map/ppermute | solution.py:21
  15.3 8.0 %collective-permute-start.5 = (f32[4,8,128]{2,1,0:T(8,128)S(1)}, f32[4,8,128]{2,1,0:T(8,128)S(1)}, u32[]{:S(2)}, u32[]{:S(2)}) collective-permute-start(f32[4,8,128]{2,1,0:T(8,128)S(1)} %get-tuple-element.33), channel_id=1, source_target_pairs={{0,112},{16,0},{32,16},{48,32},{64,48},{80,64},{96,80},{112,96},{1... | collective-permute-start | bytes 49160 | tf_op jit(solution)/shard_map/ppermute | solution.py:21
  21.2 1.9 %copy-start = (f32[8192,128]{1,0:T(8,128)}, f32[8192,128]{1,0:T(8,128)S(1)}, u32[]{:S(2)}) copy-start(f32[8192,128]{1,0:T(8,128)S(1)} %get-tuple-element.21.local_in) | copy-start | bytes 12582916
  23.9 15.7 %all-to-all-start = ((f32[16,3,128]{2,1,0:T(4,128)}), f32[16,3,128]{2,1,0:T(4,128)S(1)}, u32[]{:S(2)}, u32[]{:S(2)}) async-start(f32[16,3,128]{2,1,0:T(4,128)} %weigh.1), calls=%async_computation | async-start | bytes 65536 | tf_op jit(solution)/shard_map/all_to_all | solution.py:509
  32.1 2.2 %copy-start.1 = (f32[8192,128]{1,0:T(8,128)S(1)}, f32[8192,128]{1,0:T(8,128)}, u32[]{:S(2)}) copy-start(f32[8192,128]{1,0:T(8,128)} %copy-done) | copy-start | bytes 12582916

commit v3 on v2

--- a/solution.py
+++ b/solution.py
@@ -21,15 +21,11 @@
     return lax.ppermute(x, axis, [(i, (i + step) % count) for i in range(count)])
 
 
-def to_rows(src, b, plane, y0, dst, base):
-    part = src[b, plane, pl.ds(y0, 16), :].astype(f32)
-    dst[pl.ds(base + b, 16, stride=8), :] = part
-
-
-def tile_base(first_row, k, width_y):
-    row = first_row + k
-    plane = lax.shift_right_logical(row, 7)
-    return (row + plane * (2 * PAD) + PAD + PAD * (width_y + 2 * PAD)) * 8
+def plane_to_rows(src, plane, dst, base):
+    width_y = src.shape[2]
+    for y0 in range(0, width_y, 16):
+        for b in range(8):
+            dst[pl.ds(base + y0 * 8 + b, 16, stride=8), :] = src[b, plane, y0 : y0 + 16, :].astype(f32)
 
 
 def at_row(ref, base):
@@ -47,16 +43,12 @@
     return total
 
 
-def measure(rows_ref, group, table, width_y, fields):
+def measure(rows_ref, group, table, fields):
     stacked = []
     for field in fields:
         for s in range(ATOM_DEV):
-            first = rows_ref[group * ATOM_DEV + s]
-            stacked.append(
-                jnp.concatenate(
-                    [field(tile_base(first, k, width_y)) for k in range(8)], axis=1
-                )
-            )
+            base = pl.multiple_of(rows_ref[group * ATOM_DEV + s] * 8, 8)
+            stacked.append(jnp.concatenate([field(base + k * 8) for k in range(8)], axis=1))
     values = jnp.concatenate(stacked, axis=0).astype(bf16)
     product = lax.dot_general(
         values, table, (((1,), (1,)), ((), ())), preferred_element_type=f32
@@ -97,12 +89,10 @@
     wave_sems,
     other_sems,
     *,
-    width_y,
     domain_count,
 ):
-    stride = width_y + 2 * PAD
-    planes = wave_ref.shape[1]
-    chunks = width_y // 16
+    planes, width_y = wave_ref.shape[1:3]
+    entry_count = entry_ref.shape[0]
 
     def plane_copy(plane):
         at_plane = (slice(None), pl.ds(plane, 1))
@@ -118,45 +108,24 @@
     for plane in range(planes):
         plane_copy(plane).start()
     proj_copy.start()
-
-    def clear(step, carry):
-        for plane in (0, 1, planes + PAD, planes + PAD + 1):
-            base = pl.multiple_of((plane * stride + PAD + step * 8) * 8, 8)
-            grid_ref[pl.ds(base, 64), :] = jnp.zeros((64, LANES), f32)
-        return carry
-
-    lax.fori_loop(0, width_y // 8, clear, 0)
-
     atoms_copy.wait()
     rows_copy.wait()
 
-    def place(entry, carry):
+    def place(entry):
         atom = atoms_ref[entry]
         owner = lax.shift_right_logical(atom * 171, 11)
         relative = lax.rem(owner - own_ref[0] + 1 + domain_count, domain_count)
         slot = relative * ATOM_DEV + atom - owner * ATOM_DEV
         entry_ref[slot] = entry
         rows_ref[slot] = first_rows_ref[entry]
-        return carry
-
-    lax.fori_loop(0, GROUPS * ATOM_DEV, place, 0)
+
+    share = -(-entry_count // planes)
 
     def one_plane(plane, carry):
         plane_copy(plane).wait()
-
-        def convert(step, inner):
-            y0 = pl.multiple_of(step * 16, 16)
-            base = ((plane + PAD) * stride + PAD + y0) * 8
-            for b in range(8):
-                to_rows(wave_ref, b, plane, y0, grid_ref, base)
-            return inner
-
-        lax.fori_loop(0, chunks, convert, 0)
-        base = pl.multiple_of((plane + PAD) * stride * 8, 8)
-        grid_ref[pl.ds(base, 8 * PAD), :] = grid_ref[pl.ds(base + width_y * 8, 8 * PAD), :]
-        grid_ref[pl.ds(base + (width_y + PAD) * 8, 8 * PAD), :] = grid_ref[
-            pl.ds(base + PAD * 8, 8 * PAD), :
-        ]
+        plane_to_rows(wave_ref, plane, grid_ref, (plane + PAD) * width_y * 8)
+        for i in range(share):
+            place(jnp.minimum(plane * share + i, entry_count - 1))
         return carry
 
     lax.fori_loop(0, planes, one_plane, 0)
@@ -169,7 +138,7 @@
         table = proj_scr[...].astype(bf16)
         table_ref[group] = table
         (margin_ref[...],) = measure(
-            rows_ref, group, table, width_y, [lambda base: at_row(grid_ref, base)]
+            rows_ref, group, table, [lambda base: at_row(grid_ref, base + PAD * width_y * 8)]
         )
 
 
@@ -186,11 +155,14 @@
     return jnp.where(distance == 0, center, table).astype(bf16)
 
 
-def local_kernel(wave_ref, pot_ref, local_ref, token_ref):
+def local_kernel(wave_ref, pot_ref, local_hbm, token_ref, local_ref, sems):
     token_ref[...] = jnp.zeros(token_ref.shape, f32)
     bands, planes, width_y, width_z = wave_ref.shape
     along_y = circulant(-16.0, 1.0, 0.0, width_y)
     along_z = circulant(-16.0, 1.0, 90.0, width_z)
+
+    def band_copy(b):
+        return pltpu.make_async_copy(local_ref.at[b], local_hbm.at[b], sems.at[b])
 
     def one_band(b, carry):
         for plane in range(planes):
@@ -206,30 +178,62 @@
                 for q in sides[1:]:
                     side = side + wave_ref[b, q].astype(f32)
                 summed = summed + (side if factor == 1.0 else factor * side)
-            local_ref[pl.ds(plane * width_y * bands + b, width_y, stride=bands), :] = (
-                summed * (1.0 / 24.0) + pot_ref[plane] * wave.astype(f32)
-            )
+            local_ref[b, plane] = summed * (1.0 / 24.0) + pot_ref[plane] * wave.astype(f32)
+        band_copy(b).start()
         return carry
 
     lax.fori_loop(0, bands, one_band, 0)
-
-
-def gradient_kernel(rows_ref, grid_ref, table_ref, coupling_ref, margin_ref, mixing_ref, *, width_y):
+    for b in range(bands):
+        band_copy(b).wait()
+
+
+def gradient_kernel(
+    rows_ref,
+    grid_ref,
+    table_ref,
+    coupling_ref,
+    weight_ref,
+    margin_ref,
+    mixing_ref,
+    factor_ref,
+    y_ref,
+):
+    width_y = LANES
+    edge = PAD * width_y * 8
+    planes = y_ref.shape[0] // (width_y * 8)
+
+    def one_plane(plane, carry):
+        base = pl.multiple_of(plane * width_y * 8, 8)
+        row = [at_row(grid_ref, base + edge + (y % width_y) * 8) for y in range(-2, 2)]
+        for y in range(width_y):
+            row.append(at_row(grid_ref, base + edge + ((y + 2) % width_y) * 8))
+            near = row[y + 3] - row[y + 1]
+            far = row[y + 4] - row[y]
+            y_ref[pl.ds(base + y * 8, 8), :] = (2.0 / 3.0) * near - (1.0 / 12.0) * far
+        return carry
+
+    lax.fori_loop(0, planes, one_plane, 0)
+
     def along_y(base):
-        near = at_row(grid_ref, base + 8) - at_row(grid_ref, base - 8)
-        far = at_row(grid_ref, base + 16) - at_row(grid_ref, base - 16)
-        return (2.0 / 3.0) * near - (1.0 / 12.0) * far
+        return at_row(y_ref, base)
 
     def along_z(base):
-        center = at_row(grid_ref, base)
+        center = at_row(grid_ref, base + edge)
         near = third_shift(center, 1) - third_shift(center, -1)
         far = third_shift(center, 2) - third_shift(center, -2)
         return (2.0 / 3.0) * near - (1.0 / 12.0) * far
 
     for group in range(GROUPS):
-        second, third = measure(rows_ref, group, table_ref[group], width_y, [along_y, along_z])
+        second, third = measure(rows_ref, group, table_ref[group], [along_y, along_z])
         margin_ref[0, group] = second
         margin_ref[1, group] = third
+
+    bands = weight_ref.shape[1]
+    band = lax.broadcasted_iota(jnp.int32, (bands, bands), 0)
+    other = lax.broadcasted_iota(jnp.int32, (bands, bands), 1)
+    weights = jnp.broadcast_to(weight_ref[...], (bands, bands))
+    column = jnp.sum(jnp.where(band == other, weights, 0.0), axis=1, keepdims=True)
+    factor_ref[...] = jnp.broadcast_to(-2.0 * column, factor_ref.shape)
 
     proj_count = coupling_ref.shape[0]
     symmetric = 0.5 * (coupling_ref[...] + coupling_ref[...].T)
@@ -256,34 +260,23 @@
     low_out,
     mid_out,
     high_out,
-    *,
-    width_y,
 ):
     del grid_in
-    stride = width_y + 2 * PAD
-    planes = grid_ref.shape[0] // (8 * stride) - 2 * PAD
-    chunks = width_y // 16
-    hop = stride * 8
-
-    def convert(step, carry):
-        y0 = pl.multiple_of(step * 16, 16)
-        for plane in range(PAD):
-            low = (plane * stride + PAD + y0) * 8
-            high = ((plane + planes + PAD) * stride + PAD + y0) * 8
-            for b in range(8):
-                to_rows(low_ref, b, plane, y0, grid_ref, low)
-                to_rows(high_ref, b, plane, y0, grid_ref, high)
-        return carry
-
-    lax.fori_loop(0, chunks, convert, 0)
+    width_y = low_ref.shape[2]
+    hop = width_y * 8
+    planes = grid_ref.shape[0] // hop - 2 * PAD
+
+    for index in range(PAD):
+        plane_to_rows(low_ref, index, grid_ref, index * hop)
+        plane_to_rows(high_ref, index, grid_ref, (planes + PAD + index) * hop)
 
     def along_x(base):
-        near = at_row(grid_ref, base + hop) - at_row(grid_ref, base - hop)
-        far = at_row(grid_ref, base + 2 * hop) - at_row(grid_ref, base - 2 * hop)
+        near = at_row(grid_ref, base + 3 * hop) - at_row(grid_ref, base + hop)
+        far = at_row(grid_ref, base + 4 * hop) - at_row(grid_ref, base)
         return (2.0 / 3.0) * near - (1.0 / 12.0) * far
 
     for group, margin_ref in enumerate((low_out, mid_out, high_out)):
-        (first,) = measure(rows_ref, group, table_ref[group], width_y, [along_x])
+        (first,) = measure(rows_ref, group, table_ref[group], [along_x])
         margin_ref[0] = first
         margin_ref[1] = yz_ref[0, group]
         margin_ref[2] = yz_ref[1, group]
@@ -292,22 +285,37 @@
 
 def apply_kernel(
     rows_ref,
-    local_in,
+    local_hbm,
     low_ref,
     high_ref,
     table_ref,
     scaled_low_ref,
     scaled_ref,
     scaled_high_ref,
-    local_ref,
     out_hbm,
     out_ref,
+    add_ref,
+    local_ref,
     sems,
 ):
-    del local_in
     bands, planes, width_y, _ = out_ref.shape
-    chunks = width_y // 16
     lane = lax.broadcasted_iota(jnp.int32, (8, LANES), 1)
+
+    def local_copy(plane):
+        at_plane = (slice(None), pl.ds(plane, 1))
+        return pltpu.make_async_copy(
+            local_hbm.at[at_plane], local_ref.at[at_plane], sems.at[0, plane]
+        )
+
+    for plane in range(planes):
+        local_copy(plane).start()
+
+    def clear(plane, carry):
+        size = width_y * 8
+        add_ref[pl.ds(pl.multiple_of(plane * size, size), size), :] = jnp.zeros((size, LANES), f32)
+        return carry
+
+    lax.fori_loop(0, planes, clear, 0)
 
     for group, source in enumerate((scaled_low_ref, scaled_ref, scaled_high_ref)):
         scaled = source[3]
@@ -321,13 +329,13 @@
             base = pl.multiple_of(rows_ref[group * ATOM_DEV + s] * 8, 8)
             for k in range(8):
                 where = pl.ds(base + k * 8, 8)
-                local_ref[where, :] = (
-                    local_ref[where, :] + terms[s * 8 : s * 8 + 8, k * LANES : (k + 1) * LANES]
+                add_ref[where, :] = (
+                    add_ref[where, :] + terms[s * 8 : s * 8 + 8, k * LANES : (k + 1) * LANES]
                 )
 
     def plane_copy(plane):
         at_plane = (slice(None), pl.ds(plane, 1))
-        return pltpu.make_async_copy(out_ref.at[at_plane], out_hbm.at[at_plane], sems.at[plane])
+        return pltpu.make_async_copy(out_ref.at[at_plane], out_hbm.at[at_plane], sems.at[1, plane])
 
     near, far = -2.0 / 3.0, 1.0 / 24.0
     halo_terms = {
@@ -336,27 +344,31 @@
         planes - 2: ((high_ref, 0, far),),
         planes - 1: ((high_ref, 0, near), (high_ref, 1, far)),
     }
-    for plane in range(planes):
-
-        def finish(step, carry, plane=plane):
-            y0 = pl.multiple_of(step * 16, 16)
-            at_y = pl.ds(y0, 16)
+    def finish(plane, terms):
+        local_copy(plane).wait()
+        base = plane * width_y * 8
+        for y0 in range(0, width_y, 16):
             for b in range(bands):
-                base = (plane * width_y + y0) * 8 + b
-                value = local_ref[pl.ds(base, 16, stride=8), :]
-                for ref, index, factor in halo_terms.get(plane, ()):
-                    value = value + factor * ref[b, index, at_y, :].astype(f32)
-                out_ref[b, plane, at_y, :] = value.astype(bf16)
-            return carry
-
-        lax.fori_loop(0, chunks, finish, 0)
+                value = add_ref[pl.ds(base + y0 * 8 + b, 16, stride=8), :]
+                value = value + local_ref[b, plane, y0 : y0 + 16, :]
+                for ref, index, factor in terms:
+                    value = value + factor * ref[b, index, y0 : y0 + 16, :].astype(f32)
+                out_ref[b, plane, y0 : y0 + 16, :] = value.astype(bf16)
         plane_copy(plane).start()
+
+    def inner(plane, carry):
+        finish(plane, ())
+        return carry
+
+    lax.fori_loop(PAD, planes - PAD, inner, 0)
+    for plane, terms in halo_terms.items():
+        finish(plane, terms)
     for plane in range(planes):
         plane_copy(plane).wait()
 
 
-def weigh_kernel(own_ref, above_ref, below_ref, weight_ref, _, copies_ref):
-    weighted = -2.0 * weight_ref[...] * own_ref[3]
+def weigh_kernel(own_ref, above_ref, below_ref, factor_ref, _, copies_ref):
+    weighted = factor_ref[...] * own_ref[3]
     parts = []
     for k in range(3):
         total = own_ref[k] + above_ref[k] + below_ref[k]
@@ -407,7 +419,7 @@
     entry_count, proj_count, tile_len = projectors.shape
     assert (band_count, proj_count, width_y, width_z) == (8, 8, 128, LANES)
     assert entry_count == GROUPS * ATOM_DEV
-    grid_rows = (plane_count + 2 * PAD) * (width_y + 2 * PAD) * 8
+    grid_rows = (plane_count + 2 * PAD) * width_y * 8
     block = ((8, LANES), f32)
     blocks = ((4, 8, LANES), f32)
     edge = ((band_count, PAD, width_y, width_z), bf16)
@@ -425,9 +437,7 @@
 
     own_index = lax.axis_index("dom").astype(jnp.int32).reshape(1)
     rows, wave, grid, table, low, mid, high = call(
-        functools.partial(
-            relayout_kernel, width_y=width_y, domain_count=lax.axis_size("dom")
-        ),
+        functools.partial(relayout_kernel, domain_count=lax.axis_size("dom")),
         "relayout",
         [
             ((entry_count,), jnp.int32),
@@ -454,27 +464,30 @@
     from_above = ring(low, "dom", -1)
     from_below = ring(high, "dom", 1)
 
-    yz_margins, mixing = call(
-        functools.partial(gradient_kernel, width_y=width_y),
+    yz_margins, mixing, factor = call(
+        gradient_kernel,
         "gradient",
-        [((2, GROUPS, 8, LANES), f32), ((LANES, LANES), f32)],
-        [SMEM] + [VMEM] * 3,
-        [VMEM, VMEM],
-    )(rows, grid, table, coupling)
+        [((2, GROUPS, 8, LANES), f32), ((LANES, LANES), f32), block],
+        [SMEM] + [VMEM] * 4,
+        [VMEM] * 3,
+        [pltpu.VMEM((plane_count * width_y * 8, LANES), f32)],
+    )(rows, grid, table, coupling, band_weights[None, :])
 
     local, token = call(
         local_kernel,
         "local",
-        [((plane_count * width_y * 8, LANES), f32), block],
+        [(wavefunctions.shape, f32), block],
         [VMEM, VMEM],
-        [VMEM, VMEM],
+        [HBM, VMEM],
+        [pltpu.VMEM(wavefunctions.shape, f32), pltpu.SemaphoreType.DMA((band_count,))],
+
     )(wave, potential)
 
     (scaled,) = call(scale_kernel, "scale", [block], [VMEM] * 4, [VMEM], limit=2)(
         mid, from_above, from_below, mixing
     )
     _, low_sums, mid_sums, high_sums = call(
-        functools.partial(first_kernel, width_y=width_y),
+        first_kernel,
         "first",
         [((grid_rows, LANES), f32), blocks, blocks, blocks],
         [SMEM] + [VMEM] * 6,
@@ -491,20 +504,22 @@
         [VMEM] * 5,
         [VMEM],
         limit=2,
-    )(mid_sums, sums_above, sums_below, band_weights[:, None], token)
-
-    _, applied = call(
+    )(mid_sums, sums_above, sums_below, factor, token)
+
+    (applied,) = call(
         apply_kernel,
         "apply",
-        [((plane_count * width_y * 8, LANES), f32), (wavefunctions.shape, bf16)],
-        [SMEM] + [VMEM] * 7,
-        [VMEM, HBM],
+        [(wavefunctions.shape, bf16)],
+        [SMEM, HBM] + [VMEM] * 6,
+        [HBM],
         [
             pltpu.VMEM(wavefunctions.shape, bf16),
-            pltpu.SemaphoreType.DMA((plane_count,)),
+            pltpu.VMEM((plane_count * width_y * 8, LANES), f32),
+            pltpu.VMEM(wavefunctions.shape, f32),
+            pltpu.SemaphoreType.DMA((2, plane_count)),
         ],
-        input_output_aliases={1: 0},
-    )(rows, local, low_halo, high_halo, table, sums_below, mid_sums, sums_above)
+        limit=16,
+    )(rows, in_hbm(local), low_halo, high_halo, table, sums_below, mid_sums, sums_above)
 
     gathered = lax.all_to_all(copies, "band", 0, 0)
     summed = gathered.sum(0)[:, : ATOM_DEV * proj_count]

time: 40.7 us -> 37.3 us (0.916)
  local copies, waits for them, and re-layouts: 4.3 us -> 0.09 us
  waiting for transfers between devices: 3.86 us -> 4.66 us
    unnamed x10 -> x6, local copies, waits for them, and re-layouts: 4.13 us -> 0.01 us
    all_to_all x1, waiting for transfers between devices: 2.5 us -> 3.64 us  [per_device(): gathered = lax.all_to_all(copies, 'band', 0, 0)]
  transfers between devices with their start and end apart: 7 -> 7, of which waited for: 2 -> 3; matrix products, arithmetic and copies ran while one was open for 0% -> 0% of each run, Pallas kernels for 30% -> 35%
where the time goes in v3:
time: 37.3 us; the launch traced here: 37 us
  Pallas kernels  16.3 us (44%)
  starting transfers between devices  14.6 us (39%)
  waiting for transfers between devices  4.66 us (12%)
  between operations  0.73 us (2%)
  other arithmetic  0.7 us (2%)
    all_to_all x1, starting transfers between devices, per_device(): gathered = lax.all_to_all(copies, 'band', 0, 0)  8.13 us
    ppermute x6, starting transfers between devices, ring(): lax.ppermute(x, axis, [(i, (i + step) % count) for i in range(count)])  6.45 us
    pallas_call x1, Pallas kernels, per_device(): call(apply_kernel, 'apply', [(wavefunctions.shape, bf16)], [SMEM, HBM] +...  3.95 us
    all_to_all x1, waiting for transfers between devices, per_device(): gathered = lax.all_to_all(copies, 'band', 0, 0)  3.64 us
    pallas_call x1, Pallas kernels, per_device(): call(local_kernel, 'local', [(wavefunctions.shape, f32), block], [VMEM, V...  3.51 us
    pallas_call x1, Pallas kernels, per_device(): call(gradient_kernel, 'gradient', [((2, GROUPS, 8, LANES), f32), ((LANES,...  2.74 us
    pallas_call x1, Pallas kernels, per_device(): call(functools.partial(relayout_kernel, domain_count=lax.axis_size('dom')...  2.67 us
    pallas_call x1, Pallas kernels, per_device(): call(first_kernel, 'first', [((grid_rows, LANES), f32), blocks, blocks, b...  1.39 us
  transfers between devices with their start and end apart: 7, of which 3 were waited for; matrix products, arithmetic and copies ran while one was open for 0% of the time, Pallas kernels for 35%

profile of v3, /device:TPU:0, one launch (start us, length us, event | category | flops | bytes accessed | tf_op | source)
XLA Modules:
  0.0 37.0 jit_solution(10107816627167807854)
XLA Ops:
  0.6 0.0 copy-start.2
  0.6 0.0 copy-start.1
  0.6 1.2 %edges.1 = (bf16[8,2,128,128]{3,2,1,0:T(8,128)(2,1)S(1)}, bf16[8,2,128,128]{3,2,1,0:T(8,128)(2,1)S(1)}) custom-call(bf16[8,8,128,128]{3,2,1,0:T(8,128)(2,1)} %wave_ref.1), custom_call_target="tpu_custom_call" | custom-call | flops 1000 | bytes 1000 | tf_op jit(solution)/shard_map/edges/pallas_call | solution.py:427
  1.9 0.0 collective-permute-start
  1.9 2.9 %collective-permute-start.1 = (bf16[8,2,128,128]{3,2,1,0:T(8,128)(2,1)S(1)}, bf16[8,2,128,128]{3,2,1,0:T(8,128)(2,1)S(1)}, u32[]{:S(2)}, u32[]{:S(2)}) collective-permute-start(bf16[8,2,128,128]{3,2,1,0:T(8,128)(2,1)S(1)} %get-tuple-element.23), channel_id=1, source_target_pairs={{0,112},{16,0},{32,16},{48,32},{64,48},{80,64},{96,80},{112,96},{1... | collective-permute-start | bytes 1572872 | tf_op jit(solution)/shard_map/ppermute | solution.py:21
  4.9 2.7 %relayout.1 = (s32[36]{0:T(128)S(1)}, bf16[8,8,128,128]{3,2,1,0:T(8,128)(2,1)S(1)}, f32[12288,128]{1,0:T(8,128)S(1)}, bf16[3,128,1024]{2,1,0:T(8,128)(2,1)S(1)},...) custom-call(s32[1]{0:T(128)} %bitcast.own_ref, s32[36]{0:T(128)} %atoms_hbm.1, ...), custom_call_target="tpu_custom_call" | custom-call | flops 1000 | bytes 1000 | tf_op jit(solution)/shard_map/relayout/pallas_call | solution.py:439
  7.5 0.0 collective-permute-start.2
  7.6 0.5 %collective-permute-start.3 = (f32[8,128]{1,0:T(8,128)S(1)}, f32[8,128]{1,0:T(8,128)S(1)}, u32[]{:S(2)}, u32[]{:S(2)}) collective-permute-start(f32[8,128]{1,0:T(8,128)S(1)} %get-tuple-element.29), channel_id=1, source_target_pairs={{0,16},{16,32},{32,48},{48,64},{64,80},{80,96},{96,112},{112,0},{1... | collective-permute-start | bytes 12296 | tf_op jit(solution)/shard_map/ppermute | solution.py:21
  8.1 0.0 copy-done.2
  8.1 0.0 copy-done.1
  8.1 2.7 %gradient.1 = (f32[2,3,8,128]{3,2,1,0:T(8,128)S(1)}, f32[128,128]{1,0:T(8,128)S(1)}, f32[8,128]{1,0:T(8,128)S(1)}) custom-call(s32[36]{0:T(128)S(1)} %get-tuple-element.19.rows_ref, f32[12288,128]{1,0:T(8,128)S(1)} %get-tuple-element.25.grid_ref.grid_in, bf16[3,128,1024]{2,1,0:T(8,128)(2,1)S(1)} %get-tuple-element.24.table_ref, f32[8,8]{1,0:T(8,128)S(1)} %copy-done.1, ...), custom_call_target="tpu_custom_call" | custom-call | flops 1000 | bytes 1000 | tf_op jit(solution)/shard_map/gradient/pallas_call | solution.py:467
  10.8 0.0 copy-start
  10.8 0.8 %collective-permute-done.2.above_ref = f32[8,128]{1,0:T(8,128)S(1)} collective-permute-done((f32[8,128]{1,0:T(8,128)S(1)}, f32[8,128]{1,0:T(8,128)S(1)}, u32[]{:S(2)}, u32[]{:S(2)}) %collective-permute-start.2) | collective-permute-done | bytes 4128 | tf_op jit(solution)/shard_map/ppermute | solution.py:21
  11.6 0.2 collective-permute-done.3.below_ref
  11.8 0.2 scale.1.scaled_ref
  12.0 0.0 collective-permute-done.low_ref
  12.0 0.0 collective-permute-done.1.high_ref
  12.0 1.4 %first.1 = (f32[12288,128]{1,0:T(8,128)S(1)}, f32[4,8,128]{2,1,0:T(8,128)S(1)}, f32[4,8,128]{2,1,0:T(8,128)S(1)}, f32[4,8,128]{2,1,0:T(8,128)S(1)}) custom-call(s32[36]{0:T(128)S(1)} %get-tuple-element.19.rows_ref, f32[12288,128]{1,0:T(8,128)S(1)} %get-tuple-element.25.grid_ref.grid_in, ...), custom_call_target="tpu_custom_call", output_to_operand_aliasing={{0}: (1, {})} | custom-call | flops 1000 | bytes 1000 | tf_op jit(solution)/shard_map/first/pallas_call | solution.py:489
  13.4 0.4 %collective-permute-start.4 = (f32[4,8,128]{2,1,0:T(8,128)S(1)}, f32[4,8,128]{2,1,0:T(8,128)S(1)}, u32[]{:S(2)}, u32[]{:S(2)}) collective-permute-start(f32[4,8,128]{2,1,0:T(8,128)S(1)} %get-tuple-element.31), channel_id=1, source_target_pairs={{0,16},{16,32},{32,48},{48,64},{64,80},{80,96},{96,112},{112,0},{1... | collective-permute-start | bytes 49160 | tf_op jit(solution)/shard_map/ppermute | solution.py:21
  13.8 2.5 %collective-permute-start.5 = (f32[4,8,128]{2,1,0:T(8,128)S(1)}, f32[4,8,128]{2,1,0:T(8,128)S(1)}, u32[]{:S(2)}, u32[]{:S(2)}) collective-permute-start(f32[4,8,128]{2,1,0:T(8,128)S(1)} %get-tuple-element.33), channel_id=1, source_target_pairs={{0,112},{16,0},{32,16},{48,32},{64,48},{80,64},{96,80},{112,96},{1... | collective-permute-start | bytes 49160 | tf_op jit(solution)/shard_map/ppermute | solution.py:21
  16.3 0.0 copy-done
  16.3 3.5 %local.1 = (f32[8,8,128,128]{3,2,1,0:T(8,128)}, f32[8,128]{1,0:T(8,128)S(1)}) custom-call(bf16[8,8,128,128]{3,2,1,0:T(8,128)(2,1)S(1)} %get-tuple-element.20.wave_ref, f32[8,128,128]{2,1,0:T(8,128)S(1)} %copy-done), custom_call_target="tpu_custom_call" | custom-call | flops 1000 | bytes 1000 | tf_op jit(solution)/shard_map/local/pallas_call | solution.py:476
  19.9 0.0 collective-permute-done.4.scaled_low_ref.below_ref
  19.9 0.0 collective-permute-done.5.scaled_high_ref.above_ref
  19.9 0.6 %weigh.1 = f32[16,3,128]{2,1,0:T(4,128)} custom-call(f32[4,8,128]{2,1,0:T(8,128)S(1)} %get-tuple-element.32.scaled_ref.own_ref, f32[4,8,128]{2,1,0:T(8,128)S(1)} %collective-permute-done.5.scaled_high_ref.above_ref, f32[4,8,128]{2,1,0:T(8,128)S(1)} %collective-permute-done.4.scaled_low_ref.below_ref, f32[8,128]{1,0:T(8,128)S(1)} %get-tuple-element.34.factor_ref, ...), custom_call_target="tpu_custom_call" | custom-call | flops 1000 | bytes 1000 | tf_op jit(solution)/shard_map/weigh/pallas_call | solution.py:500
  20.5 8.1 %all-to-all-start = ((f32[16,3,128]{2,1,0:T(4,128)}), f32[16,3,128]{2,1,0:T(4,128)S(1)}, u32[]{:S(2)}, u32[]{:S(2)}) async-start(f32[16,3,128]{2,1,0:T(4,128)} %weigh.1), calls=%async_computation | async-start | bytes 65536 | tf_op jit(solution)/shard_map/all_to_all | solution.py:524
  28.6 4.0 %apply.1 = bf16[8,8,128,128]{3,2,1,0:T(8,128)(2,1)} custom-call(s32[36]{0:T(128)S(1)} %get-tuple-element.19.rows_ref, f32[8,8,128,128]{3,2,1,0:T(8,128)} %get-tuple-element.21.local_hbm, bf16[8,2,128,128]{3,2,1,0:T(8,128)(2,1)S(1)} %collective-permute-done.low_ref, bf16[8,2,128,128]{3,2,1,0:T(8,128)(2,1)S(1)} %collective-permute-done.1.high_ref, ...), custom_call_target="tpu_custom_call" | custom-call | flops 1000 | bytes 1000 | tf_op jit(solution)/shard_map/apply/pallas_call | solution.py:509
  32.6 3.6 %all-to-all-done = f32[16,3,128]{2,1,0:T(4,128)S(1)} async-done(((f32[16,3,128]{2,1,0:T(4,128)}), f32[16,3,128]{2,1,0:T(4,128)S(1)}, u32[]{:S(2)}, u32[]{:S(2)}) %all-to-all-start) | async-done | bytes 24608 | tf_op jit(solution)/shard_map/all_to_all | solution.py:524
  36.3 0.1 reshape.11
  36.4 0.7 %reduce_sum.19 = f32[3,12]{1,0:T(4,128)} reduce(f32[3,12,8]{2,1,0:T(8,128)S(1)} %reshape.11, f32[]{:T(128)} %constant.7.clone.1), dimensions={2}, to_apply=%region_1.0 | reduce | flops 252 | bytes 1300 | tf_op jit(solution)/shard_map/reduce_sum | solution.py:526
  (1 shorter events, 0.0 us)
Async XLA Ops:
  0.6 7.4 %copy-start.2 = (f32[8]{0:T(128)S(1)}, f32[8]{0:T(128)}, u32[]{:S(2)}) copy-start(f32[8]{0:T(128)} %param.13) | copy-start | bytes 100
  0.6 7.4 %copy-start.1 = (f32[8,8]{1,0:T(8,128)S(1)}, f32[8,8]{1,0:T(8,128)}, u32[]{:S(2)}) copy-start(f32[8,8]{1,0:T(8,128)} %coupling_ref.1) | copy-start | bytes 772
  1.9 10.1 %collective-permute-start = (bf16[8,2,128,128]{3,2,1,0:T(8,128)(2,1)S(1)}, bf16[8,2,128,128]{3,2,1,0:T(8,128)(2,1)S(1)}, u32[]{:S(2)}, u32[]{:S(2)}) collective-permute-start(bf16[8,2,128,128]{3,2,1,0:T(8,128)(2,1)S(1)} %get-tuple-element.22), channel_id=1, source_target_pairs={{0,16},{16,32},{32,48},{48,64},{64,80},{80,96},{96,112},{112,0},{1... | collective-permute-start | bytes 1572872 | tf_op jit(solution)/shard_map/ppermute | solution.py:21
  1.9 10.1 %collective-permute-start.1 = (bf16[8,2,128,128]{3,2,1,0:T(8,128)(2,1)S(1)}, bf16[8,2,128,128]{3,2,1,0:T(8,128)(2,1)S(1)}, u32[]{:S(2)}, u32[]{:S(2)}) collective-permute-start(bf16[8,2,128,128]{3,2,1,0:T(8,128)(2,1)S(1)} %get-tuple-element.23), channel_id=1, source_target_pairs={{0,112},{16,0},{32,16},{48,32},{64,48},{80,64},{96,80},{112,96},{1... | collective-permute-start | bytes 1572872 | tf_op jit(solution)/shard_map/ppermute | solution.py:21
  7.5 4.1 %collective-permute-start.2 = (f32[8,128]{1,0:T(8,128)S(1)}, f32[8,128]{1,0:T(8,128)S(1)}, u32[]{:S(2)}, u32[]{:S(2)}) collective-permute-start(f32[8,128]{1,0:T(8,128)S(1)} %get-tuple-element.28), channel_id=1, source_target_pairs={{0,112},{16,0},{32,16},{48,32},{64,48},{80,64},{96,80},{112,96},{1... | collective-permute-start | bytes 12296 | tf_op jit(solution)/shard_map/ppermute | solution.py:21
  7.6 4.3 %collective-permute-start.3 = (f32[8,128]{1,0:T(8,128)S(1)}, f32[8,128]{1,0:T(8,128)S(1)}, u32[]{:S(2)}, u32[]{:S(2)}) collective-permute-start(f32[8,128]{1,0:T(8,128)S(1)} %get-tuple-element.29), channel_id=1, source_target_pairs={{0,16},{16,32},{32,48},{48,64},{64,80},{80,96},{96,112},{112,0},{1... | collective-permute-start | bytes 12296 | tf_op jit(solution)/shard_map/ppermute | solution.py:21
  10.8 5.5 %copy-start = (f32[8,128,128]{2,1,0:T(8,128)S(1)}, f32[8,128,128]{2,1,0:T(8,128)}, u32[]{:S(2)}) copy-start(f32[8,128,128]{2,1,0:T(8,128)} %pot_ref.1) | copy-start | bytes 1572868
  13.4 6.5 %collective-permute-start.4 = (f32[4,8,128]{2,1,0:T(8,128)S(1)}, f32[4,8,128]{2,1,0:T(8,128)S(1)}, u32[]{:S(2)}, u32[]{:S(2)}) collective-permute-start(f32[4,8,128]{2,1,0:T(8,128)S(1)} %get-tuple-element.31), channel_id=1, source_target_pairs={{0,16},{16,32},{32,48},{48,64},{64,80},{80,96},{96,112},{112,0},{1... | collective-permute-start | bytes 49160 | tf_op jit(solution)/shard_map/ppermute | solution.py:21
  13.8 6.1 %collective-permute-start.5 = (f32[4,8,128]{2,1,0:T(8,128)S(1)}, f32[4,8,128]{2,1,0:T(8,128)S(1)}, u32[]{:S(2)}, u32[]{:S(2)}) collective-permute-start(f32[4,8,128]{2,1,0:T(8,128)S(1)} %get-tuple-element.33), channel_id=1, source_target_pairs={{0,112},{16,0},{32,16},{48,32},{64,48},{80,64},{96,80},{112,96},{1... | collective-permute-start | bytes 49160 | tf_op jit(solution)/shard_map/ppermute | solution.py:21
  20.5 15.7 %all-to-all-start = ((f32[16,3,128]{2,1,0:T(4,128)}), f32[16,3,128]{2,1,0:T(4,128)S(1)}, u32[]{:S(2)}, u32[]{:S(2)}) async-start(f32[16,3,128]{2,1,0:T(4,128)} %weigh.1), calls=%async_computation | async-start | bytes 65536 | tf_op jit(solution)/shard_map/all_to_all | solution.py:524

commit v4 on v3

v4 whole, which is shorter than its diff:
```python
import functools

import jax
import jax.numpy as jnp
from jax import lax
from jax.experimental import pallas as pl
from jax.experimental.pallas import tpu as pltpu
from jax.sharding import PartitionSpec as P

ATOM_DEV = 12
GROUPS = 3
LANES = 128
PAD = 2

f32 = jnp.float32
bf16 = jnp.bfloat16


def partner_a(i):
    return i ^ 1


def partner_b(i, count):
    return (i + 1 if i % 2 else i - 1) % count


def swap_a(x):
    return lax.ppermute(x, "dom", [(i, partner_a(i)) for i in range(lax.axis_size("dom"))])


def swap_b(x):
    count = lax.axis_size("dom")
    return lax.ppermute(x, "dom", [(i, partner_b(i, count)) for i in range(count)])


def send_c(x):
    count = lax.axis_size("dom")
    return lax.ppermute(x, "dom", [(i, partner_a(partner_b(i, count))) for i in range(count)])


def own_domain():
    index = lax.axis_index("dom")
    return index, lax.bitwise_and(index, 1)


def plane_to_rows(src, plane, dst, base):
    width_y = src.shape[2]
    for y0 in range(0, width_y, 16):
        for b in range(8):
            dst[pl.ds(base + y0 * 8 + b, 16, stride=8), :] = src[b, plane, y0 : y0 + 16, :].astype(f32)


def at_row(ref, base):
    return ref[pl.ds(pl.multiple_of(base, 8), 8), :]


def diagonal_blocks(product, field):
    lane = lax.broadcasted_iota(jnp.int32, (8, LANES), 1)
    total = jnp.zeros((8, LANES), f32)
    for s in range(ATOM_DEV):
        start = (field * ATOM_DEV + s) * 8
        total = total + jnp.where(
            lax.shift_right_logical(lane, 3) == s, product[start : start + 8, :], 0.0
        )
    return total


def measure(rows_ref, group, table, fields):
    stacked = []
    for field in fields:
        for s in range(ATOM_DEV):
            base = pl.multiple_of(rows_ref[group * ATOM_DEV + s] * 8, 8)
            stacked.append(jnp.concatenate([field(base + k * 8) for k in range(8)], axis=1))
    values = jnp.concatenate(stacked, axis=0).astype(bf16)
    product = lax.dot_general(
        values, table, (((1,), (1,)), ((), ())), preferred_element_type=f32
    )
    return [diagonal_blocks(product, q) for q in range(len(fields))]


def start_rows(rows_in, rows_ref, sem):
    copy = pltpu.make_async_copy(rows_in, rows_ref, sem)
    copy.start()
    return copy


def edge_kernel(wave_ref, to_a_ref, to_b_ref, sems):
    planes = wave_ref.shape[1]
    _, odd = own_domain()
    upper = planes - PAD
    copies = [
        start_rows(wave_ref.at[:, pl.ds(upper * (1 - odd), PAD)], to_a_ref, sems.at[0]),
        start_rows(wave_ref.at[:, pl.ds(upper * odd, PAD)], to_b_ref, sems.at[1]),
    ]
    for copy in copies:
        copy.wait()


def relayout_kernel(
    atoms_hbm,
    first_rows_hbm,
    wave_hbm,
    proj_hbm,
    rows_out,
    grid_ref,
    table_ref,
    margin_ref,
    to_a_ref,
    to_c_ref,
    wave_ref,
    atoms_ref,
    first_rows_ref,
    rows_ref,
    entry_ref,
    proj_ref,
    proj_scr,
    wave_sems,
    other_sems,
    *,
    domain_count,
):
    planes, width_y = wave_ref.shape[1:3]
    entry_count = rows_ref.shape[0]
    index, odd = own_domain()

    def plane_copy(plane):
        at_plane = (slice(None), pl.ds(plane, 1))
        return pltpu.make_async_copy(
            wave_hbm.at[at_plane], wave_ref.at[at_plane], wave_sems.at[plane]
        )

    atoms_copy = start_rows(atoms_hbm, atoms_ref, other_sems.at[0])
    first_copy = start_rows(first_rows_hbm, first_rows_ref, other_sems.at[1])
    for plane in range(planes):
        plane_copy(plane).start()
    proj_copy = start_rows(proj_hbm, proj_ref, other_sems.at[2])
    proj_scr[:, ATOM_DEV * 8 :, :] = jnp.zeros(
        (GROUPS, LANES - ATOM_DEV * 8, proj_scr.shape[2]), f32
    )
    atoms_copy.wait()
    first_copy.wait()
    for entry in range(entry_count):
        atom = atoms_ref[entry]
        owner = lax.shift_right_logical(atom * 171, 11)
        above = lax.rem(owner - index + 1 + domain_count, domain_count)
        group = jnp.where(odd == 1, above, 2 - above)
        slot = group * ATOM_DEV + atom - owner * ATOM_DEV
        entry_ref[slot] = entry
        rows_ref[slot] = first_rows_ref[entry]
    rows_copy = start_rows(rows_ref, rows_out, other_sems.at[3])

    def one_plane(plane, carry):
        plane_copy(plane).wait()
        plane_to_rows(wave_ref, plane, grid_ref, (plane + PAD) * width_y * 8)
        return carry

    lax.fori_loop(0, planes, one_plane, 0)
    proj_copy.wait()
    for group in range(GROUPS):
        for s in range(ATOM_DEV):
            entry = entry_ref[group * ATOM_DEV + s]
            proj_scr[group, s * 8 : s * 8 + 8, :] = proj_ref[entry].astype(f32)
        table = proj_scr[group].astype(bf16)
        table_ref[group] = table
        (sums,) = measure(
            rows_ref,
            group,
            table,
            [lambda base: at_row(grid_ref, base + PAD * width_y * 8)],
        )
        margin_ref[group] = sums
        if group < 2:
            to_a_ref[group] = sums
        else:
            to_c_ref[...] = sums
    rows_copy.wait()


def forward_kernel(margin_ref, from_a_ref, to_b_ref):
    to_b_ref[0] = margin_ref[2]
    to_b_ref[1] = margin_ref[1] + from_a_ref[0]


def third_shift(center, offset):
    return pltpu.roll(center, (-offset) % center.shape[-1], 1)


def circulant(near, far, center, length):
    row = lax.broadcasted_iota(jnp.int32, (length, length), 0)
    column = lax.broadcasted_iota(jnp.int32, (length, length), 1)
    distance = lax.bitwise_and(row - column, length - 1)
    table = jnp.where((distance == 1) | (distance == length - 1), near, 0.0)
    table = jnp.where((distance == 2) | (distance == length - 2), far, table)
    return jnp.where(distance == 0, center, table).astype(bf16)


def gradient_kernel(
    rows_in,
    grid_in,
    halo_a_ref,
    table_ref,
    coupling_hbm,
    weight_hbm,
    _,
    grid_ref,
    margin_ref,
    mixing_ref,
    factor_ref,
    y_ref,
    rows_ref,
    coupling_ref,
    weight_ref,
    sems,
):
    del grid_in
    copies = [
        start_rows(rows_in, rows_ref, sems.at[0]),
        start_rows(coupling_hbm, coupling_ref, sems.at[1]),
        start_rows(weight_hbm, weight_ref, sems.at[2]),
    ]
    width_y = LANES
    edge = PAD * width_y * 8
    planes = y_ref.shape[0] // (width_y * 8)

    def one_plane(plane, carry):
        base = pl.multiple_of(plane * width_y * 8, 8)
        row = [at_row(grid_ref, base + edge + (y % width_y) * 8) for y in range(-2, 2)]
        for y in range(width_y):
            row.append(at_row(grid_ref, base + edge + ((y + 2) % width_y) * 8))
            near = row[y + 3] - row[y + 1]
            far = row[y + 4] - row[y]
            y_ref[pl.ds(base + y * 8, 8), :] = (2.0 / 3.0) * near - (1.0 / 12.0) * far
        return carry

    lax.fori_loop(0, planes, one_plane, 0)

    def along_y(base):
        return at_row(y_ref, base)

    def along_z(base):
        center = at_row(grid_ref, base + edge)
        near = third_shift(center, 1) - third_shift(center, -1)
        far = third_shift(center, 2) - third_shift(center, -2)
        return (2.0 / 3.0) * near - (1.0 / 12.0) * far

    _, odd = own_domain()
    for i in range(PAD):
        plane = i + (planes + PAD) * (1 - odd)
        plane_to_rows(halo_a_ref, i, grid_ref, plane * width_y * 8)

    for copy in copies:
        copy.wait()
    for group in range(GROUPS):
        second, third = measure(rows_ref, group, table_ref[group], [along_y, along_z])
        margin_ref[0, group] = second
        margin_ref[1, group] = third

    bands = weight_ref.shape[1]
    band = lax.broadcasted_iota(jnp.int32, (bands, bands), 0)
    other = lax.broadcasted_iota(jnp.int32, (bands, bands), 1)
    weights = jnp.broadcast_to(weight_ref[...], (bands, bands))
    column = jnp.sum(jnp.where(band == other, weights, 0.0), axis=1, keepdims=True)
    factor_ref[...] = jnp.broadcast_to(-2.0 * column, factor_ref.shape)

    proj_count = coupling_ref.shape[0]
    symmetric = 0.5 * (coupling_ref[...] + coupling_ref[...].T)
    index = lax.broadcasted_iota(jnp.int32, (proj_count, LANES), 0)
    lane = lax.broadcasted_iota(jnp.int32, (proj_count, LANES), 1)
    spread = (lax.bitwise_and(lane, proj_count - 1) == index).astype(f32)
    tiled = jnp.dot(
        symmetric, spread, precision=lax.Precision.HIGHEST, preferred_element_type=f32
    )
    for a in range(LANES // proj_count):
        keep = (lax.shift_right_logical(lane, 3) == a) & (lane < ATOM_DEV * proj_count)
        mixing_ref[a * proj_count : (a + 1) * proj_count, :] = jnp.where(keep, tiled, 0.0)


def first_kernel(
    rows_in,
    grid_in,
    halo_b_ref,
    table_ref,
    yz_ref,
    grid_ref,
    force_ref,
    rows_ref,
    rows_sem,
):
    del grid_in
    rows_copy = start_rows(rows_in, rows_ref, rows_sem)
    width_y = halo_b_ref.shape[2]
    hop = width_y * 8
    planes = grid_ref.shape[0] // hop - 2 * PAD
    _, odd = own_domain()

    for i in range(PAD):
        plane_to_rows(halo_b_ref, i, grid_ref, (i + (planes + PAD) * odd) * hop)

    def along_x(base):
        near = at_row(grid_ref, base + 3 * hop) - at_row(grid_ref, base + hop)
        far = at_row(grid_ref, base + 4 * hop) - at_row(grid_ref, base)
        return (2.0 / 3.0) * near - (1.0 / 12.0) * far

    rows_copy.wait()
    for group in range(GROUPS):
        (first,) = measure(rows_ref, group, table_ref[group], [along_x])
        force_ref[group, 0] = first
        force_ref[group, 1] = yz_ref[0, group]
        force_ref[group, 2] = yz_ref[1, group]


def combine_kernel(
    margin_ref,
    from_a_ref,
    from_b_ref,
    from_c_ref,
    mixing_ref,
    factor_ref,
    force_ref,
    scaled_ref,
    copies_ref,
    *,
    domain_count,
):
    totals = jnp.concatenate(
        [
            margin_ref[0] + from_a_ref[1] + from_c_ref[...],
            margin_ref[1] + from_a_ref[0] + from_b_ref[0],
            margin_ref[2] + from_b_ref[1],
        ],
        axis=0,
    )
    scaled = jnp.dot(
        totals, mixing_ref[...], precision=lax.Precision.HIGHEST, preferred_element_type=f32
    )
    parts = []
    for group in range(GROUPS):
        one = scaled[group * 8 : group * 8 + 8]
        scaled_ref[group] = one
        weighted = factor_ref[...] * one
        for k in range(3):
            parts.append(jnp.sum(force_ref[group, k] * weighted, axis=0, keepdims=True))
    summed = jnp.concatenate(parts, axis=0)
    for step in (1, 2, 4):
        summed = summed + pltpu.roll(summed, LANES - step, 1)
    component = lax.bitwise_and(lax.broadcasted_iota(jnp.int32, (1, LANES), 1), 7)
    copies_ref[...] = jnp.zeros(copies_ref.shape, f32)
    bands = copies_ref.shape[0] // domain_count
    index, odd = own_domain()
    owners = (
        index + 1 - 2 * odd,
        index,
        lax.rem(index - 1 + 2 * odd + domain_count, domain_count),
    )
    for group, owner in enumerate(owners):
        row = jnp.zeros((1, LANES), f32)
        for k in range(3):
            value = summed[group * 3 + k : group * 3 + k + 1]
            value = pltpu.roll(value, k, 1) if k else value
            row = row + jnp.where(component == k, value, 0.0)
        for b in range(bands):
            copies_ref[owner * bands + b] = row


def total_kernel(gathered_ref, forces_ref):
    atoms = forces_ref.shape[1]
    row = jnp.sum(jnp.sum(gathered_ref[...], axis=0), axis=0, keepdims=True)
    lane = lax.broadcasted_iota(jnp.int32, (8, LANES), 1)
    component = lax.broadcasted_iota(jnp.int32, (8, LANES), 0)
    split = jnp.where(lax.bitwise_and(lane, 7) == component, row, 0.0)
    source = lax.broadcasted_iota(jnp.int32, (LANES, LANES), 0)
    target = lax.broadcasted_iota(jnp.int32, (LANES, LANES), 1)
    collect = (lax.shift_right_logical(source, 3) == target).astype(f32)
    forces = jnp.dot(
        split, collect, precision=lax.Precision.HIGHEST, preferred_element_type=f32
    )
    forces_ref[...] = forces[:3, :atoms]


def apply_kernel(
    rows_in,
    wave_hbm,
    pot_hbm,
    halo_a_ref,
    halo_b_ref,
    table_ref,
    scaled_ref,
    out_hbm,
    out_ref,
    add_ref,
    wave_ref,
    pot_ref,
    rows_ref,
    sems,
    edge_sems,
):
    bands, planes, width_y, width_z = out_ref.shape
    lane = lax.broadcasted_iota(jnp.int32, (8, LANES), 1)

    def wave_copy(plane):
        return pltpu.make_async_copy(
            wave_hbm.at[:, pl.ds(plane, 1)],
            wave_ref.at[:, pl.ds(plane + PAD, 1)],
            sems.at[0, plane],
        )

    def out_copy(plane):
        at_plane = (slice(None), pl.ds(plane, 1))
        return pltpu.make_async_copy(
            out_ref.at[at_plane], out_hbm.at[at_plane], sems.at[1, plane]
        )

    rows_copy = start_rows(rows_in, rows_ref, edge_sems.at[0])
    _, odd = own_domain()
    far_end = planes + PAD
    edge_copies = [
        start_rows(halo_a_ref, wave_ref.at[:, pl.ds(far_end * (1 - odd), PAD)], edge_sems.at[1]),
        start_rows(halo_b_ref, wave_ref.at[:, pl.ds(far_end * odd, PAD)], edge_sems.at[2]),
        start_rows(pot_hbm, pot_ref, edge_sems.at[3]),
    ]
    for plane in range(planes):
        wave_copy(plane).start()

    def clear(plane, carry):
        size = width_y * 8
        add_ref[pl.ds(pl.multiple_of(plane * size, size), size), :] = jnp.zeros((size, LANES), f32)
        return carry

    lax.fori_loop(0, planes, clear, 0)
    rows_copy.wait()

    for group in range(GROUPS):
        scaled = scaled_ref[group]
        blocks = [
            jnp.where(lax.shift_right_logical(lane, 3) == s, scaled, 0.0)
            for s in range(ATOM_DEV)
        ]
        coef = jnp.concatenate(blocks, axis=0).astype(bf16)
        terms = jnp.dot(coef, table_ref[group], preferred_element_type=f32)
        for s in range(ATOM_DEV):
            base = pl.multiple_of(rows_ref[group * ATOM_DEV + s] * 8, 8)
            for k in range(8):
                where = pl.ds(base + k * 8, 8)
                add_ref[where, :] = (
                    add_ref[where, :] + terms[s * 8 : s * 8 + 8, k * LANES : (k + 1) * LANES]
                )

    along_y = circulant(-16.0, 1.0, 0.0, width_y)
    along_z = circulant(-16.0, 1.0, 90.0, width_z)
    for copy in edge_copies:
        copy.wait()
    for plane in range(PAD):
        wave_copy(plane).wait()

    def finish(plane, carry):
        @pl.when(plane + PAD < planes)
        def _():
            wave_copy(plane + PAD).wait()

        for b in range(bands):
            wave = wave_ref[b, plane + PAD]
            summed = jnp.dot(
                jnp.concatenate([wave, along_y], axis=1),
                jnp.concatenate([along_z, wave], axis=0),
                preferred_element_type=f32,
            )
            near = wave_ref[b, plane + 1].astype(f32) + wave_ref[b, plane + 3].astype(f32)
            far = wave_ref[b, plane].astype(f32) + wave_ref[b, plane + 4].astype(f32)
            value = (summed + far - 16.0 * near) * (1.0 / 24.0)
            value = value + pot_ref[plane] * wave.astype(f32)
            added = add_ref[pl.ds(plane * width_y * 8 + b, width_y, stride=8), :]
            out_ref[b, plane] = (value + added).astype(bf16)
        out_copy(plane).start()
        return carry

    lax.fori_loop(0, planes, finish, 0)
    for plane in range(planes):
        out_copy(plane).wait()


VMEM = pl.BlockSpec(memory_space=pltpu.VMEM)
SMEM = pl.BlockSpec(memory_space=pltpu.SMEM)
HBM = pl.BlockSpec(memory_space=pltpu.HBM)
ANY = pl.BlockSpec(memory_space=pl.ANY)
MIB = 2**20


def in_hbm(x):
    return pltpu.with_memory_space_constraint(x, pltpu.HBM)


def call(kernel, name, outs, ins, out_specs, scratch=(), limit=8, **kwargs):
    return pl.pallas_call(
        kernel,
        out_shape=tuple(
            pltpu.HBM(shape, dtype) if spec is HBM else jax.ShapeDtypeStruct(shape, dtype)
            for (shape, dtype), spec in zip(outs, out_specs)
        ),
        in_specs=ins,
        out_specs=tuple(out_specs),
        scratch_shapes=list(scratch),
        compiler_params=pltpu.CompilerParams(vmem_limit_bytes=limit * MIB),
        cost_estimate=pl.CostEstimate(flops=1000, bytes_accessed=1000, transcendentals=0),
        name=name,
        **kwargs,
    )


def per_device(
    wavefunctions, potential, projectors, margin_atoms, tile_rows, coupling, band_weights
):
    band_count, plane_count, width_y, width_z = wavefunctions.shape
    entry_count, proj_count, tile_len = projectors.shape
    assert (band_count, proj_count, width_y, width_z) == (8, 8, 128, LANES)
    assert entry_count == GROUPS * ATOM_DEV
    grid_rows = (plane_count + 2 * PAD) * width_y * 8
    domain_count = lax.axis_size("dom")
    block = ((8, LANES), f32)
    pair = ((2, 8, LANES), f32)
    blocks = ((GROUPS, 8, LANES), f32)
    edge = ((band_count, PAD, width_y, width_z), bf16)
    slots = ((entry_count,), jnp.int32)
    slots_smem = pltpu.SMEM((entry_count,), jnp.int32)

    to_a, to_b = call(
        edge_kernel,
        "edges",
        [edge, edge],
        [HBM],
        [VMEM, VMEM],
        [pltpu.SemaphoreType.DMA((2,))],
    )(in_hbm(wavefunctions))
    halo_a = swap_a(to_a)
    halo_b = swap_b(to_b)

    rows, grid, table, margins, margins_to_a, margins_to_c = call(
        functools.partial(relayout_kernel, domain_count=domain_count),
        "relayout",
        [
            slots,
            ((grid_rows, LANES), f32),
            ((GROUPS, LANES, tile_len), bf16),
            blocks,
            pair,
            block,
        ],
        [HBM] * 4,
        [ANY] + [VMEM] * 5,
        [
            pltpu.VMEM(wavefunctions.shape, bf16),
            slots_smem,
            slots_smem,
            slots_smem,
            slots_smem,
            pltpu.VMEM(projectors.shape, bf16),
            pltpu.VMEM((GROUPS, LANES, tile_len), f32),
            pltpu.SemaphoreType.DMA((plane_count,)),
            pltpu.SemaphoreType.DMA((4,)),
        ],
    )(*map(in_hbm, (margin_atoms, tile_rows, wavefunctions, projectors)))

    from_a = swap_a(margins_to_a)
    from_c = send_c(margins_to_c)
    (margins_to_b,) = call(forward_kernel, "forward", [pair], [VMEM] * 2, [VMEM], limit=2)(
        margins, from_a
    )
    from_b = swap_b(margins_to_b)

    grid, yz_margins, mixing, factor = call(
        gradient_kernel,
        "gradient",
        [
            ((grid_rows, LANES), f32),
            ((2, GROUPS, 8, LANES), f32),
            ((LANES, LANES), f32),
            block,
        ],
        [ANY] + [VMEM] * 3 + [HBM] * 2 + [VMEM],
        [VMEM] * 4,
        [
            pltpu.VMEM((plane_count * width_y * 8, LANES), f32),
            slots_smem,
            pltpu.VMEM(coupling.shape, f32),
            pltpu.VMEM((1, band_count), f32),
            pltpu.SemaphoreType.DMA((3,)),
        ],
        input_output_aliases={1: 0},
    )(
        rows,
        grid,
        halo_a,
        table,
        in_hbm(coupling),
        in_hbm(band_weights[None, :]),
        margins_to_b,
    )

    _, force_margins = call(
        first_kernel,
        "first",
        [((grid_rows, LANES), f32), ((GROUPS, 3, 8, LANES), f32)],
        [ANY] + [VMEM] * 4,
        [VMEM] * 2,
        [slots_smem, pltpu.SemaphoreType.DMA],
        input_output_aliases={1: 0},
    )(rows, grid, halo_b, table, yz_margins)

    device_count = domain_count * lax.axis_size("band")
    scaled, copies = call(
        functools.partial(combine_kernel, domain_count=domain_count),
        "combine",
        [blocks, ((device_count, 1, LANES), f32)],
        [VMEM] * 7,
        [VMEM] * 2,
        limit=2,
    )(margins, from_a, from_b, from_c, mixing, factor, force_margins)
    gathered = lax.all_to_all(copies, ("dom", "band"), 0, 0)

    (applied,) = call(
        apply_kernel,
        "apply",
        [(wavefunctions.shape, bf16)],
        [ANY, HBM, HBM] + [VMEM] * 4,
        [HBM],
        [
            pltpu.VMEM(wavefunctions.shape, bf16),
            pltpu.VMEM((plane_count * width_y * 8, LANES), f32),
            pltpu.VMEM((band_count, plane_count + 2 * PAD, width_y, width_z), bf16),
            pltpu.VMEM(potential.shape, f32),
            slots_smem,
            pltpu.SemaphoreType.DMA((2, plane_count)),
            pltpu.SemaphoreType.DMA((4,)),
        ],
        limit=16,
    )(rows, in_hbm(wavefunctions), in_hbm(potential), halo_a, halo_b, table, scaled)

    (forces,) = call(
        total_kernel, "total", [((3, ATOM_DEV), f32)], [VMEM], [VMEM], limit=2
    )(gathered.reshape(device_count // 8, 8, LANES))
    return (applied, forces)


def solution(mesh):
    placed = (
        P("band", "dom", None, None),
        P("dom", None, None),
        P("dom", None, None),
        P("dom"),
        P("dom"),
        P(),
        P("band"),
    )
    return jax.shard_map(
        per_device,
        mesh=mesh,
        in_specs=placed,
        out_specs=(P("band", "dom", None, None), P(None, "dom")),
        check_vma=False,
    )
```

time: 37.3 us -> 36.4 us (0.976)
  the two profiles are of different devices: /device:TPU:0 before, /device:TPU:1 now
where the time goes in v4:
time: 36.4 us; the launch traced here: 36.2 us
  starting transfers between devices  16 us (44%)
  Pallas kernels  14.6 us (40%)
  waiting for transfers between devices  4.89 us (13%)
  between operations  0.71 us (2%)
    all_to_all x1, starting transfers between devices, per_device(): gathered = lax.all_to_all(copies, ('dom', 'band'), 0, 0)  10.6 us
    pallas_call x1, Pallas kernels, per_device(): call(apply_kernel, 'apply', [(wavefunctions.shape, bf16)], [ANY, HBM, HBM...  5.72 us
    all_to_all x1, waiting for transfers between devices, per_device(): gathered = lax.all_to_all(copies, ('dom', 'band'), 0, 0)  4.05 us
    ppermute x2, starting transfers between devices, swap_a(): lax.ppermute(x, 'dom', [(i, partner_a(i)) for i in range(lax.axis_size('d...  3.25 us
    pallas_call x1, Pallas kernels, per_device(): call(gradient_kernel, 'gradient', [((grid_rows, LANES), f32), ((2, GROUPS...  2.41 us
    pallas_call x1, Pallas kernels, per_device(): call(functools.partial(relayout_kernel, domain_count=domain_count), 'rela...  2.27 us
    ppermute x2, starting transfers between devices, swap_b(): lax.ppermute(x, 'dom', [(i, partner_b(i, count)) for i in range(count)])  1.27 us
    pallas_call x1, Pallas kernels, per_device(): call(edge_kernel, 'edges', [edge, edge], [HBM], [VMEM, VMEM], [pltpu.Sema...  1.23 us
  transfers between devices with their start and end apart: 6, of which 2 were waited for; matrix products, arithmetic and copies ran while one was open for 0% of the time, Pallas kernels for 32%

profile of v4, /device:TPU:1, one launch (start us, length us, event | category | flops | bytes accessed | tf_op | source)
XLA Modules:
  0.0 36.2 jit_solution(6683984835720554481)
XLA Ops:
  0.6 1.2 %edges.1 = (bf16[8,2,128,128]{3,2,1,0:T(8,128)(2,1)S(1)}, bf16[8,2,128,128]{3,2,1,0:T(8,128)(2,1)S(1)}) custom-call(bf16[8,8,128,128]{3,2,1,0:T(8,128)(2,1)} %wave_hbm.3), custom_call_target="tpu_custom_call" | custom-call | flops 1000 | bytes 1000 | tf_op jit(solution)/shard_map/edges/pallas_call | solution.py:525
  1.9 1.5 %collective-permute-start = (bf16[8,2,128,128]{3,2,1,0:T(8,128)(2,1)S(1)}, bf16[8,2,128,128]{3,2,1,0:T(8,128)(2,1)S(1)}, u32[]{:S(2)}, u32[]{:S(2)}) collective-permute-start(bf16[8,2,128,128]{3,2,1,0:T(8,128)(2,1)S(1)} %get-tuple-element.18), channel_id=1, source_target_pairs={{0,16},{16,0},{32,48},{48,32},{64,80},{80,64},{96,112},{112,96},{1... | collective-permute-start | bytes 1572872 | tf_op jit(solution)/shard_map/ppermute | solution.py:28
  3.4 1.3 %collective-permute-start.1 = (bf16[8,2,128,128]{3,2,1,0:T(8,128)(2,1)S(1)}, bf16[8,2,128,128]{3,2,1,0:T(8,128)(2,1)S(1)}, u32[]{:S(2)}, u32[]{:S(2)}) collective-permute-start(bf16[8,2,128,128]{3,2,1,0:T(8,128)(2,1)S(1)} %get-tuple-element.19), channel_id=1, source_target_pairs={{0,112},{16,32},{32,16},{48,64},{64,48},{80,96},{96,80},{112,0},{1... | collective-permute-start | bytes 1572872 | tf_op jit(solution)/shard_map/ppermute | solution.py:33
  4.6 2.3 %relayout.1 = (s32[36]{0:T(128)S(1)}, f32[12288,128]{1,0:T(8,128)S(1)}, bf16[3,128,1024]{2,1,0:T(8,128)(2,1)S(1)}, f32[3,8,128]{2,1,0:T(8,128)S(1)}, f32[2,8,128]{2,1,0:T(8,128)S(1)}, /*index=5*/f32[8,128]{1,0:T(8,128)S(1)}) custom-call(s32[36]{0:T(128)} %atoms_hbm.1, s32[36]{0:T(128)} %first_rows_hbm.1, bf16[8,8,128,128]{3,2,1,0:T(8,128)(2,1)} %wave_hbm.3, ...), custom_call_target="tpu_custom_call" | custom-call | flops 1000 | bytes 1000 | tf_op jit(solution)/shard_map/relayout/pallas_call | solution.py:536
  6.9 1.8 %collective-permute-start.2 = (f32[2,8,128]{2,1,0:T(8,128)S(1)}, f32[2,8,128]{2,1,0:T(8,128)S(1)}, u32[]{:S(2)}, u32[]{:S(2)}) collective-permute-start(f32[2,8,128]{2,1,0:T(8,128)S(1)} %get-tuple-element.22), channel_id=1, source_target_pairs={{0,16},{16,0},{32,48},{48,32},{64,80},{80,64},{96,112},{112,96},{1... | collective-permute-start | bytes 24584 | tf_op jit(solution)/shard_map/ppermute | solution.py:28
  8.7 0.8 %collective-permute-done.2.from_a_ref = f32[2,8,128]{2,1,0:T(8,128)S(1)} collective-permute-done((f32[2,8,128]{2,1,0:T(8,128)S(1)}, f32[2,8,128]{2,1,0:T(8,128)S(1)}, u32[]{:S(2)}, u32[]{:S(2)}) %collective-permute-start.2) | collective-permute-done | bytes 8224 | tf_op jit(solution)/shard_map/ppermute | solution.py:28
  9.5 0.0 collective-permute-start.3
  9.5 0.8 %collective-permute-start.4 = (f32[8,128]{1,0:T(8,128)S(1)}, f32[8,128]{1,0:T(8,128)S(1)}, u32[]{:S(2)}, u32[]{:S(2)}) collective-permute-start(f32[8,128]{1,0:T(8,128)S(1)} %get-tuple-element.23), channel_id=1, source_target_pairs={{0,96},{16,48},{32,0},{48,80},{64,32},{80,112},{96,64},{112,16},{1... | collective-permute-start | bytes 12296 | tf_op jit(solution)/shard_map/ppermute | solution.py:38
  10.3 0.0 collective-permute-done.halo_a_ref
  10.4 2.4 %gradient.1 = (f32[12288,128]{1,0:T(8,128)S(1)}, f32[2,3,8,128]{3,2,1,0:T(8,128)S(1)}, f32[128,128]{1,0:T(8,128)S(1)}, f32[8,128]{1,0:T(8,128)S(1)}) custom-call(s32[36]{0:T(128)S(1)} %get-tuple-element.17.rows_in, f32[12288,128]{1,0:T(8,128)S(1)} %get-tuple-element.24.grid_in, ...), custom_call_target="tpu_custom_call", output_to_operand_aliasing={{0}: (1, {})} | custom-call | flops 1000 | bytes 1000 | tf_op jit(solution)/shard_map/gradient/pallas_call | solution.py:569
  12.8 0.0 collective-permute-done.1.halo_b_ref
  12.8 1.1 %first.1 = (f32[12288,128]{1,0:T(8,128)S(1)}, f32[3,3,8,128]{3,2,1,0:T(8,128)S(1)}) custom-call(s32[36]{0:T(128)S(1)} %get-tuple-element.17.rows_in, f32[12288,128]{1,0:T(8,128)S(1)} %get-tuple-element.27.grid_in, bf16[8,2,128,128]{3,2,1,0:T(8,128)(2,1)S(1)} %collective-permute-done.1.halo_b_ref, ...), custom_call_target="tpu_custom_call", output_to_operand_aliasing={{0}: (1, {})} | custom-call | flops 1000 | bytes 1000 | tf_op jit(solution)/shard_map/first/pallas_call | solution.py:598
  13.9 0.0 collective-permute-done.4.from_c_ref
  13.9 0.0 collective-permute-done.3.from_b_ref
  13.9 1.1 %combine.1 = (f32[3,8,128]{2,1,0:T(8,128)S(1)}, f32[128,1,128]{2,1,0:T(1,128)}) custom-call(f32[3,8,128]{2,1,0:T(8,128)S(1)} %get-tuple-element.21.margin_ref, f32[2,8,128]{2,1,0:T(8,128)S(1)} %collective-permute-done.2.from_a_ref, f32[2,8,128]{2,1,0:T(8,128)S(1)} %collective-permute-done.3.from_b_ref, f32[8,128]{1,0:T(8,128)S(1)} %collective-permute-done.4.from_c_ref, ...), custom_call_target="tpu_custom_call" | custom-call | flops 1000 | bytes 1000 | tf_op jit(solution)/shard_map/combine/pallas_call | solution.py:609
  15.0 10.6 %all-to-all-start = ((f32[128,1,128]{2,1,0:T(1,128)}), f32[128,1,128]{2,1,0:T(1,128)S(1)}, u32[]{:S(2)}, u32[]{:S(2)}) async-start(f32[128,1,128]{2,1,0:T(1,128)} %get-tuple-element.31), calls=%async_computation | async-start | bytes 131072 | tf_op jit(solution)/shard_map/all_to_all | solution.py:617
  25.6 5.7 %apply.1 = bf16[8,8,128,128]{3,2,1,0:T(8,128)(2,1)} custom-call(s32[36]{0:T(128)S(1)} %get-tuple-element.17.rows_in, bf16[8,8,128,128]{3,2,1,0:T(8,128)(2,1)} %wave_hbm.3, f32[8,128,128]{2,1,0:T(8,128)} %pot_hbm.1, bf16[8,2,128,128]{3,2,1,0:T(8,128)(2,1)S(1)} %collective-permute-done.halo_a_ref, ...), custom_call_target="tpu_custom_call" | custom-call | flops 1000 | bytes 1000 | tf_op jit(solution)/shard_map/apply/pallas_call | solution.py:619
  31.4 4.1 %all-to-all-done = f32[128,1,128]{2,1,0:T(1,128)S(1)} async-done(((f32[128,1,128]{2,1,0:T(1,128)}), f32[128,1,128]{2,1,0:T(1,128)S(1)}, u32[]{:S(2)}, u32[]{:S(2)}) %all-to-all-start) | async-done | bytes 65568 | tf_op jit(solution)/shard_map/all_to_all | solution.py:617
  35.4 0.8 %total.1 = f32[3,12]{1,0:T(4,128)} custom-call(f32[16,8,128]{2,1,0:T(8,128)S(1)} %bitcast.2), custom_call_target="tpu_custom_call" | custom-call | flops 1000 | bytes 1000 | tf_op jit(solution)/shard_map/total/pallas_call | solution.py:637
  (1 shorter events, 0.0 us)
Async XLA Ops:
  1.9 8.5 %collective-permute-start = (bf16[8,2,128,128]{3,2,1,0:T(8,128)(2,1)S(1)}, bf16[8,2,128,128]{3,2,1,0:T(8,128)(2,1)S(1)}, u32[]{:S(2)}, u32[]{:S(2)}) collective-permute-start(bf16[8,2,128,128]{3,2,1,0:T(8,128)(2,1)S(1)} %get-tuple-element.18), channel_id=1, source_target_pairs={{0,16},{16,0},{32,48},{48,32},{64,80},{80,64},{96,112},{112,96},{1... | collective-permute-start | bytes 1572872 | tf_op jit(solution)/shard_map/ppermute | solution.py:28
  3.4 9.4 %collective-permute-start.1 = (bf16[8,2,128,128]{3,2,1,0:T(8,128)(2,1)S(1)}, bf16[8,2,128,128]{3,2,1,0:T(8,128)(2,1)S(1)}, u32[]{:S(2)}, u32[]{:S(2)}) collective-permute-start(bf16[8,2,128,128]{3,2,1,0:T(8,128)(2,1)S(1)} %get-tuple-element.19), channel_id=1, source_target_pairs={{0,112},{16,32},{32,16},{48,64},{64,48},{80,96},{96,80},{112,0},{1... | collective-permute-start | bytes 1572872 | tf_op jit(solution)/shard_map/ppermute | solution.py:33
  6.9 2.6 %collective-permute-start.2 = (f32[2,8,128]{2,1,0:T(8,128)S(1)}, f32[2,8,128]{2,1,0:T(8,128)S(1)}, u32[]{:S(2)}, u32[]{:S(2)}) collective-permute-start(f32[2,8,128]{2,1,0:T(8,128)S(1)} %get-tuple-element.22), channel_id=1, source_target_pairs={{0,16},{16,0},{32,48},{48,32},{64,80},{80,64},{96,112},{112,96},{1... | collective-permute-start | bytes 24584 | tf_op jit(solution)/shard_map/ppermute | solution.py:28
  9.5 4.4 %collective-permute-start.3 = (f32[2,8,128]{2,1,0:T(8,128)S(1)}, f32[2,8,128]{2,1,0:T(8,128)S(1)}, u32[]{:S(2)}, u32[]{:S(2)}) collective-permute-start(f32[2,8,128]{2,1,0:T(8,128)S(1)} %forward.1._), channel_id=1, source_target_pairs={{0,112},{16,32},{32,16},{48,64},{64,48},{80,96},{96,80},{112,0},{1... | collective-permute-start | bytes 24584 | tf_op jit(solution)/shard_map/ppermute | solution.py:33
  9.5 4.4 %collective-permute-start.4 = (f32[8,128]{1,0:T(8,128)S(1)}, f32[8,128]{1,0:T(8,128)S(1)}, u32[]{:S(2)}, u32[]{:S(2)}) collective-permute-start(f32[8,128]{1,0:T(8,128)S(1)} %get-tuple-element.23), channel_id=1, source_target_pairs={{0,96},{16,48},{32,0},{48,80},{64,32},{80,112},{96,64},{112,16},{1... | collective-permute-start | bytes 12296 | tf_op jit(solution)/shard_map/ppermute | solution.py:38
  15.0 20.4 %all-to-all-start = ((f32[128,1,128]{2,1,0:T(1,128)}), f32[128,1,128]{2,1,0:T(1,128)S(1)}, u32[]{:S(2)}, u32[]{:S(2)}) async-start(f32[128,1,128]{2,1,0:T(1,128)} %get-tuple-element.31), calls=%async_computation | async-start | bytes 131072 | tf_op jit(solution)/shard_map/all_to_all | solution.py:617

commit v5 on v4

--- a/solution.py
+++ b/solution.py
@@ -172,13 +172,15 @@
         if group < 2:
             to_a_ref[group] = sums
         else:
-            to_c_ref[...] = sums
+            to_c_ref[...] = jnp.zeros(to_c_ref.shape, f32)
+            to_c_ref[0] = sums
     rows_copy.wait()
 
 
 def forward_kernel(margin_ref, from_a_ref, to_b_ref):
     to_b_ref[0] = margin_ref[2]
     to_b_ref[1] = margin_ref[1] + from_a_ref[0]
+    to_b_ref[2:] = jnp.zeros((to_b_ref.shape[0] - 2, 8, LANES), f32)
 
 
 def third_shift(center, offset):
@@ -275,6 +277,15 @@
         mixing_ref[a * proj_count : (a + 1) * proj_count, :] = jnp.where(keep, tiled, 0.0)
 
 
+def along_x(grid_ref, hop):
+    def field(base):
+        near = at_row(grid_ref, base + 3 * hop) - at_row(grid_ref, base + hop)
+        far = at_row(grid_ref, base + 4 * hop) - at_row(grid_ref, base)
+        return (2.0 / 3.0) * near - (1.0 / 12.0) * far
+
+    return field
+
+
 def first_kernel(
     rows_in,
     grid_in,
@@ -295,18 +306,30 @@
 
     for i in range(PAD):
         plane_to_rows(halo_b_ref, i, grid_ref, (i + (planes + PAD) * odd) * hop)
-
-    def along_x(base):
-        near = at_row(grid_ref, base + 3 * hop) - at_row(grid_ref, base + hop)
-        far = at_row(grid_ref, base + 4 * hop) - at_row(grid_ref, base)
-        return (2.0 / 3.0) * near - (1.0 / 12.0) * far
-
     rows_copy.wait()
-    for group in range(GROUPS):
-        (first,) = measure(rows_ref, group, table_ref[group], [along_x])
-        force_ref[group, 0] = first
-        force_ref[group, 1] = yz_ref[0, group]
-        force_ref[group, 2] = yz_ref[1, group]
+    (force_ref[0],) = measure(rows_ref, 0, table_ref[0], [along_x(grid_ref, hop)])
+    for k in range(2):
+        force_ref[1 + k] = yz_ref[k, 0]
+
+
+def rest_kernel(rows_in, grid_ref, table_ref, yz_ref, _, force_ref, rows_ref, rows_sem):
+    rows_copy = start_rows(rows_in, rows_ref, rows_sem)
+    rows_copy.wait()
+    for group in range(1, GROUPS):
+        (force_ref[group - 1, 0],) = measure(
+            rows_ref, group, table_ref[group], [along_x(grid_ref, LANES * 8)]
+        )
+        for k in range(2):
+            force_ref[group - 1, 1 + k] = yz_ref[k, group]
+
+
+def pieces(x, count):
+    out = []
+    for _ in range(count):
+        piece = x.astype(bf16)
+        out.append(piece)
+        x = x - piece.astype(f32)
+    return out
 
 
 def combine_kernel(
@@ -317,49 +340,54 @@
     mixing_ref,
     factor_ref,
     force_ref,
+    force_from_a_ref,
     scaled_ref,
     copies_ref,
-    *,
-    domain_count,
 ):
     totals = jnp.concatenate(
         [
-            margin_ref[0] + from_a_ref[1] + from_c_ref[...],
+            margin_ref[0] + from_a_ref[1] + from_c_ref[0],
             margin_ref[1] + from_a_ref[0] + from_b_ref[0],
             margin_ref[2] + from_b_ref[1],
         ],
         axis=0,
     )
-    scaled = jnp.dot(
-        totals, mixing_ref[...], precision=lax.Precision.HIGHEST, preferred_element_type=f32
-    )
+    count = totals.shape[0]
+    upper, lower = pieces(totals, 2)
+    mixed = [
+        jnp.dot(
+            jnp.concatenate([upper, lower], axis=0), mixing, preferred_element_type=f32
+        )
+        for mixing in pieces(mixing_ref[...], 2)
+    ]
+    scaled = mixed[0][:count] + (mixed[0][count:] + mixed[1][:count])
     parts = []
     for group in range(GROUPS):
         one = scaled[group * 8 : group * 8 + 8]
         scaled_ref[group] = one
+        if group == 0:
+            continue
         weighted = factor_ref[...] * one
         for k in range(3):
-            parts.append(jnp.sum(force_ref[group, k] * weighted, axis=0, keepdims=True))
+            force = force_ref[group - 1, k]
+            if group == 1:
+                force = force + force_from_a_ref[k]
+            parts.append(jnp.sum(force * weighted, axis=0, keepdims=True))
     summed = jnp.concatenate(parts, axis=0)
     for step in (1, 2, 4):
         summed = summed + pltpu.roll(summed, LANES - step, 1)
     component = lax.bitwise_and(lax.broadcasted_iota(jnp.int32, (1, LANES), 1), 7)
-    copies_ref[...] = jnp.zeros(copies_ref.shape, f32)
-    bands = copies_ref.shape[0] // domain_count
-    index, odd = own_domain()
-    owners = (
-        index + 1 - 2 * odd,
-        index,
-        lax.rem(index - 1 + 2 * odd + domain_count, domain_count),
-    )
-    for group, owner in enumerate(owners):
+    tiles = copies_ref.shape[0] // 2
+    _, odd = own_domain()
+    for group, half in ((1, 1 - odd), (2, odd)):
         row = jnp.zeros((1, LANES), f32)
         for k in range(3):
-            value = summed[group * 3 + k : group * 3 + k + 1]
+            part = (group - 1) * 3 + k
+            value = summed[part : part + 1]
             value = pltpu.roll(value, k, 1) if k else value
             row = row + jnp.where(component == k, value, 0.0)
-        for b in range(bands):
-            copies_ref[owner * bands + b] = row
+        for tile in range(tiles):
+            copies_ref[half * tiles + tile] = jnp.broadcast_to(row, (8, LANES))
 
 
 def total_kernel(gathered_ref, forces_ref):
@@ -371,8 +399,9 @@
     source = lax.broadcasted_iota(jnp.int32, (LANES, LANES), 0)
     target = lax.broadcasted_iota(jnp.int32, (LANES, LANES), 1)
     collect = (lax.shift_right_logical(source, 3) == target).astype(f32)
-    forces = jnp.dot(
-        split, collect, precision=lax.Precision.HIGHEST, preferred_element_type=f32
+    forces = sum(
+        jnp.dot(piece, collect.astype(bf16), preferred_element_type=f32)
+        for piece in pieces(split, 3)
     )
     forces_ref[...] = forces[:3, :atoms]
 
@@ -530,8 +559,8 @@
         [VMEM, VMEM],
         [pltpu.SemaphoreType.DMA((2,))],
     )(in_hbm(wavefunctions))
+    halo_b = swap_b(to_b)
     halo_a = swap_a(to_a)
-    halo_b = swap_b(to_b)
 
     rows, grid, table, margins, margins_to_a, margins_to_c = call(
         functools.partial(relayout_kernel, domain_count=domain_count),
@@ -542,7 +571,7 @@
             ((GROUPS, LANES, tile_len), bf16),
             blocks,
             pair,
-            block,
+            ((6, 8, LANES), f32),
         ],
         [HBM] * 4,
         [ANY] + [VMEM] * 5,
@@ -560,11 +589,11 @@
     )(*map(in_hbm, (margin_atoms, tile_rows, wavefunctions, projectors)))
 
     from_a = swap_a(margins_to_a)
+    (margins_to_b,) = call(forward_kernel, "forward", [((4, 8, LANES), f32)], [VMEM] * 2, [VMEM], limit=2)(
+        margins, from_a
+    )
+    from_b = swap_b(margins_to_b)
     from_c = send_c(margins_to_c)
-    (margins_to_b,) = call(forward_kernel, "forward", [pair], [VMEM] * 2, [VMEM], limit=2)(
-        margins, from_a
-    )
-    from_b = swap_b(margins_to_b)
 
     grid, yz_margins, mixing, factor = call(
         gradient_kernel,
@@ -595,26 +624,41 @@
         margins_to_b,
     )
 
-    _, force_margins = call(
+    grid, force_to_a = call(
         first_kernel,
         "first",
-        [((grid_rows, LANES), f32), ((GROUPS, 3, 8, LANES), f32)],
+        [((grid_rows, LANES), f32), blocks],
         [ANY] + [VMEM] * 4,
         [VMEM] * 2,
         [slots_smem, pltpu.SemaphoreType.DMA],
         input_output_aliases={1: 0},
     )(rows, grid, halo_b, table, yz_margins)
-
-    device_count = domain_count * lax.axis_size("band")
+    force_from_a = swap_a(force_to_a)
+    (force_margins,) = call(
+        rest_kernel,
+        "rest",
+        [((2, 3, 8, LANES), f32)],
+        [ANY] + [VMEM] * 4,
+        [VMEM],
+        [slots_smem, pltpu.SemaphoreType.DMA],
+    )(rows, grid, table, yz_margins, force_to_a)
+
+    bands = lax.axis_size("band")
+    pairs = [
+        [dom * bands + band for dom in (i, partner_b(i, domain_count)) for band in range(bands)]
+        for i in range(1, domain_count, 2)
+    ]
     scaled, copies = call(
-        functools.partial(combine_kernel, domain_count=domain_count),
+        combine_kernel,
         "combine",
-        [blocks, ((device_count, 1, LANES), f32)],
-        [VMEM] * 7,
+        [blocks, ((2 * bands // 8, 8, LANES), f32)],
+        [VMEM] * 8,
         [VMEM] * 2,
         limit=2,
-    )(margins, from_a, from_b, from_c, mixing, factor, force_margins)
-    gathered = lax.all_to_all(copies, ("dom", "band"), 0, 0)
+    )(margins, from_a, from_b, from_c, mixing, factor, force_margins, force_from_a)
+    gathered = lax.all_to_all(
+        copies.reshape(2 * bands, 1, LANES), ("dom", "band"), 0, 0, axis_index_groups=pairs
+    )
 
     (applied,) = call(
         apply_kernel,
@@ -636,7 +680,7 @@
 
     (forces,) = call(
         total_kernel, "total", [((3, ATOM_DEV), f32)], [VMEM], [VMEM], limit=2
-    )(gathered.reshape(device_count // 8, 8, LANES))
+    )(gathered.reshape(2 * bands // 8, 8, LANES))
     return (applied, forces)
 
 

time: 36.4 us -> 34.4 us (0.945)
  the two profiles are of different devices: /device:TPU:1 before, /device:TPU:0 now
where the time goes in v5:
time: 34.4 us; the launch traced here: 34.2 us
  starting transfers between devices  16.5 us (48%)
  Pallas kernels  15.2 us (44%)
  waiting for transfers between devices  1.74 us (5%)
  between operations  0.74 us (2%)
    all_to_all x1, starting transfers between devices, per_device(): lax.all_to_all(copies.reshape(2 * bands, 1, LANES), ('dom', 'band'), 0, 0...  10.5 us
    pallas_call x1, Pallas kernels, per_device(): call(apply_kernel, 'apply', [(wavefunctions.shape, bf16)], [ANY, HBM, HBM...  5.72 us
    ppermute x2, starting transfers between devices, swap_b(): lax.ppermute(x, 'dom', [(i, partner_b(i, count)) for i in range(count)])  4.85 us
    pallas_call x1, Pallas kernels, per_device(): call(gradient_kernel, 'gradient', [((grid_rows, LANES), f32), ((2, GROUPS...  2.41 us
    pallas_call x1, Pallas kernels, per_device(): call(functools.partial(relayout_kernel, domain_count=domain_count), 'rela...  2.26 us
    all_to_all x1, waiting for transfers between devices, per_device(): lax.all_to_all(copies.reshape(2 * bands, 1, LANES), ('dom', 'band'), 0, 0...  1.31 us
    pallas_call x1, Pallas kernels, per_device(): call(edge_kernel, 'edges', [edge, edge], [HBM], [VMEM, VMEM], [pltpu.Sema...  1.23 us
    pallas_call x1, Pallas kernels, per_device(): call(combine_kernel, 'combine', [blocks, ((2 * bands // 8, 8, LANES), f32...  1.03 us
  transfers between devices with their start and end apart: 7, of which 3 were waited for; matrix products, arithmetic and copies ran while one was open for 0% of the time, Pallas kernels for 36%

profile of v5, /device:TPU:0, one launch (start us, length us, event | category | flops | bytes accessed | tf_op | source)
XLA Modules:
  0.0 34.2 jit_solution(10711860992513667419)
XLA Ops:
  0.6 1.2 %edges.1 = (bf16[8,2,128,128]{3,2,1,0:T(8,128)(2,1)S(1)}, bf16[8,2,128,128]{3,2,1,0:T(8,128)(2,1)S(1)}) custom-call(bf16[8,8,128,128]{3,2,1,0:T(8,128)(2,1)} %wave_hbm.3), custom_call_target="tpu_custom_call" | custom-call | flops 1000 | bytes 1000 | tf_op jit(solution)/shard_map/edges/pallas_call | solution.py:554
  1.9 0.1 collective-permute-start
  2.0 2.9 %collective-permute-start.1 = (bf16[8,2,128,128]{3,2,1,0:T(8,128)(2,1)S(1)}, bf16[8,2,128,128]{3,2,1,0:T(8,128)(2,1)S(1)}, u32[]{:S(2)}, u32[]{:S(2)}) collective-permute-start(bf16[8,2,128,128]{3,2,1,0:T(8,128)(2,1)S(1)} %get-tuple-element.20), channel_id=1, source_target_pairs={{0,112},{16,32},{32,16},{48,64},{64,48},{80,96},{96,80},{112,0},{1... | collective-permute-start | bytes 1572872 | tf_op jit(solution)/shard_map/ppermute | solution.py:33
  4.9 2.3 %relayout.1 = (s32[36]{0:T(128)S(1)}, f32[12288,128]{1,0:T(8,128)S(1)}, bf16[3,128,1024]{2,1,0:T(8,128)(2,1)S(1)}, f32[3,8,128]{2,1,0:T(8,128)S(1)}, f32[2,8,128]{2,1,0:T(8,128)S(1)}, /*index=5*/f32[6,8,128]{2,1,0:T(8,128)S(1)}) custom-call(s32[36]{0:T(128)} %atoms_hbm.1, s32[36]{0:T(128)} %first_rows_hbm.1, bf16[8,8,128,128]{3,2,1,0:T(8,128)(2,1)} %wave_hbm.3, ...), custom_call_target="tpu_custom_call" | custom-call | flops 1000 | bytes 1000 | tf_op jit(solution)/shard_map/relayout/pallas_call | solution.py:565
  7.2 0.1 collective-permute-start.2
  7.3 0.9 %collective-permute-start.4 = (f32[6,8,128]{2,1,0:T(8,128)S(1)}, f32[6,8,128]{2,1,0:T(8,128)S(1)}, u32[]{:S(2)}, u32[]{:S(2)}) collective-permute-start(f32[6,8,128]{2,1,0:T(8,128)S(1)} %get-tuple-element.24), channel_id=1, source_target_pairs={{0,96},{16,48},{32,0},{48,80},{64,32},{80,112},{96,64},{112,16},{1... | collective-permute-start | bytes 73736 | tf_op jit(solution)/shard_map/ppermute | solution.py:38
  8.2 0.3 collective-permute-done.2.from_a_ref
  8.4 1.9 %collective-permute-start.3 = (f32[4,8,128]{2,1,0:T(8,128)S(1)}, f32[4,8,128]{2,1,0:T(8,128)S(1)}, u32[]{:S(2)}, u32[]{:S(2)}) collective-permute-start(f32[4,8,128]{2,1,0:T(8,128)S(1)} %forward.1._), channel_id=1, source_target_pairs={{0,112},{16,32},{32,16},{48,64},{64,48},{80,96},{96,80},{112,0},{1... | collective-permute-start | bytes 49160 | tf_op jit(solution)/shard_map/ppermute | solution.py:33
  10.3 0.0 collective-permute-done.halo_a_ref
  10.3 2.4 %gradient.1 = (f32[12288,128]{1,0:T(8,128)S(1)}, f32[2,3,8,128]{3,2,1,0:T(8,128)S(1)}, f32[128,128]{1,0:T(8,128)S(1)}, f32[8,128]{1,0:T(8,128)S(1)}) custom-call(s32[36]{0:T(128)S(1)} %get-tuple-element.18.rows_in, f32[12288,128]{1,0:T(8,128)S(1)} %get-tuple-element.25.grid_in, ...), custom_call_target="tpu_custom_call", output_to_operand_aliasing={{0}: (1, {})} | custom-call | flops 1000 | bytes 1000 | tf_op jit(solution)/shard_map/gradient/pallas_call | solution.py:598
  12.8 0.0 collective-permute-done.1.halo_b_ref
  12.8 0.8 %first.1 = (f32[12288,128]{1,0:T(8,128)S(1)}, f32[3,8,128]{2,1,0:T(8,128)S(1)}) custom-call(s32[36]{0:T(128)S(1)} %get-tuple-element.18.rows_in, f32[12288,128]{1,0:T(8,128)S(1)} %get-tuple-element.28.grid_in, bf16[8,2,128,128]{3,2,1,0:T(8,128)(2,1)S(1)} %collective-permute-done.1.halo_b_ref, ...), custom_call_target="tpu_custom_call", output_to_operand_aliasing={{0}: (1, {})} | custom-call | flops 1000 | bytes 1000 | tf_op jit(solution)/shard_map/first/pallas_call | solution.py:627
  13.6 0.1 collective-permute-start.5
  13.7 1.0 %rest.1.force_ref = f32[2,3,8,128]{3,2,1,0:T(8,128)S(1)} custom-call(s32[36]{0:T(128)S(1)} %get-tuple-element.18.rows_in, f32[12288,128]{1,0:T(8,128)S(1)} %get-tuple-element.30.grid_ref, bf16[3,128,1024]{2,1,0:T(8,128)(2,1)S(1)} %get-tuple-element.21.table_ref, f32[2,3,8,128]{3,2,1,0:T(8,128)S(1)} %get-tuple-element.29.yz_ref, ...), custom_call_target="tpu_custom_call" | custom-call | flops 1000 | bytes 1000 | tf_op jit(solution)/shard_map/rest/pallas_call | solution.py:637
  14.7 0.0 collective-permute-done.3.from_b_ref
  14.7 0.0 collective-permute-done.4.from_c_ref
  14.7 0.2 collective-permute-done.5.force_from_a_ref
  14.9 1.0 %combine.1 = (f32[3,8,128]{2,1,0:T(8,128)S(1)}, f32[4,8,128]{2,1,0:T(8,128)}) custom-call(f32[3,8,128]{2,1,0:T(8,128)S(1)} %get-tuple-element.22.margin_ref, f32[2,8,128]{2,1,0:T(8,128)S(1)} %collective-permute-done.2.from_a_ref, f32[4,8,128]{2,1,0:T(8,128)S(1)} %collective-permute-done.3.from_b_ref, f32[6,8,128]{2,1,0:T(8,128)S(1)} %collective-permute-done.4.from_c_ref, ...), custom_call_target="tpu_custom_call" | custom-call | flops 1000 | bytes 1000 | tf_op jit(solution)/shard_map/combine/pallas_call | solution.py:651
  15.9 10.5 %all-to-all-start = ((f32[32,1,128]{2,1,0:T(1,128)}), f32[32,1,128]{2,1,0:T(1,128)S(1)}, u32[]{:S(2)}, u32[]{:S(2)}) async-start(f32[32,1,128]{2,1,0:T(1,128)} %bitcast.2), calls=%async_computation | async-start | bytes 32768 | tf_op jit(solution)/shard_map/all_to_all | solution.py:659
  26.4 5.7 %apply.1 = bf16[8,8,128,128]{3,2,1,0:T(8,128)(2,1)} custom-call(s32[36]{0:T(128)S(1)} %get-tuple-element.18.rows_in, bf16[8,8,128,128]{3,2,1,0:T(8,128)(2,1)} %wave_hbm.3, f32[8,128,128]{2,1,0:T(8,128)} %pot_hbm.1, bf16[8,2,128,128]{3,2,1,0:T(8,128)(2,1)S(1)} %collective-permute-done.halo_a_ref, ...), custom_call_target="tpu_custom_call" | custom-call | flops 1000 | bytes 1000 | tf_op jit(solution)/shard_map/apply/pallas_call | solution.py:663
  32.1 1.3 %all-to-all-done = f32[32,1,128]{2,1,0:T(1,128)S(1)} async-done(((f32[32,1,128]{2,1,0:T(1,128)}), f32[32,1,128]{2,1,0:T(1,128)S(1)}, u32[]{:S(2)}, u32[]{:S(2)}) %all-to-all-start) | async-done | bytes 16416 | tf_op jit(solution)/shard_map/all_to_all | solution.py:659
  33.4 0.7 %total.1 = f32[3,12]{1,0:T(4,128)} custom-call(f32[4,8,128]{2,1,0:T(8,128)S(1)} %bitcast.5), custom_call_target="tpu_custom_call" | custom-call | flops 1000 | bytes 1000 | tf_op jit(solution)/shard_map/total/pallas_call | solution.py:681
  (1 shorter events, 0.0 us)
Async XLA Ops:
  1.9 8.5 %collective-permute-start = (bf16[8,2,128,128]{3,2,1,0:T(8,128)(2,1)S(1)}, bf16[8,2,128,128]{3,2,1,0:T(8,128)(2,1)S(1)}, u32[]{:S(2)}, u32[]{:S(2)}) collective-permute-start(bf16[8,2,128,128]{3,2,1,0:T(8,128)(2,1)S(1)} %get-tuple-element.19), channel_id=1, source_target_pairs={{0,16},{16,0},{32,48},{48,32},{64,80},{80,64},{96,112},{112,96},{1... | collective-permute-start | bytes 1572872 | tf_op jit(solution)/shard_map/ppermute | solution.py:28
  2.0 10.8 %collective-permute-start.1 = (bf16[8,2,128,128]{3,2,1,0:T(8,128)(2,1)S(1)}, bf16[8,2,128,128]{3,2,1,0:T(8,128)(2,1)S(1)}, u32[]{:S(2)}, u32[]{:S(2)}) collective-permute-start(bf16[8,2,128,128]{3,2,1,0:T(8,128)(2,1)S(1)} %get-tuple-element.20), channel_id=1, source_target_pairs={{0,112},{16,32},{32,16},{48,64},{64,48},{80,96},{96,80},{112,0},{1... | collective-permute-start | bytes 1572872 | tf_op jit(solution)/shard_map/ppermute | solution.py:33
  7.2 1.3 %collective-permute-start.2 = (f32[2,8,128]{2,1,0:T(8,128)S(1)}, f32[2,8,128]{2,1,0:T(8,128)S(1)}, u32[]{:S(2)}, u32[]{:S(2)}) collective-permute-start(f32[2,8,128]{2,1,0:T(8,128)S(1)} %get-tuple-element.23), channel_id=1, source_target_pairs={{0,16},{16,0},{32,48},{48,32},{64,80},{80,64},{96,112},{112,96},{1... | collective-permute-start | bytes 24584 | tf_op jit(solution)/shard_map/ppermute | solution.py:28
  7.3 7.4 %collective-permute-start.4 = (f32[6,8,128]{2,1,0:T(8,128)S(1)}, f32[6,8,128]{2,1,0:T(8,128)S(1)}, u32[]{:S(2)}, u32[]{:S(2)}) collective-permute-start(f32[6,8,128]{2,1,0:T(8,128)S(1)} %get-tuple-element.24), channel_id=1, source_target_pairs={{0,96},{16,48},{32,0},{48,80},{64,32},{80,112},{96,64},{112,16},{1... | collective-permute-start | bytes 73736 | tf_op jit(solution)/shard_map/ppermute | solution.py:38
  8.4 6.3 %collective-permute-start.3 = (f32[4,8,128]{2,1,0:T(8,128)S(1)}, f32[4,8,128]{2,1,0:T(8,128)S(1)}, u32[]{:S(2)}, u32[]{:S(2)}) collective-permute-start(f32[4,8,128]{2,1,0:T(8,128)S(1)} %forward.1._), channel_id=1, source_target_pairs={{0,112},{16,32},{32,16},{48,64},{64,48},{80,96},{96,80},{112,0},{1... | collective-permute-start | bytes 49160 | tf_op jit(solution)/shard_map/ppermute | solution.py:33
  13.6 1.3 %collective-permute-start.5 = (f32[3,8,128]{2,1,0:T(8,128)S(1)}, f32[3,8,128]{2,1,0:T(8,128)S(1)}, u32[]{:S(2)}, u32[]{:S(2)}) collective-permute-start(f32[3,8,128]{2,1,0:T(8,128)S(1)} %get-tuple-element.31._), channel_id=1, source_target_pairs={{0,16},{16,0},{32,48},{48,32},{64,80},{80,64},{96,112},{112,96},{1... | collective-permute-start | bytes 36872 | tf_op jit(solution)/shard_map/ppermute | solution.py:28
  15.9 17.5 %all-to-all-start = ((f32[32,1,128]{2,1,0:T(1,128)}), f32[32,1,128]{2,1,0:T(1,128)S(1)}, u32[]{:S(2)}, u32[]{:S(2)}) async-start(f32[32,1,128]{2,1,0:T(1,128)} %bitcast.2), calls=%async_computation | async-start | bytes 32768 | tf_op jit(solution)/shard_map/all_to_all | solution.py:659

commit v6 on v5

--- a/solution.py
+++ b/solution.py
@@ -43,11 +43,13 @@
     return index, lax.bitwise_and(index, 1)
 
 
-def plane_to_rows(src, plane, dst, base):
-    width_y = src.shape[2]
+def plane_to_rows(sources, plane, dst, base):
+    bands, _, width_y, _ = sources[0].shape
     for y0 in range(0, width_y, 16):
-        for b in range(8):
-            dst[pl.ds(base + y0 * 8 + b, 16, stride=8), :] = src[b, plane, y0 : y0 + 16, :].astype(f32)
+        for i, source in enumerate(sources):
+            for b in range(bands):
+                part = source[b, plane, y0 : y0 + 16, :].astype(f32)
+                dst[pl.ds(base + y0 * 8 + i * bands + b, 16, stride=8), :] = part
 
 
 def at_row(ref, base):
@@ -65,33 +67,60 @@
     return total
 
 
-def measure(rows_ref, group, table, fields):
-    stacked = []
-    for field in fields:
-        for s in range(ATOM_DEV):
-            base = pl.multiple_of(rows_ref[group * ATOM_DEV + s] * 8, 8)
-            stacked.append(jnp.concatenate([field(base + k * 8) for k in range(8)], axis=1))
-    values = jnp.concatenate(stacked, axis=0).astype(bf16)
+def tile_values(rows_ref, group, field):
+    tiles = []
+    for s in range(ATOM_DEV):
+        base = pl.multiple_of(rows_ref[group * ATOM_DEV + s] * 8, 8)
+        tiles.append(jnp.concatenate([field(base + k * 8) for k in range(8)], axis=1))
+    return jnp.concatenate(tiles, axis=0)
+
+
+def z_gradient_values(rows_ref, group, grid_ref, offset, stencil):
+    rows = []
+    for s in range(ATOM_DEV):
+        base = pl.multiple_of(rows_ref[group * ATOM_DEV + s] * 8, 8)
+        rows.append(grid_ref[pl.ds(base + offset, 64), :])
+    values = jnp.concatenate(rows, axis=0).astype(bf16)
+    values = jnp.dot(values, stencil, preferred_element_type=f32) * (1.0 / 12.0)
+    tiles = []
+    for s in range(ATOM_DEV):
+        start = s * 64
+        tiles.append(
+            jnp.concatenate(
+                [values[start + k * 8 : start + k * 8 + 8, :] for k in range(8)], axis=1
+            )
+        )
+    return jnp.concatenate(tiles, axis=0)
+
+
+def contract(fields, table):
+    values = jnp.concatenate(fields, axis=0).astype(bf16)
     product = lax.dot_general(
         values, table, (((1,), (1,)), ((), ())), preferred_element_type=f32
     )
     return [diagonal_blocks(product, q) for q in range(len(fields))]
 
 
-def start_rows(rows_in, rows_ref, sem):
-    copy = pltpu.make_async_copy(rows_in, rows_ref, sem)
+def measure(rows_ref, group, table, field):
+    return contract([tile_values(rows_ref, group, field)], table)[0]
+
+
+def start_copy(source, target, sem):
+    copy = pltpu.make_async_copy(source, target, sem)
     copy.start()
     return copy
 
 
-def edge_kernel(wave_ref, to_a_ref, to_b_ref, sems):
+def edge_kernel(wave_ref, to_b_ref, *rest):
+    *to_a_refs, sems = rest
     planes = wave_ref.shape[1]
     _, odd = own_domain()
     upper = planes - PAD
-    copies = [
-        start_rows(wave_ref.at[:, pl.ds(upper * (1 - odd), PAD)], to_a_ref, sems.at[0]),
-        start_rows(wave_ref.at[:, pl.ds(upper * odd, PAD)], to_b_ref, sems.at[1]),
-    ]
+    copies = [start_copy(wave_ref.at[:, pl.ds(upper * odd, PAD)], to_b_ref, sems.at[0])]
+    for i, to_a_ref in enumerate(to_a_refs):
+        count = to_a_ref.shape[0]
+        source = wave_ref.at[pl.ds(i * count, count), pl.ds(upper * (1 - odd), PAD)]
+        copies.append(start_copy(source, to_a_ref, sems.at[1 + i]))
     for copy in copies:
         copy.wait()
 
@@ -101,7 +130,7 @@
     first_rows_hbm,
     wave_hbm,
     proj_hbm,
-    rows_out,
+    rows_ref,
     grid_ref,
     table_ref,
     margin_ref,
@@ -110,7 +139,6 @@
     wave_ref,
     atoms_ref,
     first_rows_ref,
-    rows_ref,
     entry_ref,
     proj_ref,
     proj_scr,
@@ -129,17 +157,18 @@
             wave_hbm.at[at_plane], wave_ref.at[at_plane], wave_sems.at[plane]
         )
 
-    atoms_copy = start_rows(atoms_hbm, atoms_ref, other_sems.at[0])
-    first_copy = start_rows(first_rows_hbm, first_rows_ref, other_sems.at[1])
+    atoms_copy = start_copy(atoms_hbm, atoms_ref, other_sems.at[0])
+    first_copy = start_copy(first_rows_hbm, first_rows_ref, other_sems.at[1])
     for plane in range(planes):
         plane_copy(plane).start()
-    proj_copy = start_rows(proj_hbm, proj_ref, other_sems.at[2])
+    proj_copy = start_copy(proj_hbm, proj_ref, other_sems.at[2])
     proj_scr[:, ATOM_DEV * 8 :, :] = jnp.zeros(
         (GROUPS, LANES - ATOM_DEV * 8, proj_scr.shape[2]), f32
     )
     atoms_copy.wait()
     first_copy.wait()
-    for entry in range(entry_count):
+
+    def place(entry):
         atom = atoms_ref[entry]
         owner = lax.shift_right_logical(atom * 171, 11)
         above = lax.rem(owner - index + 1 + domain_count, domain_count)
@@ -147,11 +176,13 @@
         slot = group * ATOM_DEV + atom - owner * ATOM_DEV
         entry_ref[slot] = entry
         rows_ref[slot] = first_rows_ref[entry]
-    rows_copy = start_rows(rows_ref, rows_out, other_sems.at[3])
+
+    for entry in range(entry_count):
+        place(entry)
 
     def one_plane(plane, carry):
         plane_copy(plane).wait()
-        plane_to_rows(wave_ref, plane, grid_ref, (plane + PAD) * width_y * 8)
+        plane_to_rows([wave_ref], plane, grid_ref, (plane + PAD) * width_y * 8)
         return carry
 
     lax.fori_loop(0, planes, one_plane, 0)
@@ -162,11 +193,8 @@
             proj_scr[group, s * 8 : s * 8 + 8, :] = proj_ref[entry].astype(f32)
         table = proj_scr[group].astype(bf16)
         table_ref[group] = table
-        (sums,) = measure(
-            rows_ref,
-            group,
-            table,
-            [lambda base: at_row(grid_ref, base + PAD * width_y * 8)],
+        sums = measure(
+            rows_ref, group, table, lambda base: at_row(grid_ref, base + PAD * width_y * 8)
         )
         margin_ref[group] = sums
         if group < 2:
@@ -174,17 +202,12 @@
         else:
             to_c_ref[...] = jnp.zeros(to_c_ref.shape, f32)
             to_c_ref[0] = sums
-    rows_copy.wait()
 
 
 def forward_kernel(margin_ref, from_a_ref, to_b_ref):
     to_b_ref[0] = margin_ref[2]
     to_b_ref[1] = margin_ref[1] + from_a_ref[0]
     to_b_ref[2:] = jnp.zeros((to_b_ref.shape[0] - 2, 8, LANES), f32)
-
-
-def third_shift(center, offset):
-    return pltpu.roll(center, (-offset) % center.shape[-1], 1)
 
 
 def circulant(near, far, center, length):
@@ -196,10 +219,21 @@
     return jnp.where(distance == 0, center, table).astype(bf16)
 
 
+def first_circulant(length):
+    row = lax.broadcasted_iota(jnp.int32, (length, length), 0)
+    column = lax.broadcasted_iota(jnp.int32, (length, length), 1)
+    distance = lax.bitwise_and(row - column, length - 1)
+    table = jnp.zeros((length, length), f32)
+    for offset, factor in ((1, 8.0), (2, -1.0), (length - 1, -8.0), (length - 2, 1.0)):
+        table = jnp.where(distance == offset, factor, table)
+    return table.astype(bf16)
+
+
 def gradient_kernel(
-    rows_in,
+    rows_ref,
     grid_in,
-    halo_a_ref,
+    halo_a0_ref,
+    halo_a1_ref,
     table_ref,
     coupling_hbm,
     weight_hbm,
@@ -209,16 +243,14 @@
     mixing_ref,
     factor_ref,
     y_ref,
-    rows_ref,
     coupling_ref,
     weight_ref,
     sems,
 ):
     del grid_in
     copies = [
-        start_rows(rows_in, rows_ref, sems.at[0]),
-        start_rows(coupling_hbm, coupling_ref, sems.at[1]),
-        start_rows(weight_hbm, weight_ref, sems.at[2]),
+        start_copy(coupling_hbm, coupling_ref, sems.at[0]),
+        start_copy(weight_hbm, weight_ref, sems.at[1]),
     ]
     width_y = LANES
     edge = PAD * width_y * 8
@@ -236,24 +268,22 @@
 
     lax.fori_loop(0, planes, one_plane, 0)
 
-    def along_y(base):
-        return at_row(y_ref, base)
-
-    def along_z(base):
-        center = at_row(grid_ref, base + edge)
-        near = third_shift(center, 1) - third_shift(center, -1)
-        far = third_shift(center, 2) - third_shift(center, -2)
-        return (2.0 / 3.0) * near - (1.0 / 12.0) * far
-
     _, odd = own_domain()
     for i in range(PAD):
         plane = i + (planes + PAD) * (1 - odd)
-        plane_to_rows(halo_a_ref, i, grid_ref, plane * width_y * 8)
+        plane_to_rows([halo_a0_ref, halo_a1_ref], i, grid_ref, plane * width_y * 8)
 
     for copy in copies:
         copy.wait()
+    stencil = first_circulant(width_y)
     for group in range(GROUPS):
-        second, third = measure(rows_ref, group, table_ref[group], [along_y, along_z])
+        second, third = contract(
+            [
+                tile_values(rows_ref, group, lambda base: at_row(y_ref, base)),
+                z_gradient_values(rows_ref, group, grid_ref, edge, stencil),
+            ],
+            table_ref[group],
+        )
         margin_ref[0, group] = second
         margin_ref[1, group] = third
 
@@ -287,40 +317,25 @@
 
 
 def first_kernel(
-    rows_in,
+    rows_ref,
     grid_in,
     halo_b_ref,
     table_ref,
     yz_ref,
     grid_ref,
     force_ref,
-    rows_ref,
-    rows_sem,
 ):
     del grid_in
-    rows_copy = start_rows(rows_in, rows_ref, rows_sem)
     width_y = halo_b_ref.shape[2]
     hop = width_y * 8
     planes = grid_ref.shape[0] // hop - 2 * PAD
     _, odd = own_domain()
 
     for i in range(PAD):
-        plane_to_rows(halo_b_ref, i, grid_ref, (i + (planes + PAD) * odd) * hop)
-    rows_copy.wait()
-    (force_ref[0],) = measure(rows_ref, 0, table_ref[0], [along_x(grid_ref, hop)])
+        plane_to_rows([halo_b_ref], i, grid_ref, (i + (planes + PAD) * odd) * hop)
+    force_ref[0] = measure(rows_ref, 0, table_ref[0], along_x(grid_ref, hop))
     for k in range(2):
         force_ref[1 + k] = yz_ref[k, 0]
-
-
-def rest_kernel(rows_in, grid_ref, table_ref, yz_ref, _, force_ref, rows_ref, rows_sem):
-    rows_copy = start_rows(rows_in, rows_ref, rows_sem)
-    rows_copy.wait()
-    for group in range(1, GROUPS):
-        (force_ref[group - 1, 0],) = measure(
-            rows_ref, group, table_ref[group], [along_x(grid_ref, LANES * 8)]
-        )
-        for k in range(2):
-            force_ref[group - 1, 1 + k] = yz_ref[k, group]
 
 
 def pieces(x, count):
@@ -332,18 +347,26 @@
     return out
 
 
-def combine_kernel(
+def rest_kernel(
+    rows_ref,
+    grid_ref,
+    table_ref,
+    yz_ref,
     margin_ref,
     from_a_ref,
     from_b_ref,
     from_c_ref,
     mixing_ref,
     factor_ref,
-    force_ref,
-    force_from_a_ref,
+    _,
     scaled_ref,
-    copies_ref,
+    weighted_ref,
+    parts_ref,
 ):
+    forces = []
+    for group in range(1, GROUPS):
+        first = measure(rows_ref, group, table_ref[group], along_x(grid_ref, LANES * 8))
+        forces.append([first, yz_ref[0, group], yz_ref[1, group]])
     totals = jnp.concatenate(
         [
             margin_ref[0] + from_a_ref[1] + from_c_ref[0],
@@ -361,19 +384,26 @@
         for mixing in pieces(mixing_ref[...], 2)
     ]
     scaled = mixed[0][:count] + (mixed[0][count:] + mixed[1][:count])
-    parts = []
     for group in range(GROUPS):
-        one = scaled[group * 8 : group * 8 + 8]
-        scaled_ref[group] = one
-        if group == 0:
-            continue
-        weighted = factor_ref[...] * one
-        for k in range(3):
-            force = force_ref[group - 1, k]
-            if group == 1:
-                force = force + force_from_a_ref[k]
-            parts.append(jnp.sum(force * weighted, axis=0, keepdims=True))
-    summed = jnp.concatenate(parts, axis=0)
+        scaled_ref[group] = scaled[group * 8 : group * 8 + 8]
+    weighted = [factor_ref[...] * scaled[group * 8 : group * 8 + 8] for group in (1, 2)]
+    weighted_ref[...] = weighted[0]
+    parts_ref[...] = jnp.concatenate(
+        [
+            jnp.sum(force * weight, axis=0, keepdims=True)
+            for weight, force_group in zip(weighted, forces)
+            for force in force_group
+        ]
+        + [jnp.zeros((2, LANES), f32)],
+        axis=0,
+    )
+
+
+def combine_kernel(parts_ref, weighted_ref, force_from_a_ref, copies_ref):
+    from_a = [
+        jnp.sum(force_from_a_ref[k] * weighted_ref[...], axis=0, keepdims=True) for k in range(3)
+    ]
+    summed = parts_ref[...] + jnp.concatenate(from_a + [jnp.zeros((5, LANES), f32)], axis=0)
     for step in (1, 2, 4):
         summed = summed + pltpu.roll(summed, LANES - step, 1)
     component = lax.bitwise_and(lax.broadcasted_iota(jnp.int32, (1, LANES), 1), 7)
@@ -407,10 +437,11 @@
 
 
 def apply_kernel(
-    rows_in,
+    rows_ref,
     wave_hbm,
     pot_hbm,
-    halo_a_ref,
+    halo_a0_ref,
+    halo_a1_ref,
     halo_b_ref,
     table_ref,
     scaled_ref,
@@ -419,7 +450,6 @@
     add_ref,
     wave_ref,
     pot_ref,
-    rows_ref,
     sems,
     edge_sems,
 ):
@@ -439,13 +469,21 @@
             out_ref.at[at_plane], out_hbm.at[at_plane], sems.at[1, plane]
         )
 
-    rows_copy = start_rows(rows_in, rows_ref, edge_sems.at[0])
     _, odd = own_domain()
     far_end = planes + PAD
     edge_copies = [
-        start_rows(halo_a_ref, wave_ref.at[:, pl.ds(far_end * (1 - odd), PAD)], edge_sems.at[1]),
-        start_rows(halo_b_ref, wave_ref.at[:, pl.ds(far_end * odd, PAD)], edge_sems.at[2]),
-        start_rows(pot_hbm, pot_ref, edge_sems.at[3]),
+        start_copy(
+            halo_a0_ref,
+            wave_ref.at[pl.ds(0, bands // 2), pl.ds(far_end * (1 - odd), PAD)],
+            edge_sems.at[1],
+        ),
+        start_copy(
+            halo_a1_ref,
+            wave_ref.at[pl.ds(bands // 2, bands // 2), pl.ds(far_end * (1 - odd), PAD)],
+            edge_sems.at[0],
+        ),
+        start_copy(halo_b_ref, wave_ref.at[:, pl.ds(far_end * odd, PAD)], edge_sems.at[2]),
+        start_copy(pot_hbm, pot_ref, edge_sems.at[3]),
     ]
     for plane in range(planes):
         wave_copy(plane).start()
@@ -456,7 +494,6 @@
         return carry
 
     lax.fori_loop(0, planes, clear, 0)
-    rows_copy.wait()
 
     for group in range(GROUPS):
         scaled = scaled_ref[group]
@@ -514,6 +551,14 @@
 MIB = 2**20
 
 
+def out_type(shape, dtype, spec):
+    if spec is HBM:
+        return pltpu.HBM(shape, dtype)
+    if spec is SMEM:
+        return pltpu.SMEM(shape, dtype)
+    return jax.ShapeDtypeStruct(shape, dtype)
+
+
 def in_hbm(x):
     return pltpu.with_memory_space_constraint(x, pltpu.HBM)
 
@@ -522,7 +567,7 @@
     return pl.pallas_call(
         kernel,
         out_shape=tuple(
-            pltpu.HBM(shape, dtype) if spec is HBM else jax.ShapeDtypeStruct(shape, dtype)
+            out_type(shape, dtype, spec)
             for (shape, dtype), spec in zip(outs, out_specs)
         ),
         in_specs=ins,
@@ -551,16 +596,17 @@
     slots = ((entry_count,), jnp.int32)
     slots_smem = pltpu.SMEM((entry_count,), jnp.int32)
 
-    to_a, to_b = call(
+    half_edge = ((band_count // 2, PAD, width_y, width_z), bf16)
+    to_b, *to_a = call(
         edge_kernel,
         "edges",
-        [edge, edge],
+        [edge, half_edge, half_edge],
         [HBM],
-        [VMEM, VMEM],
-        [pltpu.SemaphoreType.DMA((2,))],
+        [VMEM] * 3,
+        [pltpu.SemaphoreType.DMA((3,))],
     )(in_hbm(wavefunctions))
     halo_b = swap_b(to_b)
-    halo_a = swap_a(to_a)
+    halo_a = [swap_a(part) for part in to_a]
 
     rows, grid, table, margins, margins_to_a, margins_to_c = call(
         functools.partial(relayout_kernel, domain_count=domain_count),
@@ -574,20 +620,20 @@
             ((6, 8, LANES), f32),
         ],
         [HBM] * 4,
-        [ANY] + [VMEM] * 5,
+        [SMEM] + [VMEM] * 5,
         [
             pltpu.VMEM(wavefunctions.shape, bf16),
-            slots_smem,
             slots_smem,
             slots_smem,
             slots_smem,
             pltpu.VMEM(projectors.shape, bf16),
             pltpu.VMEM((GROUPS, LANES, tile_len), f32),
             pltpu.SemaphoreType.DMA((plane_count,)),
-            pltpu.SemaphoreType.DMA((4,)),
+            pltpu.SemaphoreType.DMA((3,)),
         ],
     )(*map(in_hbm, (margin_atoms, tile_rows, wavefunctions, projectors)))
 
+    rows = pltpu.with_memory_space_constraint(rows, pltpu.SMEM)
     from_a = swap_a(margins_to_a)
     (margins_to_b,) = call(forward_kernel, "forward", [((4, 8, LANES), f32)], [VMEM] * 2, [VMEM], limit=2)(
         margins, from_a
@@ -604,20 +650,19 @@
             ((LANES, LANES), f32),
             block,
         ],
-        [ANY] + [VMEM] * 3 + [HBM] * 2 + [VMEM],
+        [SMEM] + [VMEM] * 4 + [HBM] * 2 + [VMEM],
         [VMEM] * 4,
         [
             pltpu.VMEM((plane_count * width_y * 8, LANES), f32),
-            slots_smem,
             pltpu.VMEM(coupling.shape, f32),
             pltpu.VMEM((1, band_count), f32),
-            pltpu.SemaphoreType.DMA((3,)),
+            pltpu.SemaphoreType.DMA((2,)),
         ],
         input_output_aliases={1: 0},
     )(
         rows,
         grid,
-        halo_a,
+        *halo_a,
         table,
         in_hbm(coupling),
         in_hbm(band_weights[None, :]),
@@ -628,34 +673,44 @@
         first_kernel,
         "first",
         [((grid_rows, LANES), f32), blocks],
-        [ANY] + [VMEM] * 4,
+        [SMEM] + [VMEM] * 4,
         [VMEM] * 2,
-        [slots_smem, pltpu.SemaphoreType.DMA],
         input_output_aliases={1: 0},
     )(rows, grid, halo_b, table, yz_margins)
     force_from_a = swap_a(force_to_a)
-    (force_margins,) = call(
+    scaled, weighted, parts = call(
         rest_kernel,
         "rest",
-        [((2, 3, 8, LANES), f32)],
-        [ANY] + [VMEM] * 4,
-        [VMEM],
-        [slots_smem, pltpu.SemaphoreType.DMA],
-    )(rows, grid, table, yz_margins, force_to_a)
+        [blocks, block, block],
+        [SMEM] + [VMEM] * 10,
+        [VMEM] * 3,
+    )(
+        rows,
+        grid,
+        table,
+        yz_margins,
+        margins,
+        from_a,
+        from_b,
+        from_c,
+        mixing,
+        factor,
+        force_to_a,
+    )
 
     bands = lax.axis_size("band")
     pairs = [
         [dom * bands + band for dom in (i, partner_b(i, domain_count)) for band in range(bands)]
         for i in range(1, domain_count, 2)
     ]
-    scaled, copies = call(
+    (copies,) = call(
         combine_kernel,
         "combine",
-        [blocks, ((2 * bands // 8, 8, LANES), f32)],
-        [VMEM] * 8,
-        [VMEM] * 2,
+        [((2 * bands // 8, 8, LANES), f32)],
+        [VMEM] * 3,
+        [VMEM],
         limit=2,
-    )(margins, from_a, from_b, from_c, mixing, factor, force_margins, force_from_a)
+    )(parts, weighted, force_from_a)
     gathered = lax.all_to_all(
         copies.reshape(2 * bands, 1, LANES), ("dom", "band"), 0, 0, axis_index_groups=pairs
     )
@@ -664,19 +719,18 @@
         apply_kernel,
         "apply",
         [(wavefunctions.shape, bf16)],
-        [ANY, HBM, HBM] + [VMEM] * 4,
+        [SMEM, HBM, HBM] + [VMEM] * 5,
         [HBM],
         [
             pltpu.VMEM(wavefunctions.shape, bf16),
             pltpu.VMEM((plane_count * width_y * 8, LANES), f32),
             pltpu.VMEM((band_count, plane_count + 2 * PAD, width_y, width_z), bf16),
             pltpu.VMEM(potential.shape, f32),
-            slots_smem,
             pltpu.SemaphoreType.DMA((2, plane_count)),
             pltpu.SemaphoreType.DMA((4,)),
         ],
         limit=16,
-    )(rows, in_hbm(wavefunctions), in_hbm(potential), halo_a, halo_b, table, scaled)
+    )(rows, in_hbm(wavefunctions), in_hbm(potential), *halo_a, halo_b, table, scaled)
 
     (forces,) = call(
         total_kernel, "total", [((3, ATOM_DEV), f32)], [VMEM], [VMEM], limit=2

time: 34.4 us -> 33 us (0.959)
  Pallas kernels: 15.2 us -> 13.5 us
  waiting for transfers between devices: 1.74 us -> 2.11 us
    pallas_call x5, Pallas kernels: 9.79 us -> 8.71 us  [the longest x1 5.72 us: per_device(): call(apply_kernel, 'apply', [(wavefunctions.shape, bf16)], [SMEM, HBM, HB...]
    pallas_call x1, Pallas kernels: 2.41 us -> 1.75 us  [per_device(): call(gradient_kernel, 'gradient', [((grid_rows, LANES), f32), ((2, GROUPS...]
    ppermute x2, starting transfers between devices: 4.85 us -> 4.26 us  [swap_b(): lax.ppermute(x, 'dom', [(i, partner_b(i, count)) for i in range(count)])]
    ppermute x3 -> x4, starting transfers between devices: 0.26 us -> 0.69 us  [swap_a(): lax.ppermute(x, 'dom', [(i, partner_a(i)) for i in range(lax.axis_size('d...]
  transfers between devices with their start and end apart: 7 -> 8, of which waited for: 3 -> 4; matrix products, arithmetic and copies ran while one was open for 0% -> 0% of each run, Pallas kernels for 36% -> 32%
where the time goes in v6:
time: 33 us; the launch traced here: 32.8 us
  starting transfers between devices  16.5 us (50%)
  Pallas kernels  13.5 us (41%)
  waiting for transfers between devices  2.11 us (6%)
  between operations  0.71 us (2%)
    all_to_all x1, starting transfers between devices, per_device(): lax.all_to_all(copies.reshape(2 * bands, 1, LANES), ('dom', 'band'), 0, 0...  10.5 us
    pallas_call x1, Pallas kernels, per_device(): call(apply_kernel, 'apply', [(wavefunctions.shape, bf16)], [SMEM, HBM, HB...  5.72 us
    ppermute x2, starting transfers between devices, swap_b(): lax.ppermute(x, 'dom', [(i, partner_b(i, count)) for i in range(count)])  4.26 us
    pallas_call x1, Pallas kernels, per_device(): call(functools.partial(relayout_kernel, domain_count=domain_count), 'rela...  2.25 us
    pallas_call x1, Pallas kernels, per_device(): call(gradient_kernel, 'gradient', [((grid_rows, LANES), f32), ((2, GROUPS...  1.75 us
    all_to_all x1, waiting for transfers between devices, per_device(): lax.all_to_all(copies.reshape(2 * bands, 1, LANES), ('dom', 'band'), 0, 0...  1.31 us
    pallas_call x1, Pallas kernels, per_device(): call(edge_kernel, 'edges', [edge, half_edge, half_edge], [HBM], [VMEM] *...  1.22 us
    ppermute x1, starting transfers between devices, send_c(): lax.ppermute(x, 'dom', [(i, partner_a(partner_b(i, count))) for i in rang...  1.06 us
  transfers between devices with their start and end apart: 8, of which 4 were waited for; matrix products, arithmetic and copies ran while one was open for 0% of the time, Pallas kernels for 32%

profile of v6, /device:TPU:0, one launch (start us, length us, event | category | flops | bytes accessed | tf_op | source)
XLA Modules:
  0.0 32.8 jit_solution(4733822707319591601)
XLA Ops:
  0.6 1.2 %edges.1 = (bf16[8,2,128,128]{3,2,1,0:T(8,128)(2,1)S(1)}, bf16[4,2,128,128]{3,2,1,0:T(8,128)(2,1)S(1)}, bf16[4,2,128,128]{3,2,1,0:T(8,128)(2,1)S(1)}) custom-call(bf16[8,8,128,128]{3,2,1,0:T(8,128)(2,1)} %wave_hbm.3), custom_call_target="tpu_custom_call" | custom-call | flops 1000 | bytes 1000 | tf_op jit(solution)/shard_map/edges/pallas_call | solution.py:600
  1.9 2.4 %collective-permute-start.2 = (bf16[8,2,128,128]{3,2,1,0:T(8,128)(2,1)S(1)}, bf16[8,2,128,128]{3,2,1,0:T(8,128)(2,1)S(1)}, u32[]{:S(2)}, u32[]{:S(2)}) collective-permute-start(bf16[8,2,128,128]{3,2,1,0:T(8,128)(2,1)S(1)} %get-tuple-element.23), channel_id=1, source_target_pairs={{0,112},{16,32},{32,16},{48,64},{64,48},{80,96},{96,80},{112,0},{1... | collective-permute-start | bytes 1572872 | tf_op jit(solution)/shard_map/ppermute | solution.py:33
  4.2 0.0 collective-permute-start
  4.2 0.5 %collective-permute-start.1 = (bf16[4,2,128,128]{3,2,1,0:T(8,128)(2,1)S(1)}, bf16[4,2,128,128]{3,2,1,0:T(8,128)(2,1)S(1)}, u32[]{:S(2)}, u32[]{:S(2)}) collective-permute-start(bf16[4,2,128,128]{3,2,1,0:T(8,128)(2,1)S(1)} %get-tuple-element.22), channel_id=1, source_target_pairs={{0,16},{16,0},{32,48},{48,32},{64,80},{80,64},{96,112},{112,96},{1... | collective-permute-start | bytes 786440 | tf_op jit(solution)/shard_map/ppermute | solution.py:28
  4.7 2.2 %relayout.1 = (s32[36]{0:T(128)S(4)}, f32[12288,128]{1,0:T(8,128)S(1)}, bf16[3,128,1024]{2,1,0:T(8,128)(2,1)S(1)}, f32[3,8,128]{2,1,0:T(8,128)S(1)}, f32[2,8,128]{2,1,0:T(8,128)S(1)}, /*index=5*/f32[6,8,128]{2,1,0:T(8,128)S(1)}) custom-call(s32[36]{0:T(128)} %atoms_hbm.1, s32[36]{0:T(128)} %first_rows_hbm.1, bf16[8,8,128,128]{3,2,1,0:T(8,128)(2,1)} %wave_hbm.3, ...), custom_call_target="tpu_custom_call" | custom-call | flops 1000 | bytes 1000 | tf_op jit(solution)/shard_map/relayout/pallas_call | solution.py:611
  7.0 0.1 collective-permute-start.3
  7.1 1.1 %collective-permute-start.5 = (f32[6,8,128]{2,1,0:T(8,128)S(1)}, f32[6,8,128]{2,1,0:T(8,128)S(1)}, u32[]{:S(2)}, u32[]{:S(2)}) collective-permute-start(f32[6,8,128]{2,1,0:T(8,128)S(1)} %get-tuple-element.31), channel_id=1, source_target_pairs={{0,96},{16,48},{32,0},{48,80},{64,32},{80,112},{96,64},{112,16},{1... | collective-permute-start | bytes 73736 | tf_op jit(solution)/shard_map/ppermute | solution.py:38
  8.1 0.1 collective-permute-done.3.from_a_ref
  8.2 1.9 %collective-permute-start.4 = (f32[4,8,128]{2,1,0:T(8,128)S(1)}, f32[4,8,128]{2,1,0:T(8,128)S(1)}, u32[]{:S(2)}, u32[]{:S(2)}) collective-permute-start(f32[4,8,128]{2,1,0:T(8,128)S(1)} %forward.1._), channel_id=1, source_target_pairs={{0,112},{16,32},{32,16},{48,64},{64,48},{80,96},{96,80},{112,0},{1... | collective-permute-start | bytes 49160 | tf_op jit(solution)/shard_map/ppermute | solution.py:33
  10.2 0.0 collective-permute-done.halo_a0_ref
  10.2 0.0 collective-permute-done.1.halo_a1_ref
  10.2 1.8 %gradient.1 = (f32[12288,128]{1,0:T(8,128)S(1)}, f32[2,3,8,128]{3,2,1,0:T(8,128)S(1)}, f32[128,128]{1,0:T(8,128)S(1)}, f32[8,128]{1,0:T(8,128)S(1)}) custom-call(s32[36]{0:T(128)S(4)} %get-tuple-element.20.rows_ref, f32[12288,128]{1,0:T(8,128)S(1)} %get-tuple-element.25.grid_in, ...), custom_call_target="tpu_custom_call", output_to_operand_aliasing={{0}: (1, {})} | custom-call | flops 1000 | bytes 1000 | tf_op jit(solution)/shard_map/gradient/pallas_call | solution.py:644
  11.9 0.0 collective-permute-done.2.halo_b_ref
  11.9 0.4 %first.1 = (f32[12288,128]{1,0:T(8,128)S(1)}, f32[3,8,128]{2,1,0:T(8,128)S(1)}) custom-call(s32[36]{0:T(128)S(4)} %get-tuple-element.20.rows_ref, f32[12288,128]{1,0:T(8,128)S(1)} %get-tuple-element.28.grid_in, bf16[8,2,128,128]{3,2,1,0:T(8,128)(2,1)S(1)} %collective-permute-done.2.halo_b_ref, ...), custom_call_target="tpu_custom_call", output_to_operand_aliasing={{0}: (1, {})} | custom-call | flops 1000 | bytes 1000 | tf_op jit(solution)/shard_map/first/pallas_call | solution.py:672
  12.3 0.1 collective-permute-start.6
  12.4 0.2 collective-permute-done.4.from_b_ref
  12.6 0.0 collective-permute-done.5.from_c_ref
  12.6 0.5 %rest.1 = (f32[3,8,128]{2,1,0:T(8,128)S(1)}, f32[8,128]{1,0:T(8,128)S(1)}, f32[8,128]{1,0:T(8,128)S(1)}) custom-call(s32[36]{0:T(128)S(4)} %get-tuple-element.20.rows_ref, f32[12288,128]{1,0:T(8,128)S(1)} %get-tuple-element.30.grid_ref, bf16[3,128,1024]{2,1,0:T(8,128)(2,1)S(1)} %get-tuple-element.24.table_ref, ...), custom_call_target="tpu_custom_call" | custom-call | flops 1000 | bytes 1000 | tf_op jit(solution)/shard_map/rest/pallas_call | solution.py:681
  13.1 0.5 %collective-permute-done.6.force_from_a_ref = f32[3,8,128]{2,1,0:T(8,128)S(1)} collective-permute-done((f32[3,8,128]{2,1,0:T(8,128)S(1)}, f32[3,8,128]{2,1,0:T(8,128)S(1)}, u32[]{:S(2)}, u32[]{:S(2)}) %collective-permute-start.6) | collective-permute-done | bytes 12320 | tf_op jit(solution)/shard_map/ppermute | solution.py:28
  13.6 0.9 %combine.1 = f32[4,8,128]{2,1,0:T(8,128)} custom-call(f32[8,128]{1,0:T(8,128)S(1)} %get-tuple-element.36.parts_ref, f32[8,128]{1,0:T(8,128)S(1)} %get-tuple-element.37.weighted_ref, f32[3,8,128]{2,1,0:T(8,128)S(1)} %collective-permute-done.6.force_from_a_ref), custom_call_target="tpu_custom_call" | custom-call | flops 1000 | bytes 1000 | tf_op jit(solution)/shard_map/combine/pallas_call | solution.py:706
  14.5 10.5 %all-to-all-start = ((f32[32,1,128]{2,1,0:T(1,128)}), f32[32,1,128]{2,1,0:T(1,128)S(1)}, u32[]{:S(2)}, u32[]{:S(2)}) async-start(f32[32,1,128]{2,1,0:T(1,128)} %bitcast.2), calls=%async_computation | async-start | bytes 32768 | tf_op jit(solution)/shard_map/all_to_all | solution.py:714
  25.0 5.7 %apply.1 = bf16[8,8,128,128]{3,2,1,0:T(8,128)(2,1)} custom-call(s32[36]{0:T(128)S(4)} %get-tuple-element.20.rows_ref, bf16[8,8,128,128]{3,2,1,0:T(8,128)(2,1)} %wave_hbm.3, f32[8,128,128]{2,1,0:T(8,128)} %pot_hbm.1, bf16[4,2,128,128]{3,2,1,0:T(8,128)(2,1)S(1)} %collective-permute-done.halo_a0_ref, ...), custom_call_target="tpu_custom_call" | custom-call | flops 1000 | bytes 1000 | tf_op jit(solution)/shard_map/apply/pallas_call | solution.py:718
  30.7 1.3 %all-to-all-done = f32[32,1,128]{2,1,0:T(1,128)S(1)} async-done(((f32[32,1,128]{2,1,0:T(1,128)}), f32[32,1,128]{2,1,0:T(1,128)S(1)}, u32[]{:S(2)}, u32[]{:S(2)}) %all-to-all-start) | async-done | bytes 16416 | tf_op jit(solution)/shard_map/all_to_all | solution.py:714
  32.0 0.7 %total.1 = f32[3,12]{1,0:T(4,128)} custom-call(f32[4,8,128]{2,1,0:T(8,128)S(1)} %bitcast.5), custom_call_target="tpu_custom_call" | custom-call | flops 1000 | bytes 1000 | tf_op jit(solution)/shard_map/total/pallas_call | solution.py:735
  (1 shorter events, 0.0 us)
Async XLA Ops:
  1.9 10.1 %collective-permute-start.2 = (bf16[8,2,128,128]{3,2,1,0:T(8,128)(2,1)S(1)}, bf16[8,2,128,128]{3,2,1,0:T(8,128)(2,1)S(1)}, u32[]{:S(2)}, u32[]{:S(2)}) collective-permute-start(bf16[8,2,128,128]{3,2,1,0:T(8,128)(2,1)S(1)} %get-tuple-element.23), channel_id=1, source_target_pairs={{0,112},{16,32},{32,16},{48,64},{64,48},{80,96},{96,80},{112,0},{1... | collective-permute-start | bytes 1572872 | tf_op jit(solution)/shard_map/ppermute | solution.py:33
  4.2 5.9 %collective-permute-start = (bf16[4,2,128,128]{3,2,1,0:T(8,128)(2,1)S(1)}, bf16[4,2,128,128]{3,2,1,0:T(8,128)(2,1)S(1)}, u32[]{:S(2)}, u32[]{:S(2)}) collective-permute-start(bf16[4,2,128,128]{3,2,1,0:T(8,128)(2,1)S(1)} %get-tuple-element.21), channel_id=1, source_target_pairs={{0,16},{16,0},{32,48},{48,32},{64,80},{80,64},{96,112},{112,96},{1... | collective-permute-start | bytes 786440 | tf_op jit(solution)/shard_map/ppermute | solution.py:28
  4.2 5.9 %collective-permute-start.1 = (bf16[4,2,128,128]{3,2,1,0:T(8,128)(2,1)S(1)}, bf16[4,2,128,128]{3,2,1,0:T(8,128)(2,1)S(1)}, u32[]{:S(2)}, u32[]{:S(2)}) collective-permute-start(bf16[4,2,128,128]{3,2,1,0:T(8,128)(2,1)S(1)} %get-tuple-element.22), channel_id=1, source_target_pairs={{0,16},{16,0},{32,48},{48,32},{64,80},{80,64},{96,112},{112,96},{1... | collective-permute-start | bytes 786440 | tf_op jit(solution)/shard_map/ppermute | solution.py:28
  7.0 1.3 %collective-permute-start.3 = (f32[2,8,128]{2,1,0:T(8,128)S(1)}, f32[2,8,128]{2,1,0:T(8,128)S(1)}, u32[]{:S(2)}, u32[]{:S(2)}) collective-permute-start(f32[2,8,128]{2,1,0:T(8,128)S(1)} %get-tuple-element.27), channel_id=1, source_target_pairs={{0,16},{16,0},{32,48},{48,32},{64,80},{80,64},{96,112},{112,96},{1... | collective-permute-start | bytes 24584 | tf_op jit(solution)/shard_map/ppermute | solution.py:28
  7.1 5.5 %collective-permute-start.5 = (f32[6,8,128]{2,1,0:T(8,128)S(1)}, f32[6,8,128]{2,1,0:T(8,128)S(1)}, u32[]{:S(2)}, u32[]{:S(2)}) collective-permute-start(f32[6,8,128]{2,1,0:T(8,128)S(1)} %get-tuple-element.31), channel_id=1, source_target_pairs={{0,96},{16,48},{32,0},{48,80},{64,32},{80,112},{96,64},{112,16},{1... | collective-permute-start | bytes 73736 | tf_op jit(solution)/shard_map/ppermute | solution.py:38
  8.2 4.4 %collective-permute-start.4 = (f32[4,8,128]{2,1,0:T(8,128)S(1)}, f32[4,8,128]{2,1,0:T(8,128)S(1)}, u32[]{:S(2)}, u32[]{:S(2)}) collective-permute-start(f32[4,8,128]{2,1,0:T(8,128)S(1)} %forward.1._), channel_id=1, source_target_pairs={{0,112},{16,32},{32,16},{48,64},{64,48},{80,96},{96,80},{112,0},{1... | collective-permute-start | bytes 49160 | tf_op jit(solution)/shard_map/ppermute | solution.py:33
  12.3 1.3 %collective-permute-start.6 = (f32[3,8,128]{2,1,0:T(8,128)S(1)}, f32[3,8,128]{2,1,0:T(8,128)S(1)}, u32[]{:S(2)}, u32[]{:S(2)}) collective-permute-start(f32[3,8,128]{2,1,0:T(8,128)S(1)} %get-tuple-element.34._), channel_id=1, source_target_pairs={{0,16},{16,0},{32,48},{48,32},{64,80},{80,64},{96,112},{112,96},{1... | collective-permute-start | bytes 36872 | tf_op jit(solution)/shard_map/ppermute | solution.py:28
  14.5 17.5 %all-to-all-start = ((f32[32,1,128]{2,1,0:T(1,128)}), f32[32,1,128]{2,1,0:T(1,128)S(1)}, u32[]{:S(2)}, u32[]{:S(2)}) async-start(f32[32,1,128]{2,1,0:T(1,128)} %bitcast.2), calls=%async_computation | async-start | bytes 32768 | tf_op jit(solution)/shard_map/all_to_all | solution.py:714

commit v7 on v6

--- a/solution.py
+++ b/solution.py
@@ -111,18 +111,10 @@
     return copy
 
 
-def edge_kernel(wave_ref, to_b_ref, *rest):
-    *to_a_refs, sems = rest
-    planes = wave_ref.shape[1]
+def edge_kernel(wave_hbm, to_b_ref, sem):
+    planes = wave_hbm.shape[1]
     _, odd = own_domain()
-    upper = planes - PAD
-    copies = [start_copy(wave_ref.at[:, pl.ds(upper * odd, PAD)], to_b_ref, sems.at[0])]
-    for i, to_a_ref in enumerate(to_a_refs):
-        count = to_a_ref.shape[0]
-        source = wave_ref.at[pl.ds(i * count, count), pl.ds(upper * (1 - odd), PAD)]
-        copies.append(start_copy(source, to_a_ref, sems.at[1 + i]))
-    for copy in copies:
-        copy.wait()
+    start_copy(wave_hbm.at[:, pl.ds((planes - PAD) * odd, PAD)], to_b_ref, sem).wait()
 
 
 def relayout_kernel(
@@ -130,12 +122,15 @@
     first_rows_hbm,
     wave_hbm,
     proj_hbm,
+    _,
     rows_ref,
     grid_ref,
     table_ref,
     margin_ref,
     to_a_ref,
     to_c_ref,
+    edge_a0_ref,
+    edge_a1_ref,
     wave_ref,
     atoms_ref,
     first_rows_ref,
@@ -162,6 +157,11 @@
     for plane in range(planes):
         plane_copy(plane).start()
     proj_copy = start_copy(proj_hbm, proj_ref, other_sems.at[2])
+    edge_copies = []
+    for i, edge_ref in enumerate((edge_a0_ref, edge_a1_ref)):
+        count = edge_ref.shape[0]
+        source = wave_hbm.at[pl.ds(i * count, count), pl.ds((planes - PAD) * (1 - odd), PAD)]
+        edge_copies.append(start_copy(source, edge_ref, other_sems.at[3 + i]))
     proj_scr[:, ATOM_DEV * 8 :, :] = jnp.zeros(
         (GROUPS, LANES - ATOM_DEV * 8, proj_scr.shape[2]), f32
     )
@@ -202,6 +202,8 @@
         else:
             to_c_ref[...] = jnp.zeros(to_c_ref.shape, f32)
             to_c_ref[0] = sums
+    for copy in edge_copies:
+        copy.wait()
 
 
 def forward_kernel(margin_ref, from_a_ref, to_b_ref):
@@ -403,37 +405,22 @@
     from_a = [
         jnp.sum(force_from_a_ref[k] * weighted_ref[...], axis=0, keepdims=True) for k in range(3)
     ]
-    summed = parts_ref[...] + jnp.concatenate(from_a + [jnp.zeros((5, LANES), f32)], axis=0)
-    for step in (1, 2, 4):
-        summed = summed + pltpu.roll(summed, LANES - step, 1)
-    component = lax.bitwise_and(lax.broadcasted_iota(jnp.int32, (1, LANES), 1), 7)
-    tiles = copies_ref.shape[0] // 2
+    own = parts_ref[0:3] + jnp.concatenate(from_a, axis=0)
+    bands = copies_ref.shape[0] // 2
     _, odd = own_domain()
-    for group, half in ((1, 1 - odd), (2, odd)):
-        row = jnp.zeros((1, LANES), f32)
-        for k in range(3):
-            part = (group - 1) * 3 + k
-            value = summed[part : part + 1]
-            value = pltpu.roll(value, k, 1) if k else value
-            row = row + jnp.where(component == k, value, 0.0)
-        for tile in range(tiles):
-            copies_ref[half * tiles + tile] = jnp.broadcast_to(row, (8, LANES))
+    for value, half in ((own, 1 - odd), (parts_ref[3:6], odd)):
+        for band in range(bands):
+            copies_ref[half * bands + band] = value
 
 
 def total_kernel(gathered_ref, forces_ref):
     atoms = forces_ref.shape[1]
-    row = jnp.sum(jnp.sum(gathered_ref[...], axis=0), axis=0, keepdims=True)
-    lane = lax.broadcasted_iota(jnp.int32, (8, LANES), 1)
-    component = lax.broadcasted_iota(jnp.int32, (8, LANES), 0)
-    split = jnp.where(lax.bitwise_and(lane, 7) == component, row, 0.0)
+    rows = jnp.sum(gathered_ref[...], axis=0)
     source = lax.broadcasted_iota(jnp.int32, (LANES, LANES), 0)
     target = lax.broadcasted_iota(jnp.int32, (LANES, LANES), 1)
-    collect = (lax.shift_right_logical(source, 3) == target).astype(f32)
-    forces = sum(
-        jnp.dot(piece, collect.astype(bf16), preferred_element_type=f32)
-        for piece in pieces(split, 3)
-    )
-    forces_ref[...] = forces[:3, :atoms]
+    collect = (lax.shift_right_logical(source, 3) == target).astype(bf16)
+    forces = sum(jnp.dot(piece, collect, preferred_element_type=f32) for piece in pieces(rows, 3))
+    forces_ref[...] = forces[:, :atoms]
 
 
 def apply_kernel(
@@ -597,18 +584,12 @@
     slots_smem = pltpu.SMEM((entry_count,), jnp.int32)
 
     half_edge = ((band_count // 2, PAD, width_y, width_z), bf16)
-    to_b, *to_a = call(
-        edge_kernel,
-        "edges",
-        [edge, half_edge, half_edge],
-        [HBM],
-        [VMEM] * 3,
-        [pltpu.SemaphoreType.DMA((3,))],
+    (to_b,) = call(
+        edge_kernel, "edges", [edge], [HBM], [VMEM], [pltpu.SemaphoreType.DMA]
     )(in_hbm(wavefunctions))
     halo_b = swap_b(to_b)
-    halo_a = [swap_a(part) for part in to_a]
-
-    rows, grid, table, margins, margins_to_a, margins_to_c = call(
+
+    rows, grid, table, margins, margins_to_a, margins_to_c, *to_a = call(
         functools.partial(relayout_kernel, domain_count=domain_count),
         "relayout",
         [
@@ -618,9 +599,11 @@
             blocks,
             pair,
             ((6, 8, LANES), f32),
+            half_edge,
+            half_edge,
         ],
-        [HBM] * 4,
-        [SMEM] + [VMEM] * 5,
+        [HBM] * 4 + [VMEM],
+        [SMEM] + [VMEM] * 7,
         [
             pltpu.VMEM(wavefunctions.shape, bf16),
             slots_smem,
@@ -629,12 +612,13 @@
             pltpu.VMEM(projectors.shape, bf16),
             pltpu.VMEM((GROUPS, LANES, tile_len), f32),
             pltpu.SemaphoreType.DMA((plane_count,)),
-            pltpu.SemaphoreType.DMA((3,)),
+            pltpu.SemaphoreType.DMA((5,)),
         ],
-    )(*map(in_hbm, (margin_atoms, tile_rows, wavefunctions, projectors)))
+    )(*map(in_hbm, (margin_atoms, tile_rows, wavefunctions, projectors)), to_b)
 
     rows = pltpu.with_memory_space_constraint(rows, pltpu.SMEM)
     from_a = swap_a(margins_to_a)
+    halo_a = [swap_a(part) for part in to_a]
     (margins_to_b,) = call(forward_kernel, "forward", [((4, 8, LANES), f32)], [VMEM] * 2, [VMEM], limit=2)(
         margins, from_a
     )
@@ -706,14 +690,12 @@
     (copies,) = call(
         combine_kernel,
         "combine",
-        [((2 * bands // 8, 8, LANES), f32)],
+        [((2 * bands, 3, LANES), f32)],
         [VMEM] * 3,
         [VMEM],
         limit=2,
     )(parts, weighted, force_from_a)
-    gathered = lax.all_to_all(
-        copies.reshape(2 * bands, 1, LANES), ("dom", "band"), 0, 0, axis_index_groups=pairs
-    )
+    gathered = lax.all_to_all(copies, ("dom", "band"), 0, 0, axis_index_groups=pairs)
 
     (applied,) = call(
         apply_kernel,
@@ -734,7 +716,7 @@
 
     (forces,) = call(
         total_kernel, "total", [((3, ATOM_DEV), f32)], [VMEM], [VMEM], limit=2
-    )(gathered.reshape(2 * bands // 8, 8, LANES))
+    )(gathered)
     return (applied, forces)
 
 

time: 33 us -> 32.8 us (level)
  Pallas kernels: 13.5 us -> 13.1 us
    pallas_call x2, Pallas kernels: 2.12 us -> 1.71 us  [the longest x1 1.06 us: per_device(): call(edge_kernel, 'edges', [edge], [HBM], [VMEM], [pltpu.SemaphoreType.DMA])]
  transfers between devices with their start and end apart: 8 -> 8, of which waited for: 4 -> 4; matrix products, arithmetic and copies ran while one was open for 0% -> 0% of each run, Pallas kernels for 32% -> 33%
where the time goes in v7:
time: 32.8 us; the launch traced here: 32.5 us
  starting transfers between devices  16.3 us (50%)
  Pallas kernels  13.1 us (40%)
  waiting for transfers between devices  2.43 us (7%)
  between operations  0.71 us (2%)
    all_to_all x1, starting transfers between devices, per_device(): lax.all_to_all(copies, ('dom', 'band'), 0, 0, axis_index_groups=pairs)  10.5 us
    pallas_call x1, Pallas kernels, per_device(): call(apply_kernel, 'apply', [(wavefunctions.shape, bf16)], [SMEM, HBM, HB...  5.73 us
    ppermute x2, starting transfers between devices, swap_b(): lax.ppermute(x, 'dom', [(i, partner_b(i, count)) for i in range(count)])  4.02 us
    pallas_call x1, Pallas kernels, per_device(): call(functools.partial(relayout_kernel, domain_count=domain_count), 'rela...  2.33 us
    pallas_call x1, Pallas kernels, per_device(): call(gradient_kernel, 'gradient', [((grid_rows, LANES), f32), ((2, GROUPS...  1.74 us
    all_to_all x1, waiting for transfers between devices, per_device(): lax.all_to_all(copies, ('dom', 'band'), 0, 0, axis_index_groups=pairs)  1.39 us
    pallas_call x1, Pallas kernels, per_device(): call(edge_kernel, 'edges', [edge], [HBM], [VMEM], [pltpu.SemaphoreType.DMA])  1.06 us
    ppermute x1, starting transfers between devices, send_c(): lax.ppermute(x, 'dom', [(i, partner_a(partner_b(i, count))) for i in rang...  0.98 us
  transfers between devices with their start and end apart: 8, of which 4 were waited for; matrix products, arithmetic and copies ran while one was open for 0% of the time, Pallas kernels for 33%

profile of v7, /device:TPU:0, one launch (start us, length us, event | category | flops | bytes accessed | tf_op | source)
XLA Modules:
  0.0 32.5 jit_solution(12265611000000425140)
XLA Ops:
  0.6 1.1 %edges.1._ = bf16[8,2,128,128]{3,2,1,0:T(8,128)(2,1)S(1)} custom-call(bf16[8,8,128,128]{3,2,1,0:T(8,128)(2,1)} %wave_hbm.5), custom_call_target="tpu_custom_call" | custom-call | flops 1000 | bytes 1000 | tf_op jit(solution)/shard_map/edges/pallas_call | solution.py:587
  1.7 2.4 %collective-permute-start.2 = (bf16[8,2,128,128]{3,2,1,0:T(8,128)(2,1)S(1)}, bf16[8,2,128,128]{3,2,1,0:T(8,128)(2,1)S(1)}, u32[]{:S(2)}, u32[]{:S(2)}) collective-permute-start(bf16[8,2,128,128]{3,2,1,0:T(8,128)(2,1)S(1)} %edges.1._), channel_id=1, source_target_pairs={{0,112},{16,32},{32,16},{48,64},{64,48},{80,96},{96,80},{112,0},{1... | collective-permute-start | bytes 1572872 | tf_op jit(solution)/shard_map/ppermute | solution.py:33
  4.1 2.3 %relayout.1 = (s32[36]{0:T(128)S(4)}, f32[12288,128]{1,0:T(8,128)S(1)}, bf16[3,128,1024]{2,1,0:T(8,128)(2,1)S(1)}, f32[3,8,128]{2,1,0:T(8,128)S(1)}, f32[2,8,128...) custom-call(s32[36]{0:T(128)} %atoms_hbm.1, ...), custom_call_target="tpu_custom_call" | custom-call | flops 1000 | bytes 1000 | tf_op jit(solution)/shard_map/relayout/pallas_call | solution.py:592
  6.4 0.1 collective-permute-start
  6.5 0.5 %collective-permute-start.1 = (bf16[4,2,128,128]{3,2,1,0:T(8,128)(2,1)S(1)}, bf16[4,2,128,128]{3,2,1,0:T(8,128)(2,1)S(1)}, u32[]{:S(2)}, u32[]{:S(2)}) collective-permute-start(bf16[4,2,128,128]{3,2,1,0:T(8,128)(2,1)S(1)} %get-tuple-element.21), channel_id=1, source_target_pairs={{0,16},{16,0},{32,48},{48,32},{64,80},{80,64},{96,112},{112,96},{1... | collective-permute-start | bytes 786440 | tf_op jit(solution)/shard_map/ppermute | solution.py:28
  7.0 0.1 collective-permute-start.3
  7.1 1.0 %collective-permute-start.5 = (f32[6,8,128]{2,1,0:T(8,128)S(1)}, f32[6,8,128]{2,1,0:T(8,128)S(1)}, u32[]{:S(2)}, u32[]{:S(2)}) collective-permute-start(f32[6,8,128]{2,1,0:T(8,128)S(1)} %get-tuple-element.29), channel_id=1, source_target_pairs={{0,96},{16,48},{32,0},{48,80},{64,32},{80,112},{96,64},{112,16},{1... | collective-permute-start | bytes 73736 | tf_op jit(solution)/shard_map/ppermute | solution.py:38
  8.1 0.3 %collective-permute-done.3.from_a_ref = f32[2,8,128]{2,1,0:T(8,128)S(1)} collective-permute-done((f32[2,8,128]{2,1,0:T(8,128)S(1)}, f32[2,8,128]{2,1,0:T(8,128)S(1)}, u32[]{:S(2)}, u32[]{:S(2)}) %collective-permute-start.3) | collective-permute-done | bytes 8224 | tf_op jit(solution)/shard_map/ppermute | solution.py:28
  8.4 1.7 %collective-permute-start.4 = (f32[4,8,128]{2,1,0:T(8,128)S(1)}, f32[4,8,128]{2,1,0:T(8,128)S(1)}, u32[]{:S(2)}, u32[]{:S(2)}) collective-permute-start(f32[4,8,128]{2,1,0:T(8,128)S(1)} %forward.1._), channel_id=1, source_target_pairs={{0,112},{16,32},{32,16},{48,64},{64,48},{80,96},{96,80},{112,0},{1... | collective-permute-start | bytes 49160 | tf_op jit(solution)/shard_map/ppermute | solution.py:33
  10.1 0.0 collective-permute-done.halo_a0_ref
  10.1 0.0 collective-permute-done.1.halo_a1_ref
  10.1 1.7 %gradient.1 = (f32[12288,128]{1,0:T(8,128)S(1)}, f32[2,3,8,128]{3,2,1,0:T(8,128)S(1)}, f32[128,128]{1,0:T(8,128)S(1)}, f32[8,128]{1,0:T(8,128)S(1)}) custom-call(s32[36]{0:T(128)S(4)} %get-tuple-element.19.rows_ref, f32[12288,128]{1,0:T(8,128)S(1)} %get-tuple-element.23.grid_in, ...), custom_call_target="tpu_custom_call", output_to_operand_aliasing={{0}: (1, {})} | custom-call | flops 1000 | bytes 1000 | tf_op jit(solution)/shard_map/gradient/pallas_call | solution.py:628
  11.8 0.0 collective-permute-done.2.halo_b_ref
  11.8 0.4 %first.1 = (f32[12288,128]{1,0:T(8,128)S(1)}, f32[3,8,128]{2,1,0:T(8,128)S(1)}) custom-call(s32[36]{0:T(128)S(4)} %get-tuple-element.19.rows_ref, f32[12288,128]{1,0:T(8,128)S(1)} %get-tuple-element.26.grid_in, bf16[8,2,128,128]{3,2,1,0:T(8,128)(2,1)S(1)} %collective-permute-done.2.halo_b_ref, ...), custom_call_target="tpu_custom_call", output_to_operand_aliasing={{0}: (1, {})} | custom-call | flops 1000 | bytes 1000 | tf_op jit(solution)/shard_map/first/pallas_call | solution.py:656
  12.2 0.1 collective-permute-start.6
  12.3 0.4 %collective-permute-done.4.from_b_ref = f32[4,8,128]{2,1,0:T(8,128)S(1)} collective-permute-done((f32[4,8,128]{2,1,0:T(8,128)S(1)}, f32[4,8,128]{2,1,0:T(8,128)S(1)}, u32[]{:S(2)}, u32[]{:S(2)}) %collective-permute-start.4) | collective-permute-done | bytes 16416 | tf_op jit(solution)/shard_map/ppermute | solution.py:33
  12.8 0.0 collective-permute-done.5.from_c_ref
  12.8 0.5 %rest.1 = (f32[3,8,128]{2,1,0:T(8,128)S(1)}, f32[8,128]{1,0:T(8,128)S(1)}, f32[8,128]{1,0:T(8,128)S(1)}) custom-call(s32[36]{0:T(128)S(4)} %get-tuple-element.19.rows_ref, f32[12288,128]{1,0:T(8,128)S(1)} %get-tuple-element.28.grid_ref, bf16[3,128,1024]{2,1,0:T(8,128)(2,1)S(1)} %get-tuple-element.22.table_ref, ...), custom_call_target="tpu_custom_call" | custom-call | flops 1000 | bytes 1000 | tf_op jit(solution)/shard_map/rest/pallas_call | solution.py:665
  13.2 0.3 collective-permute-done.6.force_from_a_ref
  13.5 0.7 %combine.1 = f32[32,3,128]{2,1,0:T(4,128)} custom-call(f32[8,128]{1,0:T(8,128)S(1)} %get-tuple-element.34.parts_ref, f32[8,128]{1,0:T(8,128)S(1)} %get-tuple-element.35.weighted_ref, f32[3,8,128]{2,1,0:T(8,128)S(1)} %collective-permute-done.6.force_from_a_ref), custom_call_target="tpu_custom_call" | custom-call | flops 1000 | bytes 1000 | tf_op jit(solution)/shard_map/combine/pallas_call | solution.py:690
  14.1 10.5 %all-to-all-start = ((f32[32,3,128]{2,1,0:T(4,128)}), f32[32,3,128]{2,1,0:T(4,128)S(1)}, u32[]{:S(2)}, u32[]{:S(2)}) async-start(f32[32,3,128]{2,1,0:T(4,128)} %combine.1), calls=%async_computation | async-start | bytes 131072 | tf_op jit(solution)/shard_map/all_to_all | solution.py:698
  24.7 5.7 %apply.1 = bf16[8,8,128,128]{3,2,1,0:T(8,128)(2,1)} custom-call(s32[36]{0:T(128)S(4)} %get-tuple-element.19.rows_ref, bf16[8,8,128,128]{3,2,1,0:T(8,128)(2,1)} %wave_hbm.5, f32[8,128,128]{2,1,0:T(8,128)} %pot_hbm.1, bf16[4,2,128,128]{3,2,1,0:T(8,128)(2,1)S(1)} %collective-permute-done.halo_a0_ref, ...), custom_call_target="tpu_custom_call" | custom-call | flops 1000 | bytes 1000 | tf_op jit(solution)/shard_map/apply/pallas_call | solution.py:700
  30.4 1.4 %all-to-all-done.gathered_ref = f32[32,3,128]{2,1,0:T(4,128)S(1)} async-done(((f32[32,3,128]{2,1,0:T(4,128)}), f32[32,3,128]{2,1,0:T(4,128)S(1)}, u32[]{:S(2)}, u32[]{:S(2)}) %all-to-all-start) | async-done | bytes 49184 | tf_op jit(solution)/shard_map/all_to_all | solution.py:698
  31.8 0.8 %total.1 = f32[3,12]{1,0:T(4,128)} custom-call(f32[32,3,128]{2,1,0:T(4,128)S(1)} %all-to-all-done.gathered_ref), custom_call_target="tpu_custom_call" | custom-call | flops 1000 | bytes 1000 | tf_op jit(solution)/shard_map/total/pallas_call | solution.py:717
  (1 shorter events, 0.0 us)
Async XLA Ops:
  1.7 10.1 %collective-permute-start.2 = (bf16[8,2,128,128]{3,2,1,0:T(8,128)(2,1)S(1)}, bf16[8,2,128,128]{3,2,1,0:T(8,128)(2,1)S(1)}, u32[]{:S(2)}, u32[]{:S(2)}) collective-permute-start(bf16[8,2,128,128]{3,2,1,0:T(8,128)(2,1)S(1)} %edges.1._), channel_id=1, source_target_pairs={{0,112},{16,32},{32,16},{48,64},{64,48},{80,96},{96,80},{112,0},{1... | collective-permute-start | bytes 1572872 | tf_op jit(solution)/shard_map/ppermute | solution.py:33
  6.4 3.7 %collective-permute-start = (bf16[4,2,128,128]{3,2,1,0:T(8,128)(2,1)S(1)}, bf16[4,2,128,128]{3,2,1,0:T(8,128)(2,1)S(1)}, u32[]{:S(2)}, u32[]{:S(2)}) collective-permute-start(bf16[4,2,128,128]{3,2,1,0:T(8,128)(2,1)S(1)} %get-tuple-element.20), channel_id=1, source_target_pairs={{0,16},{16,0},{32,48},{48,32},{64,80},{80,64},{96,112},{112,96},{1... | collective-permute-start | bytes 786440 | tf_op jit(solution)/shard_map/ppermute | solution.py:28
  6.5 3.6 %collective-permute-start.1 = (bf16[4,2,128,128]{3,2,1,0:T(8,128)(2,1)S(1)}, bf16[4,2,128,128]{3,2,1,0:T(8,128)(2,1)S(1)}, u32[]{:S(2)}, u32[]{:S(2)}) collective-permute-start(bf16[4,2,128,128]{3,2,1,0:T(8,128)(2,1)S(1)} %get-tuple-element.21), channel_id=1, source_target_pairs={{0,16},{16,0},{32,48},{48,32},{64,80},{80,64},{96,112},{112,96},{1... | collective-permute-start | bytes 786440 | tf_op jit(solution)/shard_map/ppermute | solution.py:28
  7.0 1.4 %collective-permute-start.3 = (f32[2,8,128]{2,1,0:T(8,128)S(1)}, f32[2,8,128]{2,1,0:T(8,128)S(1)}, u32[]{:S(2)}, u32[]{:S(2)}) collective-permute-start(f32[2,8,128]{2,1,0:T(8,128)S(1)} %get-tuple-element.25), channel_id=1, source_target_pairs={{0,16},{16,0},{32,48},{48,32},{64,80},{80,64},{96,112},{112,96},{1... | collective-permute-start | bytes 24584 | tf_op jit(solution)/shard_map/ppermute | solution.py:28
  7.1 5.7 %collective-permute-start.5 = (f32[6,8,128]{2,1,0:T(8,128)S(1)}, f32[6,8,128]{2,1,0:T(8,128)S(1)}, u32[]{:S(2)}, u32[]{:S(2)}) collective-permute-start(f32[6,8,128]{2,1,0:T(8,128)S(1)} %get-tuple-element.29), channel_id=1, source_target_pairs={{0,96},{16,48},{32,0},{48,80},{64,32},{80,112},{96,64},{112,16},{1... | collective-permute-start | bytes 73736 | tf_op jit(solution)/shard_map/ppermute | solution.py:38
  8.4 4.4 %collective-permute-start.4 = (f32[4,8,128]{2,1,0:T(8,128)S(1)}, f32[4,8,128]{2,1,0:T(8,128)S(1)}, u32[]{:S(2)}, u32[]{:S(2)}) collective-permute-start(f32[4,8,128]{2,1,0:T(8,128)S(1)} %forward.1._), channel_id=1, source_target_pairs={{0,112},{16,32},{32,16},{48,64},{64,48},{80,96},{96,80},{112,0},{1... | collective-permute-start | bytes 49160 | tf_op jit(solution)/shard_map/ppermute | solution.py:33
  12.2 1.3 %collective-permute-start.6 = (f32[3,8,128]{2,1,0:T(8,128)S(1)}, f32[3,8,128]{2,1,0:T(8,128)S(1)}, u32[]{:S(2)}, u32[]{:S(2)}) collective-permute-start(f32[3,8,128]{2,1,0:T(8,128)S(1)} %get-tuple-element.32._), channel_id=1, source_target_pairs={{0,16},{16,0},{32,48},{48,32},{64,80},{80,64},{96,112},{112,96},{1... | collective-permute-start | bytes 36872 | tf_op jit(solution)/shard_map/ppermute | solution.py:28
  14.1 17.6 %all-to-all-start = ((f32[32,3,128]{2,1,0:T(4,128)}), f32[32,3,128]{2,1,0:T(4,128)S(1)}, u32[]{:S(2)}, u32[]{:S(2)}) async-start(f32[32,3,128]{2,1,0:T(4,128)} %combine.1), calls=%async_computation | async-start | bytes 131072 | tf_op jit(solution)/shard_map/all_to_all | solution.py:698

commit v8 on v7

--- a/solution.py
+++ b/solution.py
@@ -416,11 +416,14 @@
 def total_kernel(gathered_ref, forces_ref):
     atoms = forces_ref.shape[1]
     rows = jnp.sum(gathered_ref[...], axis=0)
+    rows = jnp.concatenate([rows, jnp.zeros((8 - rows.shape[0], LANES), f32)], axis=0)
     source = lax.broadcasted_iota(jnp.int32, (LANES, LANES), 0)
     target = lax.broadcasted_iota(jnp.int32, (LANES, LANES), 1)
     collect = (lax.shift_right_logical(source, 3) == target).astype(bf16)
-    forces = sum(jnp.dot(piece, collect, preferred_element_type=f32) for piece in pieces(rows, 3))
-    forces_ref[...] = forces[:, :atoms]
+    split = jnp.concatenate([piece.astype(f32) for piece in pieces(rows, 3)], axis=0)
+    products = jnp.dot(split.astype(bf16), collect, preferred_element_type=f32)
+    forces = products[0:8] + (products[8:16] + products[16:24])
+    forces_ref[...] = forces[:3, :atoms]
 
 
 def apply_kernel(
@@ -574,7 +577,7 @@
     entry_count, proj_count, tile_len = projectors.shape
     assert (band_count, proj_count, width_y, width_z) == (8, 8, 128, LANES)
     assert entry_count == GROUPS * ATOM_DEV
-    grid_rows = (plane_count + 2 * PAD) * width_y * 8
+    grid_rows = (plane_count + 2 * PAD) * width_y * 8 + 8
     domain_count = lax.axis_size("dom")
     block = ((8, LANES), f32)
     pair = ((2, 8, LANES), f32)
@@ -705,7 +708,7 @@
         [HBM],
         [
             pltpu.VMEM(wavefunctions.shape, bf16),
-            pltpu.VMEM((plane_count * width_y * 8, LANES), f32),
+            pltpu.VMEM((plane_count * width_y * 8 + 8, LANES), f32),
             pltpu.VMEM((band_count, plane_count + 2 * PAD, width_y, width_z), bf16),
             pltpu.VMEM(potential.shape, f32),
             pltpu.SemaphoreType.DMA((2, plane_count)),

time: 32.8 us -> 32.8 us (level)
  no operation moved by 1% of the time
where the time goes in v8:
time: 32.8 us; the launch traced here: 32.5 us
  starting transfers between devices  16.3 us (50%)
  Pallas kernels  13.3 us (41%)
  waiting for transfers between devices  2.25 us (7%)
  between operations  0.71 us (2%)
    all_to_all x1, starting transfers between devices, per_device(): lax.all_to_all(copies, ('dom', 'band'), 0, 0, axis_index_groups=pairs)  10.5 us
    pallas_call x1, Pallas kernels, per_device(): call(apply_kernel, 'apply', [(wavefunctions.shape, bf16)], [SMEM, HBM, HB...  5.91 us
    ppermute x2, starting transfers between devices, swap_b(): lax.ppermute(x, 'dom', [(i, partner_b(i, count)) for i in range(count)])  4.02 us
    pallas_call x1, Pallas kernels, per_device(): call(functools.partial(relayout_kernel, domain_count=domain_count), 'rela...  2.33 us
    pallas_call x1, Pallas kernels, per_device(): call(gradient_kernel, 'gradient', [((grid_rows, LANES), f32), ((2, GROUPS...  1.75 us
    all_to_all x1, waiting for transfers between devices, per_device(): lax.all_to_all(copies, ('dom', 'band'), 0, 0, axis_index_groups=pairs)  1.2 us
    pallas_call x1, Pallas kernels, per_device(): call(edge_kernel, 'edges', [edge], [HBM], [VMEM], [pltpu.SemaphoreType.DMA])  1.06 us
    ppermute x1, starting transfers between devices, send_c(): lax.ppermute(x, 'dom', [(i, partner_a(partner_b(i, count))) for i in rang...  0.97 us
  transfers between devices with their start and end apart: 8, of which 4 were waited for; matrix products, arithmetic and copies ran while one was open for 0% of the time, Pallas kernels for 33%

profile of v8, /device:TPU:0, one launch (start us, length us, event | category | flops | bytes accessed | tf_op | source)
XLA Modules:
  0.0 32.5 jit_solution(13311455311798664971)
XLA Ops:
  0.6 1.1 %edges.1._ = bf16[8,2,128,128]{3,2,1,0:T(8,128)(2,1)S(1)} custom-call(bf16[8,8,128,128]{3,2,1,0:T(8,128)(2,1)} %wave_hbm.5), custom_call_target="tpu_custom_call" | custom-call | flops 1000 | bytes 1000 | tf_op jit(solution)/shard_map/edges/pallas_call | solution.py:590
  1.7 2.4 %collective-permute-start.2 = (bf16[8,2,128,128]{3,2,1,0:T(8,128)(2,1)S(1)}, bf16[8,2,128,128]{3,2,1,0:T(8,128)(2,1)S(1)}, u32[]{:S(2)}, u32[]{:S(2)}) collective-permute-start(bf16[8,2,128,128]{3,2,1,0:T(8,128)(2,1)S(1)} %edges.1._), channel_id=1, source_target_pairs={{0,112},{16,32},{32,16},{48,64},{64,48},{80,96},{96,80},{112,0},{1... | collective-permute-start | bytes 1572872 | tf_op jit(solution)/shard_map/ppermute | solution.py:33
  4.1 2.3 %relayout.1 = (s32[36]{0:T(128)S(4)}, f32[12296,128]{1,0:T(8,128)S(1)}, bf16[3,128,1024]{2,1,0:T(8,128)(2,1)S(1)}, f32[3,8,128]{2,1,0:T(8,128)S(1)}, f32[2,8,128...) custom-call(s32[36]{0:T(128)} %atoms_hbm.1, ...), custom_call_target="tpu_custom_call" | custom-call | flops 1000 | bytes 1000 | tf_op jit(solution)/shard_map/relayout/pallas_call | solution.py:595
  6.4 0.1 collective-permute-start
  6.5 0.5 %collective-permute-start.1 = (bf16[4,2,128,128]{3,2,1,0:T(8,128)(2,1)S(1)}, bf16[4,2,128,128]{3,2,1,0:T(8,128)(2,1)S(1)}, u32[]{:S(2)}, u32[]{:S(2)}) collective-permute-start(bf16[4,2,128,128]{3,2,1,0:T(8,128)(2,1)S(1)} %get-tuple-element.21), channel_id=1, source_target_pairs={{0,16},{16,0},{32,48},{48,32},{64,80},{80,64},{96,112},{112,96},{1... | collective-permute-start | bytes 786440 | tf_op jit(solution)/shard_map/ppermute | solution.py:28
  7.0 0.1 collective-permute-start.3
  7.1 1.0 %collective-permute-start.5 = (f32[6,8,128]{2,1,0:T(8,128)S(1)}, f32[6,8,128]{2,1,0:T(8,128)S(1)}, u32[]{:S(2)}, u32[]{:S(2)}) collective-permute-start(f32[6,8,128]{2,1,0:T(8,128)S(1)} %get-tuple-element.29), channel_id=1, source_target_pairs={{0,96},{16,48},{32,0},{48,80},{64,32},{80,112},{96,64},{112,16},{1... | collective-permute-start | bytes 73736 | tf_op jit(solution)/shard_map/ppermute | solution.py:38
  8.1 0.3 %collective-permute-done.3.from_a_ref = f32[2,8,128]{2,1,0:T(8,128)S(1)} collective-permute-done((f32[2,8,128]{2,1,0:T(8,128)S(1)}, f32[2,8,128]{2,1,0:T(8,128)S(1)}, u32[]{:S(2)}, u32[]{:S(2)}) %collective-permute-start.3) | collective-permute-done | bytes 8224 | tf_op jit(solution)/shard_map/ppermute | solution.py:28
  8.4 1.7 %collective-permute-start.4 = (f32[4,8,128]{2,1,0:T(8,128)S(1)}, f32[4,8,128]{2,1,0:T(8,128)S(1)}, u32[]{:S(2)}, u32[]{:S(2)}) collective-permute-start(f32[4,8,128]{2,1,0:T(8,128)S(1)} %forward.1._), channel_id=1, source_target_pairs={{0,112},{16,32},{32,16},{48,64},{64,48},{80,96},{96,80},{112,0},{1... | collective-permute-start | bytes 49160 | tf_op jit(solution)/shard_map/ppermute | solution.py:33
  10.1 0.0 collective-permute-done.halo_a0_ref
  10.1 0.0 collective-permute-done.1.halo_a1_ref
  10.1 1.8 %gradient.1 = (f32[12296,128]{1,0:T(8,128)S(1)}, f32[2,3,8,128]{3,2,1,0:T(8,128)S(1)}, f32[128,128]{1,0:T(8,128)S(1)}, f32[8,128]{1,0:T(8,128)S(1)}) custom-call(s32[36]{0:T(128)S(4)} %get-tuple-element.19.rows_ref, f32[12296,128]{1,0:T(8,128)S(1)} %get-tuple-element.23.grid_in, ...), custom_call_target="tpu_custom_call", output_to_operand_aliasing={{0}: (1, {})} | custom-call | flops 1000 | bytes 1000 | tf_op jit(solution)/shard_map/gradient/pallas_call | solution.py:631
  11.8 0.0 collective-permute-done.2.halo_b_ref
  11.8 0.4 %first.1 = (f32[12296,128]{1,0:T(8,128)S(1)}, f32[3,8,128]{2,1,0:T(8,128)S(1)}) custom-call(s32[36]{0:T(128)S(4)} %get-tuple-element.19.rows_ref, f32[12296,128]{1,0:T(8,128)S(1)} %get-tuple-element.26.grid_in, bf16[8,2,128,128]{3,2,1,0:T(8,128)(2,1)S(1)} %collective-permute-done.2.halo_b_ref, ...), custom_call_target="tpu_custom_call", output_to_operand_aliasing={{0}: (1, {})} | custom-call | flops 1000 | bytes 1000 | tf_op jit(solution)/shard_map/first/pallas_call | solution.py:659
  12.3 0.1 collective-permute-start.6
  12.3 0.4 %collective-permute-done.4.from_b_ref = f32[4,8,128]{2,1,0:T(8,128)S(1)} collective-permute-done((f32[4,8,128]{2,1,0:T(8,128)S(1)}, f32[4,8,128]{2,1,0:T(8,128)S(1)}, u32[]{:S(2)}, u32[]{:S(2)}) %collective-permute-start.4) | collective-permute-done | bytes 16416 | tf_op jit(solution)/shard_map/ppermute | solution.py:33
  12.8 0.0 collective-permute-done.5.from_c_ref
  12.8 0.5 %rest.1 = (f32[3,8,128]{2,1,0:T(8,128)S(1)}, f32[8,128]{1,0:T(8,128)S(1)}, f32[8,128]{1,0:T(8,128)S(1)}) custom-call(s32[36]{0:T(128)S(4)} %get-tuple-element.19.rows_ref, f32[12296,128]{1,0:T(8,128)S(1)} %get-tuple-element.28.grid_ref, bf16[3,128,1024]{2,1,0:T(8,128)(2,1)S(1)} %get-tuple-element.22.table_ref, ...), custom_call_target="tpu_custom_call" | custom-call | flops 1000 | bytes 1000 | tf_op jit(solution)/shard_map/rest/pallas_call | solution.py:668
  13.2 0.3 collective-permute-done.6.force_from_a_ref
  13.5 0.7 %combine.1 = f32[32,3,128]{2,1,0:T(4,128)} custom-call(f32[8,128]{1,0:T(8,128)S(1)} %get-tuple-element.34.parts_ref, f32[8,128]{1,0:T(8,128)S(1)} %get-tuple-element.35.weighted_ref, f32[3,8,128]{2,1,0:T(8,128)S(1)} %collective-permute-done.6.force_from_a_ref), custom_call_target="tpu_custom_call" | custom-call | flops 1000 | bytes 1000 | tf_op jit(solution)/shard_map/combine/pallas_call | solution.py:693
  14.2 10.5 %all-to-all-start = ((f32[32,3,128]{2,1,0:T(4,128)}), f32[32,3,128]{2,1,0:T(4,128)S(1)}, u32[]{:S(2)}, u32[]{:S(2)}) async-start(f32[32,3,128]{2,1,0:T(4,128)} %combine.1), calls=%async_computation | async-start | bytes 131072 | tf_op jit(solution)/shard_map/all_to_all | solution.py:701
  24.7 5.9 %apply.1 = bf16[8,8,128,128]{3,2,1,0:T(8,128)(2,1)} custom-call(s32[36]{0:T(128)S(4)} %get-tuple-element.19.rows_ref, bf16[8,8,128,128]{3,2,1,0:T(8,128)(2,1)} %wave_hbm.5, f32[8,128,128]{2,1,0:T(8,128)} %pot_hbm.1, bf16[4,2,128,128]{3,2,1,0:T(8,128)(2,1)S(1)} %collective-permute-done.halo_a0_ref, ...), custom_call_target="tpu_custom_call" | custom-call | flops 1000 | bytes 1000 | tf_op jit(solution)/shard_map/apply/pallas_call | solution.py:703
  30.6 1.2 %all-to-all-done.gathered_ref = f32[32,3,128]{2,1,0:T(4,128)S(1)} async-done(((f32[32,3,128]{2,1,0:T(4,128)}), f32[32,3,128]{2,1,0:T(4,128)S(1)}, u32[]{:S(2)}, u32[]{:S(2)}) %all-to-all-start) | async-done | bytes 49184 | tf_op jit(solution)/shard_map/all_to_all | solution.py:701
  31.8 0.7 %total.1 = f32[3,12]{1,0:T(4,128)} custom-call(f32[32,3,128]{2,1,0:T(4,128)S(1)} %all-to-all-done.gathered_ref), custom_call_target="tpu_custom_call" | custom-call | flops 1000 | bytes 1000 | tf_op jit(solution)/shard_map/total/pallas_call | solution.py:720
  (1 shorter events, 0.0 us)
Async XLA Ops:
  1.7 10.1 %collective-permute-start.2 = (bf16[8,2,128,128]{3,2,1,0:T(8,128)(2,1)S(1)}, bf16[8,2,128,128]{3,2,1,0:T(8,128)(2,1)S(1)}, u32[]{:S(2)}, u32[]{:S(2)}) collective-permute-start(bf16[8,2,128,128]{3,2,1,0:T(8,128)(2,1)S(1)} %edges.1._), channel_id=1, source_target_pairs={{0,112},{16,32},{32,16},{48,64},{64,48},{80,96},{96,80},{112,0},{1... | collective-permute-start | bytes 1572872 | tf_op jit(solution)/shard_map/ppermute | solution.py:33
  6.4 3.7 %collective-permute-start = (bf16[4,2,128,128]{3,2,1,0:T(8,128)(2,1)S(1)}, bf16[4,2,128,128]{3,2,1,0:T(8,128)(2,1)S(1)}, u32[]{:S(2)}, u32[]{:S(2)}) collective-permute-start(bf16[4,2,128,128]{3,2,1,0:T(8,128)(2,1)S(1)} %get-tuple-element.20), channel_id=1, source_target_pairs={{0,16},{16,0},{32,48},{48,32},{64,80},{80,64},{96,112},{112,96},{1... | collective-permute-start | bytes 786440 | tf_op jit(solution)/shard_map/ppermute | solution.py:28
  6.5 3.6 %collective-permute-start.1 = (bf16[4,2,128,128]{3,2,1,0:T(8,128)(2,1)S(1)}, bf16[4,2,128,128]{3,2,1,0:T(8,128)(2,1)S(1)}, u32[]{:S(2)}, u32[]{:S(2)}) collective-permute-start(bf16[4,2,128,128]{3,2,1,0:T(8,128)(2,1)S(1)} %get-tuple-element.21), channel_id=1, source_target_pairs={{0,16},{16,0},{32,48},{48,32},{64,80},{80,64},{96,112},{112,96},{1... | collective-permute-start | bytes 786440 | tf_op jit(solution)/shard_map/ppermute | solution.py:28
  7.0 1.4 %collective-permute-start.3 = (f32[2,8,128]{2,1,0:T(8,128)S(1)}, f32[2,8,128]{2,1,0:T(8,128)S(1)}, u32[]{:S(2)}, u32[]{:S(2)}) collective-permute-start(f32[2,8,128]{2,1,0:T(8,128)S(1)} %get-tuple-element.25), channel_id=1, source_target_pairs={{0,16},{16,0},{32,48},{48,32},{64,80},{80,64},{96,112},{112,96},{1... | collective-permute-start | bytes 24584 | tf_op jit(solution)/shard_map/ppermute | solution.py:28
  7.1 5.7 %collective-permute-start.5 = (f32[6,8,128]{2,1,0:T(8,128)S(1)}, f32[6,8,128]{2,1,0:T(8,128)S(1)}, u32[]{:S(2)}, u32[]{:S(2)}) collective-permute-start(f32[6,8,128]{2,1,0:T(8,128)S(1)} %get-tuple-element.29), channel_id=1, source_target_pairs={{0,96},{16,48},{32,0},{48,80},{64,32},{80,112},{96,64},{112,16},{1... | collective-permute-start | bytes 73736 | tf_op jit(solution)/shard_map/ppermute | solution.py:38
  8.4 4.4 %collective-permute-start.4 = (f32[4,8,128]{2,1,0:T(8,128)S(1)}, f32[4,8,128]{2,1,0:T(8,128)S(1)}, u32[]{:S(2)}, u32[]{:S(2)}) collective-permute-start(f32[4,8,128]{2,1,0:T(8,128)S(1)} %forward.1._), channel_id=1, source_target_pairs={{0,112},{16,32},{32,16},{48,64},{64,48},{80,96},{96,80},{112,0},{1... | collective-permute-start | bytes 49160 | tf_op jit(solution)/shard_map/ppermute | solution.py:33
  12.3 1.3 %collective-permute-start.6 = (f32[3,8,128]{2,1,0:T(8,128)S(1)}, f32[3,8,128]{2,1,0:T(8,128)S(1)}, u32[]{:S(2)}, u32[]{:S(2)}) collective-permute-start(f32[3,8,128]{2,1,0:T(8,128)S(1)} %get-tuple-element.32._), channel_id=1, source_target_pairs={{0,16},{16,0},{32,48},{48,32},{64,80},{80,64},{96,112},{112,96},{1... | collective-permute-start | bytes 36872 | tf_op jit(solution)/shard_map/ppermute | solution.py:28
  14.2 17.6 %all-to-all-start = ((f32[32,3,128]{2,1,0:T(4,128)}), f32[32,3,128]{2,1,0:T(4,128)S(1)}, u32[]{:S(2)}, u32[]{:S(2)}) async-start(f32[32,3,128]{2,1,0:T(4,128)} %combine.1), calls=%async_computation | async-start | bytes 131072 | tf_op jit(solution)/shard_map/all_to_all | solution.py:701

commit v9 on v8

--- a/solution.py
+++ b/solution.py
@@ -263,9 +263,9 @@
         row = [at_row(grid_ref, base + edge + (y % width_y) * 8) for y in range(-2, 2)]
         for y in range(width_y):
             row.append(at_row(grid_ref, base + edge + ((y + 2) % width_y) * 8))
-            near = row[y + 3] - row[y + 1]
-            far = row[y + 4] - row[y]
-            y_ref[pl.ds(base + y * 8, 8), :] = (2.0 / 3.0) * near - (1.0 / 12.0) * far
+            y_ref[pl.ds(base + y * 8, 8), :] = 8.0 * (row[y + 3] - row[y + 1]) - (
+                row[y + 4] - row[y]
+            )
         return carry
 
     lax.fori_loop(0, planes, one_plane, 0)
@@ -281,7 +281,7 @@
     for group in range(GROUPS):
         second, third = contract(
             [
-                tile_values(rows_ref, group, lambda base: at_row(y_ref, base)),
+                tile_values(rows_ref, group, lambda base: at_row(y_ref, base)) * (1.0 / 12.0),
                 z_gradient_values(rows_ref, group, grid_ref, edge, stencil),
             ],
             table_ref[group],

time: 32.8 us -> 32.7 us (level)
  no operation moved by 1% of the time
where the time goes in v9:
time: 32.7 us; the launch traced here: 32.4 us
  starting transfers between devices  16.2 us (50%)
  Pallas kernels  13.2 us (40%)
  waiting for transfers between devices  2.25 us (7%)
  between operations  0.71 us (2%)
    all_to_all x1, starting transfers between devices, per_device(): lax.all_to_all(copies, ('dom', 'band'), 0, 0, axis_index_groups=pairs)  10.5 us
    pallas_call x1, Pallas kernels, per_device(): call(apply_kernel, 'apply', [(wavefunctions.shape, bf16)], [SMEM, HBM, HB...  5.91 us
    ppermute x2, starting transfers between devices, swap_b(): lax.ppermute(x, 'dom', [(i, partner_b(i, count)) for i in range(count)])  4.02 us
    pallas_call x1, Pallas kernels, per_device(): call(functools.partial(relayout_kernel, domain_count=domain_count), 'rela...  2.33 us
    pallas_call x1, Pallas kernels, per_device(): call(gradient_kernel, 'gradient', [((grid_rows, LANES), f32), ((2, GROUPS...  1.61 us
    all_to_all x1, waiting for transfers between devices, per_device(): lax.all_to_all(copies, ('dom', 'band'), 0, 0, axis_index_groups=pairs)  1.2 us
    pallas_call x1, Pallas kernels, per_device(): call(edge_kernel, 'edges', [edge], [HBM], [VMEM], [pltpu.SemaphoreType.DMA])  1.06 us
    ppermute x1, starting transfers between devices, send_c(): lax.ppermute(x, 'dom', [(i, partner_a(partner_b(i, count))) for i in rang...  0.97 us
  transfers between devices with their start and end apart: 8, of which 4 were waited for; matrix products, arithmetic and copies ran while one was open for 0% of the time, Pallas kernels for 33%

profile of v9, /device:TPU:0, one launch (start us, length us, event | category | flops | bytes accessed | tf_op | source)
XLA Modules:
  0.0 32.4 jit_solution(14184392962870623627)
XLA Ops:
  0.6 1.1 %edges.1._ = bf16[8,2,128,128]{3,2,1,0:T(8,128)(2,1)S(1)} custom-call(bf16[8,8,128,128]{3,2,1,0:T(8,128)(2,1)} %wave_hbm.5), custom_call_target="tpu_custom_call" | custom-call | flops 1000 | bytes 1000 | tf_op jit(solution)/shard_map/edges/pallas_call | solution.py:590
  1.7 2.4 %collective-permute-start.2 = (bf16[8,2,128,128]{3,2,1,0:T(8,128)(2,1)S(1)}, bf16[8,2,128,128]{3,2,1,0:T(8,128)(2,1)S(1)}, u32[]{:S(2)}, u32[]{:S(2)}) collective-permute-start(bf16[8,2,128,128]{3,2,1,0:T(8,128)(2,1)S(1)} %edges.1._), channel_id=1, source_target_pairs={{0,112},{16,32},{32,16},{48,64},{64,48},{80,96},{96,80},{112,0},{1... | collective-permute-start | bytes 1572872 | tf_op jit(solution)/shard_map/ppermute | solution.py:33
  4.1 2.3 %relayout.1 = (s32[36]{0:T(128)S(4)}, f32[12296,128]{1,0:T(8,128)S(1)}, bf16[3,128,1024]{2,1,0:T(8,128)(2,1)S(1)}, f32[3,8,128]{2,1,0:T(8,128)S(1)}, f32[2,8,128...) custom-call(s32[36]{0:T(128)} %atoms_hbm.1, ...), custom_call_target="tpu_custom_call" | custom-call | flops 1000 | bytes 1000 | tf_op jit(solution)/shard_map/relayout/pallas_call | solution.py:595
  6.4 0.1 collective-permute-start
  6.5 0.5 %collective-permute-start.1 = (bf16[4,2,128,128]{3,2,1,0:T(8,128)(2,1)S(1)}, bf16[4,2,128,128]{3,2,1,0:T(8,128)(2,1)S(1)}, u32[]{:S(2)}, u32[]{:S(2)}) collective-permute-start(bf16[4,2,128,128]{3,2,1,0:T(8,128)(2,1)S(1)} %get-tuple-element.21), channel_id=1, source_target_pairs={{0,16},{16,0},{32,48},{48,32},{64,80},{80,64},{96,112},{112,96},{1... | collective-permute-start | bytes 786440 | tf_op jit(solution)/shard_map/ppermute | solution.py:28
  7.0 0.1 collective-permute-start.3
  7.1 1.0 %collective-permute-start.5 = (f32[6,8,128]{2,1,0:T(8,128)S(1)}, f32[6,8,128]{2,1,0:T(8,128)S(1)}, u32[]{:S(2)}, u32[]{:S(2)}) collective-permute-start(f32[6,8,128]{2,1,0:T(8,128)S(1)} %get-tuple-element.29), channel_id=1, source_target_pairs={{0,96},{16,48},{32,0},{48,80},{64,32},{80,112},{96,64},{112,16},{1... | collective-permute-start | bytes 73736 | tf_op jit(solution)/shard_map/ppermute | solution.py:38
  8.0 0.3 %collective-permute-done.3.from_a_ref = f32[2,8,128]{2,1,0:T(8,128)S(1)} collective-permute-done((f32[2,8,128]{2,1,0:T(8,128)S(1)}, f32[2,8,128]{2,1,0:T(8,128)S(1)}, u32[]{:S(2)}, u32[]{:S(2)}) %collective-permute-start.3) | collective-permute-done | bytes 8224 | tf_op jit(solution)/shard_map/ppermute | solution.py:28
  8.4 1.7 %collective-permute-start.4 = (f32[4,8,128]{2,1,0:T(8,128)S(1)}, f32[4,8,128]{2,1,0:T(8,128)S(1)}, u32[]{:S(2)}, u32[]{:S(2)}) collective-permute-start(f32[4,8,128]{2,1,0:T(8,128)S(1)} %forward.1._), channel_id=1, source_target_pairs={{0,112},{16,32},{32,16},{48,64},{64,48},{80,96},{96,80},{112,0},{1... | collective-permute-start | bytes 49160 | tf_op jit(solution)/shard_map/ppermute | solution.py:33
  10.1 0.0 collective-permute-done.halo_a0_ref
  10.1 0.0 collective-permute-done.1.halo_a1_ref
  10.1 1.6 %gradient.1 = (f32[12296,128]{1,0:T(8,128)S(1)}, f32[2,3,8,128]{3,2,1,0:T(8,128)S(1)}, f32[128,128]{1,0:T(8,128)S(1)}, f32[8,128]{1,0:T(8,128)S(1)}) custom-call(s32[36]{0:T(128)S(4)} %get-tuple-element.19.rows_ref, f32[12296,128]{1,0:T(8,128)S(1)} %get-tuple-element.23.grid_in, ...), custom_call_target="tpu_custom_call", output_to_operand_aliasing={{0}: (1, {})} | custom-call | flops 1000 | bytes 1000 | tf_op jit(solution)/shard_map/gradient/pallas_call | solution.py:631
  11.7 0.0 collective-permute-done.2.halo_b_ref
  11.7 0.4 %first.1 = (f32[12296,128]{1,0:T(8,128)S(1)}, f32[3,8,128]{2,1,0:T(8,128)S(1)}) custom-call(s32[36]{0:T(128)S(4)} %get-tuple-element.19.rows_ref, f32[12296,128]{1,0:T(8,128)S(1)} %get-tuple-element.26.grid_in, bf16[8,2,128,128]{3,2,1,0:T(8,128)(2,1)S(1)} %collective-permute-done.2.halo_b_ref, ...), custom_call_target="tpu_custom_call", output_to_operand_aliasing={{0}: (1, {})} | custom-call | flops 1000 | bytes 1000 | tf_op jit(solution)/shard_map/first/pallas_call | solution.py:659
  12.1 0.1 collective-permute-start.6
  12.2 0.6 %collective-permute-done.4.from_b_ref = f32[4,8,128]{2,1,0:T(8,128)S(1)} collective-permute-done((f32[4,8,128]{2,1,0:T(8,128)S(1)}, f32[4,8,128]{2,1,0:T(8,128)S(1)}, u32[]{:S(2)}, u32[]{:S(2)}) %collective-permute-start.4) | collective-permute-done | bytes 16416 | tf_op jit(solution)/shard_map/ppermute | solution.py:33
  12.8 0.0 collective-permute-done.5.from_c_ref
  12.8 0.5 %rest.1 = (f32[3,8,128]{2,1,0:T(8,128)S(1)}, f32[8,128]{1,0:T(8,128)S(1)}, f32[8,128]{1,0:T(8,128)S(1)}) custom-call(s32[36]{0:T(128)S(4)} %get-tuple-element.19.rows_ref, f32[12296,128]{1,0:T(8,128)S(1)} %get-tuple-element.28.grid_ref, bf16[3,128,1024]{2,1,0:T(8,128)(2,1)S(1)} %get-tuple-element.22.table_ref, ...), custom_call_target="tpu_custom_call" | custom-call | flops 1000 | bytes 1000 | tf_op jit(solution)/shard_map/rest/pallas_call | solution.py:668
  13.3 0.1 collective-permute-done.6.force_from_a_ref
  13.4 0.7 %combine.1 = f32[32,3,128]{2,1,0:T(4,128)} custom-call(f32[8,128]{1,0:T(8,128)S(1)} %get-tuple-element.34.parts_ref, f32[8,128]{1,0:T(8,128)S(1)} %get-tuple-element.35.weighted_ref, f32[3,8,128]{2,1,0:T(8,128)S(1)} %collective-permute-done.6.force_from_a_ref), custom_call_target="tpu_custom_call" | custom-call | flops 1000 | bytes 1000 | tf_op jit(solution)/shard_map/combine/pallas_call | solution.py:693
  14.0 10.5 %all-to-all-start = ((f32[32,3,128]{2,1,0:T(4,128)}), f32[32,3,128]{2,1,0:T(4,128)S(1)}, u32[]{:S(2)}, u32[]{:S(2)}) async-start(f32[32,3,128]{2,1,0:T(4,128)} %combine.1), calls=%async_computation | async-start | bytes 131072 | tf_op jit(solution)/shard_map/all_to_all | solution.py:701
  24.5 5.9 %apply.1 = bf16[8,8,128,128]{3,2,1,0:T(8,128)(2,1)} custom-call(s32[36]{0:T(128)S(4)} %get-tuple-element.19.rows_ref, bf16[8,8,128,128]{3,2,1,0:T(8,128)(2,1)} %wave_hbm.5, f32[8,128,128]{2,1,0:T(8,128)} %pot_hbm.1, bf16[4,2,128,128]{3,2,1,0:T(8,128)(2,1)S(1)} %collective-permute-done.halo_a0_ref, ...), custom_call_target="tpu_custom_call" | custom-call | flops 1000 | bytes 1000 | tf_op jit(solution)/shard_map/apply/pallas_call | solution.py:703
  30.5 1.2 %all-to-all-done.gathered_ref = f32[32,3,128]{2,1,0:T(4,128)S(1)} async-done(((f32[32,3,128]{2,1,0:T(4,128)}), f32[32,3,128]{2,1,0:T(4,128)S(1)}, u32[]{:S(2)}, u32[]{:S(2)}) %all-to-all-start) | async-done | bytes 49184 | tf_op jit(solution)/shard_map/all_to_all | solution.py:701
  31.7 0.7 %total.1 = f32[3,12]{1,0:T(4,128)} custom-call(f32[32,3,128]{2,1,0:T(4,128)S(1)} %all-to-all-done.gathered_ref), custom_call_target="tpu_custom_call" | custom-call | flops 1000 | bytes 1000 | tf_op jit(solution)/shard_map/total/pallas_call | solution.py:720
  (1 shorter events, 0.0 us)
Async XLA Ops:
  1.7 10.0 %collective-permute-start.2 = (bf16[8,2,128,128]{3,2,1,0:T(8,128)(2,1)S(1)}, bf16[8,2,128,128]{3,2,1,0:T(8,128)(2,1)S(1)}, u32[]{:S(2)}, u32[]{:S(2)}) collective-permute-start(bf16[8,2,128,128]{3,2,1,0:T(8,128)(2,1)S(1)} %edges.1._), channel_id=1, source_target_pairs={{0,112},{16,32},{32,16},{48,64},{64,48},{80,96},{96,80},{112,0},{1... | collective-permute-start | bytes 1572872 | tf_op jit(solution)/shard_map/ppermute | solution.py:33
  6.4 3.7 %collective-permute-start = (bf16[4,2,128,128]{3,2,1,0:T(8,128)(2,1)S(1)}, bf16[4,2,128,128]{3,2,1,0:T(8,128)(2,1)S(1)}, u32[]{:S(2)}, u32[]{:S(2)}) collective-permute-start(bf16[4,2,128,128]{3,2,1,0:T(8,128)(2,1)S(1)} %get-tuple-element.20), channel_id=1, source_target_pairs={{0,16},{16,0},{32,48},{48,32},{64,80},{80,64},{96,112},{112,96},{1... | collective-permute-start | bytes 786440 | tf_op jit(solution)/shard_map/ppermute | solution.py:28
  6.5 3.6 %collective-permute-start.1 = (bf16[4,2,128,128]{3,2,1,0:T(8,128)(2,1)S(1)}, bf16[4,2,128,128]{3,2,1,0:T(8,128)(2,1)S(1)}, u32[]{:S(2)}, u32[]{:S(2)}) collective-permute-start(bf16[4,2,128,128]{3,2,1,0:T(8,128)(2,1)S(1)} %get-tuple-element.21), channel_id=1, source_target_pairs={{0,16},{16,0},{32,48},{48,32},{64,80},{80,64},{96,112},{112,96},{1... | collective-permute-start | bytes 786440 | tf_op jit(solution)/shard_map/ppermute | solution.py:28
  7.0 1.4 %collective-permute-start.3 = (f32[2,8,128]{2,1,0:T(8,128)S(1)}, f32[2,8,128]{2,1,0:T(8,128)S(1)}, u32[]{:S(2)}, u32[]{:S(2)}) collective-permute-start(f32[2,8,128]{2,1,0:T(8,128)S(1)} %get-tuple-element.25), channel_id=1, source_target_pairs={{0,16},{16,0},{32,48},{48,32},{64,80},{80,64},{96,112},{112,96},{1... | collective-permute-start | bytes 24584 | tf_op jit(solution)/shard_map/ppermute | solution.py:28
  7.1 5.7 %collective-permute-start.5 = (f32[6,8,128]{2,1,0:T(8,128)S(1)}, f32[6,8,128]{2,1,0:T(8,128)S(1)}, u32[]{:S(2)}, u32[]{:S(2)}) collective-permute-start(f32[6,8,128]{2,1,0:T(8,128)S(1)} %get-tuple-element.29), channel_id=1, source_target_pairs={{0,96},{16,48},{32,0},{48,80},{64,32},{80,112},{96,64},{112,16},{1... | collective-permute-start | bytes 73736 | tf_op jit(solution)/shard_map/ppermute | solution.py:38
  8.4 4.4 %collective-permute-start.4 = (f32[4,8,128]{2,1,0:T(8,128)S(1)}, f32[4,8,128]{2,1,0:T(8,128)S(1)}, u32[]{:S(2)}, u32[]{:S(2)}) collective-permute-start(f32[4,8,128]{2,1,0:T(8,128)S(1)} %forward.1._), channel_id=1, source_target_pairs={{0,112},{16,32},{32,16},{48,64},{64,48},{80,96},{96,80},{112,0},{1... | collective-permute-start | bytes 49160 | tf_op jit(solution)/shard_map/ppermute | solution.py:33
  12.1 1.3 %collective-permute-start.6 = (f32[3,8,128]{2,1,0:T(8,128)S(1)}, f32[3,8,128]{2,1,0:T(8,128)S(1)}, u32[]{:S(2)}, u32[]{:S(2)}) collective-permute-start(f32[3,8,128]{2,1,0:T(8,128)S(1)} %get-tuple-element.32._), channel_id=1, source_target_pairs={{0,16},{16,0},{32,48},{48,32},{64,80},{80,64},{96,112},{112,96},{1... | collective-permute-start | bytes 36872 | tf_op jit(solution)/shard_map/ppermute | solution.py:28
  14.0 17.6 %all-to-all-start = ((f32[32,3,128]{2,1,0:T(4,128)}), f32[32,3,128]{2,1,0:T(4,128)S(1)}, u32[]{:S(2)}, u32[]{:S(2)}) async-start(f32[32,3,128]{2,1,0:T(4,128)} %combine.1), calls=%async_computation | async-start | bytes 131072 | tf_op jit(solution)/shard_map/all_to_all | solution.py:701
